TPU v7x, 32 devices: a whole 2x2x4 slice. The times are simulated.
32 devices in a mesh: dp: 8 (over z, x), mp: 4 (over y, core).
Axes of the slice: x: 2, y: 2, z: 4, core: 2. Of those that a mesh axis runs over, the one named last changes fastest.
Arguments:
- inputs: bfloat16 [4096, 768], P(('dp', 'mp')), may hold values from -30 to 30, as said below
- attention_gain: float32 [768], replicated, may hold values from 0.1 to 1.9
- query_weight: bfloat16 [768, 768], P(None, 'mp'), may hold values from -0.21875 to 0.21875
- key_weight: bfloat16 [768, 768], P(None, 'mp'), may hold values from -0.21875 to 0.21875
- value_weight: bfloat16 [768, 768], P(None, 'mp'), may hold values from -0.21875 to 0.21875
- out_weight: bfloat16 [768, 768], P('mp'), may hold values from -3 to 3
- bias_table: float32 [32, 12], P(None, 'mp'), may hold values from -4 to 4
- feedforward_gain: float32 [768], replicated, may hold values from 0.1 to 1.9
- gate_weight: bfloat16 [768, 2048], P(None, 'mp'), may hold values from -0.21875 to 0.21875
- up_weight: bfloat16 [768, 2048], P(None, 'mp'), may hold values from -0.21875 to 0.21875
- down_weight: bfloat16 [2048, 768], P('mp'), may hold values from -0.125 to 0.125
- segment: int32 [4096], replicated, may hold values from 0 to 12, as said below
- bucket: int32 [2047], replicated, may hold values from 0 to 31, as said below
- cotangent: bfloat16 [4096, 768], P(('dp', 'mp')), may hold values from -6 to 6
Outputs:
- layer_out: bfloat16 [4096, 768], P(('dp', 'mp'))
- input_grad: bfloat16 [4096, 768], P(('dp', 'mp'))
- attention_gain_grad: float32 [768], replicated
- query_grad: float32 [768, 768], P(None, 'mp')
- key_grad: float32 [768, 768], P(None, 'mp')
- value_grad: float32 [768, 768], P(None, 'mp')
- out_grad: float32 [768, 768], P('mp')
- table_grad: float32 [32, 12], P(None, 'mp')
- feedforward_gain_grad: float32 [768], replicated
- gate_grad: float32 [768, 2048], P(None, 'mp')
- up_grad: float32 [768, 2048], P(None, 'mp')
- down_grad: float32 [2048, 768], P('mp')
Inputs may be any that keep to these rules, and one draw needn't show every extreme that they name: `inputs`: values of order one; rows and columns differ in scale. `segment`: equal values mark one sequence and never fall along the rows. Each sequence is either all 1024 rows of two neighbouring aligned blocks of 512 rows, or one of two sequences that together fill one aligned block, each of them 512 // 4 to 384 rows. Entry 1023 + d is the bucket of offset d (key row minus query row); it is under 32 // 2 for d <= 0 and 16 or more for d > 0, and never falls as |d| grows on either side.
All inputs are finite; a program needn't handle non-finite values.
Results may differ from a plain program's by a relative error of at most 0.02.
Values may be sent and summed in bfloat16 or wider, within the bound.
No kernel may reach another device: no remote copies, remote signals or barrier semaphores. Data moves between devices by JAX's collectives and lax.ppermute only.
A program may use at most 128 MiB of HBM per device.

v0:
```python
import functools

import jax
import jax.numpy as jnp
from jax import lax
from jax.experimental import pallas as pl
from jax.experimental.pallas import tpu as pltpu
from jax.sharding import PartitionSpec as P

HEAD = 64
LOW = jnp.bfloat16
F32 = jnp.float32
CHUNK = 128
SPAN = 2048
EXTRA = 16
NEG = -1e30
ROOT = 0.7978845608
CUBE = 0.044715
VMEM = pl.BlockSpec(memory_space=pltpu.VMEM)
SMEM = pl.BlockSpec(memory_space=pltpu.SMEM)
HBM = pl.BlockSpec(memory_space=pltpu.HBM)


def dot_nn(a, b):
    return lax.dot_general(a, b, (((1,), (0,)), ((), ())), preferred_element_type=F32)


def dot_nt(a, b):
    return lax.dot_general(a, b, (((1,), (1,)), ((), ())), preferred_element_type=F32)


def dot_tn(a, b):
    return lax.dot_general(a, b, (((0,), (0,)), ((), ())), preferred_element_type=F32)


def call(kernel, outs, ins, scratch=(), smem=1, hbm=0, micros=2.0, out_smem=0, limit=20):
    return pl.pallas_call(
        kernel,
        out_shape=outs,
        in_specs=[SMEM] * smem + [VMEM] * (len(ins) - smem - hbm) + [HBM] * hbm,
        out_specs=[SMEM] * out_smem + [VMEM] * (len(outs) - out_smem),
        scratch_shapes=list(scratch),
        cost_estimate=pl.CostEstimate(flops=int(micros * 2e7), bytes_accessed=0, transcendentals=0),
        compiler_params=pltpu.CompilerParams(vmem_limit_bytes=limit * 1024 * 1024),
    )(*ins)


def in_hbm(values):
    return pltpu.with_memory_space_constraint(values, pltpu.HBM)


def shape(dims, dtype):
    return jax.ShapeDtypeStruct(dims, dtype)


def head_lanes(width, h):
    lane = lax.broadcasted_iota(jnp.int32, (1, width), 1)
    return (lane >= h * HEAD) & (lane < (h + 1) * HEAD)


def keep_head(values, h):
    return jnp.where(head_lanes(values.shape[-1], h), values, jnp.zeros_like(values))


def rows_norm(values):
    return lax.rsqrt(jnp.mean(values * values, axis=-1, keepdims=True) + 1e-06)


def aligned(start):
    return pl.ds(pl.multiple_of(start, CHUNK), CHUNK)


def lay_bias(row, table_ref, target):
    heads, buckets = table_ref.shape
    which = lax.broadcasted_iota(jnp.int32, (buckets, SPAN), 0)
    onehot = (row == which).astype(F32)
    table = table_ref[...].T
    for h in range(heads):
        rows = jnp.sum(onehot * table[:, h : h + 1], axis=0, keepdims=True)
        count = 1
        while count < 8:
            rows = jnp.concatenate([rows, pltpu.roll(rows, count, 1)], axis=0)
            count *= 2
        target[h, 0:8, :] = rows
        while count < CHUNK:
            target[h, count : 2 * count, :] = pltpu.roll(target[h, 0:count, :], count, 1)
            count *= 2


def setup_kernel(spot, segment_ref, bucket_ref, table_ref, info, row_ref, col_ref, bias_ref, *, groups, first_bits):
    rank, member = spot[0], spot[1]
    steps = row_ref.shape[1] // CHUNK
    rows = [segment_ref[pl.ds(rank * steps + k, 1), :] for k in range(steps)]
    lane = lax.broadcasted_iota(jnp.int32, (1, CHUNK), 1)

    def value(row, at):
        return jnp.max(jnp.where(lane == at, row, -1))

    before = segment_ref[pl.ds(jnp.maximum(rank * steps - 1, 0), 1), :]
    later = segment_ref[pl.ds(jnp.minimum((rank + 1) * steps, groups * steps - 1), 1), :]
    left = (value(before, CHUNK - 1) == value(rows[0], 0)) & (rank > 0)
    right = (value(later, 0) == value(rows[-1], CHUNK - 1)) & (rank < groups - 1)
    even = jnp.where(rank % 2 == 0, right.astype(jnp.int32), left.astype(jnp.int32))
    info[0] = member // 2
    info[1] = member % 2
    info[2] = left.astype(jnp.int32)
    info[3] = (left | right).astype(jnp.int32)
    info[4] = (rank >> first_bits[0]) & 1
    info[5] = (rank >> first_bits[1]) & 1
    info[6] = even
    info[7] = rank
    row = jnp.concatenate(rows, axis=1).astype(F32)
    row_ref[...] = row
    col_ref[...] = jnp.broadcast_to(row, (CHUNK, row.shape[1])).T
    lay_bias(row_of(bucket_ref, 0, bucket_ref.shape[0]), table_ref, bias_ref)


def row_of(ref, first, count):
    return jnp.concatenate([ref[pl.ds(first + k, 1), :] for k in range(count)], axis=1)


def flipped_kernel(bucket_ref, table_ref, bias_ref, flipped_ref):
    count = bucket_ref.shape[0]
    sub = lax.broadcasted_iota(jnp.int32, (CHUNK, CHUNK), 0)
    lane = lax.broadcasted_iota(jnp.int32, (CHUNK, CHUNK), 1)
    turned = dot_nn(bucket_ref[...].astype(F32).astype(LOW), (sub + lane == CHUNK - 1).astype(F32).astype(LOW))
    row = jnp.concatenate([turned[k : k + 1, :] for k in reversed(range(count))], axis=1)
    row = pltpu.roll(row, 1, 1).astype(jnp.int32)
    flipped_ref[...] = jnp.concatenate([row[:, k * CHUNK : (k + 1) * CHUNK] for k in range(count)], axis=0)
    lay_bias(row, table_ref, bias_ref)


def near_kernel(info, even_ref, odd_ref, out_ref):
    out_ref[...] = jnp.where(info[6] == 1, even_ref[...], odd_ref[...])


def fold_diagonals(tile):
    rows, cols = tile.shape
    while rows > 1:
        rows //= 2
        tile = tile[:rows] + pltpu.roll(tile[rows:], cols - rows, 1)
    return tile


def pack_columns(columns, offset=0, base=None, width=CHUNK):
    rows = columns[0].shape[0]
    lane = lax.broadcasted_iota(jnp.int32, (rows, width), 1)
    out = jnp.zeros((rows, width), F32) if base is None else base
    for k, column in enumerate(columns):
        out = jnp.where(lane == offset + k, column, out)
    return out


def by_head(packed, width):
    lane = lax.broadcasted_iota(jnp.int32, (packed.shape[0], width), 1)
    out = packed[:, 0:1]
    for h in range(1, width // HEAD):
        out = jnp.where(lane >= h * HEAD, packed[:, h : h + 1], out)
    return out


def place(y, c):
    return (2 * y + c, 2 * (1 - y) + c, 2 * y + 1 - c, 2 * (1 - y) + 1 - c)


def project(normed, rows, wq, wk, wv, q_ref, k_ref, v_ref):
    q_ref[rows, :] = (dot_nt(normed, wq[...]).astype(LOW).astype(F32) * HEAD**-0.5).astype(LOW)
    k_ref[rows, :] = dot_nt(normed, wk[...]).astype(LOW)
    v_ref[rows, :] = dot_nt(normed, wv[...]).astype(LOW)


def attend(q, keys, values, bias, first, seg_col, seg_row, scores_ref, probs_ref, acc_ref, top_ref, sum_ref):
    window, width = q.shape
    heads = width // HEAD
    for h in range(heads):
        scores_ref[h] = dot_nt(keep_head(q, h), keys)
    for h in range(heads):
        for a in range(window // CHUNK):
            rows = slice(a * CHUNK, (a + 1) * CHUNK)
            scores = scores_ref[h, rows, :] + bias[h, :, pl.ds(first - a * CHUNK, window)]
            if seg_col is not None:
                scores = jnp.where(seg_col[rows, 0:1] == seg_row[...], scores, NEG)
            top = jnp.max(scores, axis=-1, keepdims=True)
            weights = jnp.exp(scores - top)
            probs_ref[h, rows, :] = weights.astype(LOW)
            top_ref[rows, :] = pack_columns([top], h, top_ref[rows, :] if h else jnp.zeros((CHUNK, CHUNK), F32))
            total = jnp.sum(weights, axis=-1, keepdims=True)
            sum_ref[rows, :] = pack_columns([total], h, sum_ref[rows, :] if h else jnp.ones((CHUNK, CHUNK), F32))
    total = dot_nn(probs_ref[0], keep_head(values, 0))
    for h in range(1, heads):
        total = total + dot_nn(probs_ref[h], keep_head(values, h))
    acc_ref[...] = total


def own_kernel(
    info,
    x0,
    x1,
    x2,
    x3,
    gain,
    bias,
    seg_col,
    seg_row,
    wq_hbm,
    wk_hbm,
    wv_hbm,
    x_all,
    normed_ref,
    q_ref,
    k_ref,
    v_ref,
    acc_ref,
    top_ref,
    sum_ref,
    wq,
    wk,
    wv,
    scores_ref,
    probs_ref,
    sems,
):
    pairs = ((wq_hbm, wq), (wk_hbm, wk), (wv_hbm, wv))
    copies = [pltpu.make_async_copy(a, b, sems.at[k]) for k, (a, b) in enumerate(pairs)]
    for copy in copies:
        copy.start()
    for piece, spot in zip((x0, x1, x2, x3), place(info[0], info[1])):
        rows = aligned(spot * CHUNK)
        low = piece[...]
        x_all[rows, :] = low
        wide = low.astype(F32)
        normed_ref[rows, :] = (wide * rows_norm(wide) * gain[...]).astype(LOW)
    for copy in copies:
        copy.wait()
    project(normed_ref[...], slice(None), wq, wk, wv, q_ref, k_ref, v_ref)
    attend(
        q_ref[...],
        k_ref[...],
        v_ref[...],
        bias,
        SPAN // 2,
        seg_col,
        seg_row,
        scores_ref,
        probs_ref,
        acc_ref,
        top_ref,
        sum_ref,
    )


def far_start(info, window):
    return pl.multiple_of(jnp.where(info[2] == 1, SPAN // 2 - window, SPAN // 2 + window), CHUNK)


def partner_kernel(
    info,
    x0,
    x1,
    x2,
    x3,
    gain,
    wq,
    wk,
    wv,
    bias,
    q_ref,
    acc_ref,
    top_ref,
    sum_ref,
    mixed_low,
    mixed_ref,
    lse_ref,
    qp_ref,
    kp_ref,
    vp_ref,
    normed_ref,
    scores_ref,
    probs_ref,
    acc_two,
    top_two,
    sum_two,
):
    window, width = q_ref.shape
    paired = info[3]

    @pl.when(paired == 1)
    def _():
        for piece, spot in zip((x0, x1, x2, x3), place(info[0], info[1])):
            wide = piece[...].astype(F32)
            normed_ref[aligned(spot * CHUNK), :] = (wide * rows_norm(wide) * gain[...]).astype(LOW)
        project(normed_ref[...], slice(None), wq, wk, wv, qp_ref, kp_ref, vp_ref)
        attend(
            q_ref[...],
            kp_ref[...],
            vp_ref[...],
            bias,
            far_start(info, window),
            None,
            None,
            scores_ref,
            probs_ref,
            acc_two,
            top_two,
            sum_two,
        )
        for a in range(window // CHUNK):
            rows = slice(a * CHUNK, (a + 1) * CHUNK)
            top = jnp.maximum(top_ref[rows, :], top_two[rows, :])
            one, two = jnp.exp(top_ref[rows, :] - top), jnp.exp(top_two[rows, :] - top)
            whole = sum_ref[rows, :] * one + sum_two[rows, :] * two
            inverse = 1.0 / whole
            mixed = acc_ref[rows, :] * by_head(one * inverse, width)
            mixed = mixed + acc_two[rows, :] * by_head(two * inverse, width)
            mixed_ref[rows, :] = mixed
            mixed_low[rows, :] = mixed.astype(LOW)
            lse_ref[rows, :] = top + jnp.log(whole)

    @pl.when(paired == 0)
    def _():
        qp_ref[...] = jnp.zeros_like(qp_ref)
        kp_ref[...] = jnp.zeros_like(kp_ref)
        vp_ref[...] = jnp.zeros_like(vp_ref)
        for a in range(window // CHUNK):
            rows = slice(a * CHUNK, (a + 1) * CHUNK)
            whole = sum_ref[rows, :]
            mixed = acc_ref[rows, :] * by_head(1.0 / whole, width)
            mixed_ref[rows, :] = mixed
            mixed_low[rows, :] = mixed.astype(LOW)
            lse_ref[rows, :] = top_ref[rows, :] + jnp.log(whole)


def cotangent_kernel(g0, g1, g2, g3, down_w, cot_ref, d_act_ref):
    for part, piece in enumerate((g2, g3, g0, g1)):
        cot_ref[part * CHUNK : (part + 1) * CHUNK, :] = piece[...]
    d_act_ref[...] = dot_nt(cot_ref[...], down_w[...])


def feed_kernel(
    info,
    x_all,
    m0,
    m1,
    m2,
    m3,
    o0,
    o1,
    o2,
    o3,
    d_act_ref,
    gain,
    gate_w,
    up_w,
    second_ref,
    hidden_ref,
    act_ref,
    dgate_ref,
    dup_ref,
    send_ref,
    keep_ref,
    gain_ref,
):
    y, c = info[0], info[1]
    half = 2 * CHUNK
    gain_sum = jnp.zeros((1, gain.shape[1]), F32)
    for part, core in enumerate((1 - c, c)):
        rows = slice(part * half, (part + 1) * half)
        spots = (aligned((2 * y + core) * CHUNK), aligned((2 * (1 - y) + core) * CHUNK))

        def pick(ref):
            return jnp.concatenate([ref[spots[0], :], ref[spots[1], :]], axis=0)

        hidden = pick(x_all).astype(F32)
        branch = dot_nn(pick(m0), o0[...])
        for m, o in ((m1, o1), (m2, o2), (m3, o3)):
            branch = branch + dot_nn(pick(m), o[...])
        hidden = hidden + branch
        if part == 1:
            hidden_ref[...] = hidden
        unit = hidden * rows_norm(hidden)
        second = (unit * gain[...]).astype(LOW)
        second_ref[rows, :] = second
        gate = dot_nn(second, gate_w[...])
        up = dot_nn(second, up_w[...])
        d_act = d_act_ref[rows, :]
        square = gate * gate
        tanh = jnp.tanh(ROOT * gate * (1.0 + CUBE * square))
        low_half = 0.5 * (1.0 + tanh)
        gelu = gate * low_half
        slope = low_half + 0.5 * gate * (1.0 - tanh * tanh) * (ROOT * (1.0 + 3.0 * CUBE * square))
        act_ref[rows, :] = (gelu * up).astype(LOW)
        d_gate = (d_act * up * slope).astype(LOW)
        d_up = (d_act * gelu).astype(LOW)
        dgate_ref[rows, :] = d_gate
        dup_ref[rows, :] = d_up
        d_second = dot_nt(d_gate, gate_w[...]) + dot_nt(d_up, up_w[...])
        gain_sum = gain_sum + jnp.sum(d_second * unit, axis=0, keepdims=True)
        if part == 0:
            send_ref[...] = d_second.astype(LOW)
        else:
            keep_ref[...] = d_second
    gain_ref[...] = gain_sum


def feed_grad_kernel(
    info, second_ref, dgate_ref, dup_ref, act_ref, cot_ref, one_send, one_keep, two_send, two_keep, one_ref, two_ref
):
    d, units = second_ref.shape[1], dgate_ref.shape[1]
    one_ref[:d, :] = dot_tn(second_ref[...], dgate_ref[...]).astype(LOW)
    two_ref[:d, :] = dot_tn(second_ref[...], dup_ref[...]).astype(LOW)
    down = dot_tn(act_ref[...], cot_ref[...]).astype(LOW)
    half = units // 2
    quarter = half // 2
    for k, target in enumerate((one_ref, two_ref)):
        target[d : d + half, :] = down[k * half : (k + 1) * half, :units]
        for side in (0, 1):
            rows = slice(k * half + side * quarter, k * half + (side + 1) * quarter)
            target[d + half :, side * (units // 2) : (side + 1) * (units // 2)] = down[rows, units:]
    for source, side, send, keep in ((one_ref, info[4], one_send, one_keep), (two_ref, info[5], two_send, two_keep)):
        rows = send.shape[0]
        send[...] = source[pl.ds(pl.multiple_of((1 - side) * rows, 16), rows), :]
        keep[...] = source[pl.ds(pl.multiple_of(side * rows, 16), rows), :]


def feed_out_kernel(act_ref, down_w, send_ref, keep_ref):
    half = send_ref.shape[0]
    send_ref[...] = dot_nn(act_ref[:half, :], down_w[...]).astype(LOW)
    keep_ref[...] = dot_nn(act_ref[half:, :], down_w[...]).astype(LOW)


def feed_total_kernel(info, one, one_got, two, two_got, gate_ref, up_ref, down_ref, full_ref):
    d, units = gate_ref.shape
    half = units // 2
    quarter = half // 2
    parts = ((one, one_got, info[4], gate_ref), (two, two_got, info[5], up_ref))
    for k, (mine, got, side, target) in enumerate(parts):
        rows = mine.shape[0]
        full_ref[pl.ds(pl.multiple_of(side * rows, 16), rows), :] = mine[...]
        full_ref[pl.ds(pl.multiple_of((1 - side) * rows, 16), rows), :] = got[...]
        target[...] = full_ref[:d, :].astype(F32)
        down_ref[k * half : (k + 1) * half, :units] = full_ref[d : d + half, :].astype(F32)
        for part in (0, 1):
            rows = slice(k * half + part * quarter, k * half + (part + 1) * quarter)
            down_ref[rows, units:] = full_ref[d + half :, part * (units // 2) : (part + 1) * (units // 2)].astype(F32)


def feed_merge_kernel(keep_ref, got_ref, own_ref, send_ref):
    local = own_ref.shape[0]
    total = (keep_ref[...].astype(F32) + got_ref[...].astype(F32)).astype(LOW)
    own_ref[...] = total[:local, :]
    send_ref[...] = total[local:, :]


def layer_out_kernel(hidden_ref, own_ref, got_ref, out_ref):
    local = out_ref.shape[0]
    out_ref[...] = (hidden_ref[:local, :] + (own_ref[...].astype(F32) + got_ref[...].astype(F32))).astype(LOW)


def hidden_back_kernel(sum_ref, other_ref, hidden_ref, g0, g1, gain, dh_ref, low_ref):
    for part, cot in enumerate((g0, g1)):
        rows = slice(part * CHUNK, (part + 1) * CHUNK)
        flip = slice((1 - part) * CHUNK, (2 - part) * CHUNK)
        d_second = sum_ref[rows, :].astype(F32) + other_ref[flip, :].astype(F32)
        hidden = hidden_ref[rows, :]
        inverse = rows_norm(hidden)
        unit = hidden * inverse
        scaled = d_second * gain[...]
        dh = cot[...].astype(F32) + inverse * (scaled - unit * jnp.mean(unit * scaled, axis=-1, keepdims=True))
        low_ref[rows, :] = dh.astype(LOW)
        if part == 0:
            dh_ref[...] = dh


def mixed_back_kernel(
    info, pair_own, pair_other, out_w, mixed_ref, mixed_low, lse_ref, payload_ref, stat_ref, grad_ref, branch_ref, pad_ref
):
    width = mixed_ref.shape[1]
    heads = width // HEAD
    pieces = (pair_own[:CHUNK, :], pair_own[CHUNK:, :], pair_other[:CHUNK, :], pair_other[CHUNK:, :])
    for piece, spot in zip(pieces, place(info[0], info[1])):
        branch_ref[aligned(spot * CHUNK), :] = piece
    pad_ref[:width, :] = out_w[...]
    pad_ref[width:, :] = jnp.zeros((pad_ref.shape[0] - width, pad_ref.shape[1]), LOW)
    d_all = dot_nt(branch_ref[...], pad_ref[...]).astype(LOW).astype(F32)
    for a in range(d_all.shape[0] // CHUNK):
        rows = slice(a * CHUNK, (a + 1) * CHUNK)
        d_mixed = d_all[rows, :]
        product = d_mixed[:, :width] * mixed_ref[rows, :]
        deltas = [jnp.sum(keep_head(product, h), axis=-1, keepdims=True) for h in range(heads)]
        stat = pack_columns(deltas, heads, lse_ref[rows, :])
        stat_ref[rows, :] = stat
        high = stat.astype(LOW).astype(F32)
        rest = stat - high
        lane = lax.broadcasted_iota(jnp.int32, (CHUNK, CHUNK), 1)
        skip = width % CHUNK
        high = pltpu.roll(high, skip, 1)
        rest = pltpu.roll(rest, skip + 2 * heads, 1)
        tail = jnp.where(lane < skip, d_mixed[:, width - skip : width - skip + CHUNK], high)
        tail = jnp.where(lane >= skip + 2 * heads, rest, tail)
        tail = jnp.where(lane >= skip + 4 * heads, 0.0, tail)
        payload_ref[rows, : width - skip] = d_mixed[:, : width - skip].astype(LOW)
        payload_ref[rows, width - skip :] = tail.astype(LOW)
    grad_ref[...] = dot_tn(mixed_low[...], branch_ref[...]).astype(LOW)


def bend(scores_ref, products_ref, probs_ref, ds_ref, h, bias, first, lse_of, delta_of, seg_col, seg_row, fold_ref):
    window = scores_ref.shape[1]
    steps = window // CHUNK
    for a in range(steps):
        rows = slice(a * CHUNK, (a + 1) * CHUNK)
        scores = scores_ref[h, rows, :] + bias[h, :, pl.ds(first - a * CHUNK, window)]
        if seg_col is not None:
            scores = jnp.where(seg_col[rows, 0:1] == seg_row[...], scores, NEG)
        weights = jnp.exp(scores - lse_of(rows))
        d_scores = weights * (products_ref[h, rows, :] - delta_of(rows))
        ds_ref[h, rows, :] = d_scores.astype(LOW)
        if probs_ref is not None:
            probs_ref[h, rows, :] = weights.astype(LOW)
        if fold_ref is not None:
            at = (steps - a) * CHUNK
            if a == 0:
                fold_ref[h, :, :at] = jnp.zeros((CHUNK, at), F32)
                fold_ref[h, :, at:] = d_scores
            else:
                if a == steps - 1:
                    fold_ref[h, :, :CHUNK] = jnp.zeros((CHUNK, CHUNK), F32)
                fold_ref[h, :, at : at + window] += d_scores


def table_sums(fold_ref, bucket_ref, start, table_ref):
    heads, buckets = table_ref.shape
    reach = fold_ref.shape[2]
    row = row_of(bucket_ref, start // CHUNK, reach // CHUNK)
    onehot = row == lax.broadcasted_iota(jnp.int32, (buckets, reach), 0)
    columns = []
    for h in range(heads):
        folded = fold_diagonals(fold_ref[h])
        columns.append(jnp.sum(jnp.where(onehot, folded, 0.0), axis=1, keepdims=True))
    return pack_columns(columns).T[:heads, :]


def own_back_kernel(
    q_ref,
    k_ref,
    v_ref,
    payload_ref,
    stat_ref,
    bias_t,
    seg_col,
    seg_row,
    flipped_ref,
    dq_ref,
    dk_ref,
    dv_ref,
    table_ref,
    scores_ref,
    products_ref,
    probs_ref,
    ds_ref,
    fold_ref,
):
    window, width = q_ref.shape
    heads = width // HEAD
    queries, keys, values = q_ref[...], k_ref[...], v_ref[...]
    back = payload_ref[:, :width]
    stat = stat_ref[...].T
    for h in range(heads):
        scores_ref[h] = dot_nt(keep_head(keys, h), queries)
        products_ref[h] = dot_nt(keep_head(values, h), back)
    for h in range(heads):
        lse, delta = stat[h : h + 1, :], stat[heads + h : heads + h + 1, :]
        bend(
            scores_ref,
            products_ref,
            probs_ref,
            ds_ref,
            h,
            bias_t,
            SPAN // 2,
            lambda rows: lse,
            lambda rows: delta,
            seg_col,
            seg_row,
            fold_ref,
        )
    d_queries = dot_tn(ds_ref[0], keep_head(keys, 0))
    d_keys = dot_nn(ds_ref[0], keep_head(queries, 0))
    d_values = dot_nn(probs_ref[0], keep_head(back, 0))
    for h in range(1, heads):
        d_queries = d_queries + dot_tn(ds_ref[h], keep_head(keys, h))
        d_keys = d_keys + dot_nn(ds_ref[h], keep_head(queries, h))
        d_values = d_values + dot_nn(probs_ref[h], keep_head(back, h))
    dq_ref[...] = d_queries
    dk_ref[...] = d_keys
    dv_ref[...] = d_values
    table_ref[...] = table_sums(fold_ref, flipped_ref, SPAN // 2 - window, table_ref)


def far_back_kernel(
    info,
    q_ref,
    kp_ref,
    vp_ref,
    payload_ref,
    stat_ref,
    bias,
    bucket_ref,
    dq_in,
    table_in,
    dq_ref,
    table_ref,
    scores_ref,
    products_ref,
    ds_ref,
    fold_ref,
):
    window, width = q_ref.shape
    heads = width // HEAD

    @pl.when(info[3] == 1)
    def _():
        queries, keys, values = q_ref[...], kp_ref[...], vp_ref[...]
        back = payload_ref[:, :width]
        first = far_start(info, window)
        for h in range(heads):
            scores_ref[h] = dot_nt(keep_head(queries, h), keys)
            products_ref[h] = dot_nt(keep_head(back, h), values)
        for h in range(heads):
            bend(
                scores_ref,
                products_ref,
                None,
                ds_ref,
                h,
                bias,
                first,
                lambda rows: stat_ref[rows, h : h + 1],
                lambda rows: stat_ref[rows, heads + h : heads + h + 1],
                None,
                None,
                fold_ref,
            )
        d_queries = dq_in[...]
        for h in range(heads):
            d_queries = d_queries + dot_nn(ds_ref[h], keep_head(keys, h))
        dq_ref[...] = (d_queries * HEAD**-0.5).astype(LOW)
        table_ref[...] = table_in[...] + table_sums(fold_ref, bucket_ref, first - window, table_ref)

    @pl.when(info[3] == 0)
    def _():
        dq_ref[...] = (dq_in[...] * HEAD**-0.5).astype(LOW)
        table_ref[...] = table_in[...]


def partner_back_kernel(
    info,
    k_ref,
    v_ref,
    qp_ref,
    from_even,
    from_odd,
    bias_t,
    dk_in,
    dv_in,
    dq_ref,
    normed_ref,
    x_all,
    gain,
    wq,
    wk,
    wv,
    grad_in,
    gain_in,
    one_send,
    one_keep,
    two_send,
    two_keep,
    send_ref,
    keep_ref,
    small_ref,
    d_all,
    scores_ref,
    products_ref,
    probs_ref,
    ds_ref,
):
    window, width = k_ref.shape
    heads = width // HEAD
    y, c = info[0], info[1]
    d_all[:, :width] = dq_ref[...]

    @pl.when(info[3] == 1)
    def _():
        payload = jnp.where(info[6] == 1, from_even[...], from_odd[...])
        queries, keys, values = qp_ref[...], k_ref[...], v_ref[...]
        back = payload[:, :width]
        columns = payload[:, payload.shape[1] - CHUNK :].astype(F32).T
        skip = width % CHUNK
        first = far_start(info, window)
        for h in range(heads):
            scores_ref[h] = dot_nt(keep_head(keys, h), queries)
            products_ref[h] = dot_nt(keep_head(values, h), back)
        for h in range(heads):
            at = skip + h
            lse = columns[at : at + 1, :] + columns[at + 2 * heads : at + 2 * heads + 1, :]
            at = at + heads
            delta = columns[at : at + 1, :] + columns[at + 2 * heads : at + 2 * heads + 1, :]
            bend(
                scores_ref,
                products_ref,
                probs_ref,
                ds_ref,
                h,
                bias_t,
                first,
                lambda rows: lse,
                lambda rows: delta,
                None,
                None,
                None,
            )
        d_keys, d_values = dk_in[...], dv_in[...]
        for h in range(heads):
            d_keys = d_keys + dot_nn(ds_ref[h], keep_head(queries, h))
            d_values = d_values + dot_nn(probs_ref[h], keep_head(back, h))
        d_all[:, width : 2 * width] = d_keys.astype(LOW)
        d_all[:, 2 * width :] = d_values.astype(LOW)

    @pl.when(info[3] == 0)
    def _():
        d_all[:, width : 2 * width] = dk_in[...].astype(LOW)
        d_all[:, 2 * width :] = dv_in[...].astype(LOW)

    joint = dot_tn(d_all[...], normed_ref[...]).astype(LOW)
    halves = (joint[:width, :], joint[width : 2 * width, :])
    for side in (0, 1):

        @pl.when(info[4] == side)
        def _():
            one_keep[...] = halves[side]
            one_send[...] = halves[1 - side]

    halves_two = (joint[2 * width :, :], grad_in[...])
    for side in (0, 1):

        @pl.when(info[5] == side)
        def _():
            two_keep[...] = halves_two[side]
            two_send[...] = halves_two[1 - side]

    gain_sum = jnp.zeros((1, gain.shape[1]), F32)
    for part, core in enumerate((1 - c, c)):
        spots = (aligned((2 * y + core) * CHUNK), aligned((2 * (1 - y) + core) * CHUNK))
        mine = jnp.concatenate([d_all[spots[0], :], d_all[spots[1], :]], axis=0)
        d_normed = dot_nn(mine[:, :width], wq[...])
        d_normed = d_normed + dot_nn(mine[:, width : 2 * width], wk[...])
        d_normed = d_normed + dot_nn(mine[:, 2 * width :], wv[...])
        wide = jnp.concatenate([x_all[spots[0], :], x_all[spots[1], :]], axis=0).astype(F32)
        gain_sum = gain_sum + jnp.sum(d_normed * (wide * rows_norm(wide)), axis=0, keepdims=True)
        if part == 0:
            send_ref[: 2 * CHUNK, :] = d_normed.astype(LOW)
        else:
            keep_ref[...] = d_normed
    small = jnp.concatenate([gain_sum, gain_in[...], jnp.zeros((6, gain_sum.shape[1]), F32)], axis=0)
    small_ref[...] = small
    put_small(send_ref, 2 * CHUNK, small)


def put_small(target, start, small):
    high = small.astype(LOW).astype(F32)
    target[start : start + EXTRA, :] = jnp.concatenate([high, small - high], axis=0).astype(LOW)


def get_small(source, start):
    both = source[start : start + EXTRA, :].astype(F32)
    return both[: EXTRA // 2] + both[EXTRA // 2 :]


def first_merge_kernel(keep_ref, got_ref, small_in, send_ref, own_ref, small_ref):
    local = own_ref.shape[0]
    total = (keep_ref[...] + got_ref[: 2 * local, :].astype(F32)).astype(LOW)
    own_ref[...] = total[:local, :]
    send_ref[:local, :] = total[local:, :]
    small = small_in[...] + get_small(got_ref, 2 * local)
    small_ref[...] = small
    put_small(send_ref, local, small)


def input_back_kernel(own_ref, got_ref, x_ref, dh_ref, gain, small_in, table_ref, out_ref, small_ref):
    local = own_ref.shape[0]
    d_normed = own_ref[...].astype(F32) + got_ref[:local, :].astype(F32)
    wide = x_ref[...].astype(F32)
    inverse = rows_norm(wide)
    unit = wide * inverse
    scaled = d_normed * gain[...]
    back = inverse * (scaled - unit * jnp.mean(unit * scaled, axis=-1, keepdims=True))
    out_ref[...] = (dh_ref[...] + back).astype(LOW)
    small_ref[...] = small_in[...] + get_small(got_ref, local)
    heads, buckets = table_ref.shape
    small_ref[2 : 2 + heads, :buckets] = table_ref[...]


def halve_kernel(info, *refs, bits):
    count = len(bits)
    for k, bit in enumerate(bits):
        keep, got = refs[2 * k], refs[2 * k + 1]
        send_ref, keep_ref = refs[2 * count + 2 * k], refs[2 * count + 2 * k + 1]
        half = send_ref.shape[0]
        side = (info[7] >> bit) & 1
        for first, target in ((1 - side, send_ref), (side, keep_ref)):
            rows = pl.ds(pl.multiple_of(first * half, 16), half)
            target[...] = (keep[rows, :].astype(F32) + got[rows, :].astype(F32)).astype(LOW)


def sum_kernel(*refs, count, small):
    for k in range(count):
        keep, got = refs[2 * k], refs[2 * k + 1]
        target = refs[2 * count + small + k]
        rows = keep.shape[0]
        target[:rows, :] = (keep[...].astype(F32) + got[...].astype(F32)).astype(LOW)
        if small and k == 0:
            put_small(target, rows, refs[2 * count][...])


def double_kernel(info, *refs, bits, small):
    count = len(bits)
    for k, bit in enumerate(bits):
        mine, got, target = refs[2 * k], refs[2 * k + 1], refs[2 * count + k]
        extra = EXTRA if small and k == 0 else 0
        rows = mine.shape[0] - extra
        side = (info[7] >> bit) & 1
        target[pl.ds(pl.multiple_of(side * rows, 16), rows), :] = mine[:rows, :]
        target[pl.ds(pl.multiple_of((1 - side) * rows, 16), rows), :] = got[:rows, :]
        if extra:
            put_small(target, 2 * rows, get_small(mine, rows) + get_small(got, rows))


def attention_total_kernel(info, one, one_got, two, two_got, q_ref, k_ref, v_ref, out_ref, small_ref):
    rows = q_ref.shape[0]
    first = info[4] == 0
    mine, got = one[:rows, :], one_got[:rows, :]
    q_ref[...] = jnp.where(first, mine, got).astype(F32)
    k_ref[...] = jnp.where(first, got, mine).astype(F32)
    first = info[5] == 0
    v_ref[...] = jnp.where(first, two[...], two_got[...]).astype(F32)
    out_ref[...] = jnp.where(first, two_got[...], two[...]).astype(F32)
    if one.shape[0] > rows:
        small_ref[...] = get_small(one, rows) + get_small(one_got, rows)
    else:
        small_ref[...] = jnp.zeros_like(small_ref)


def swap(values, axis, bit):
    return lax.ppermute(values, axis, [(i, i ^ bit) for i in range(lax.axis_size(axis))])


def swap_odd(values):
    ends = range(1, lax.axis_size("dp") - 1, 2)
    return lax.ppermute(values, "dp", [(i, i + 1) for i in ends] + [(i + 1, i) for i in ends])


def after(values, *others):
    return lax.optimization_barrier((values, *others))[0]


def spread(own, across=None):
    across = swap(own, "mp", 2) if across is None else across
    return own, across, swap(own, "mp", 1), swap(across, "mp", 1)


def cut(values, first, count):
    return lax.dynamic_slice_in_dim(values, first, count)


class Sums:
    def __init__(self, info, rank, orders, sends, keeps):
        self.info, self.rank, self.orders, self.keeps = info, rank, orders, list(keeps)
        self.bits = len(orders[0])
        self.tiled = all((k.shape[0] >> (self.bits - 1)) % 16 == 0 for k in keeps)
        self.step, self.small = 0, None
        self.exchange(sends)

    def exchange(self, sends):
        done = self.step if self.step < self.bits else 2 * self.bits - 1 - self.step
        self.now = [order[done] for order in self.orders]
        self.gots = [swap(v, "dp", 1 << bit) for v, bit in zip(sends, self.now)]
        self.step += 1

    def pairs(self):
        return [v for pair in zip(self.keeps, self.gots) for v in pair]

    def advance(self, token, small=None):
        self.keeps[0] = after(self.keeps[0], token)
        count = len(self.keeps)
        if self.step < self.bits:
            bits = [order[self.step] for order in self.orders]
            halves = [v.shape[0] // 2 for v in self.keeps]
            if self.tiled:
                out = call(
                    functools.partial(halve_kernel, bits=bits),
                    [shape((h, v.shape[1]), LOW) for h, v in zip(halves, self.keeps) for _ in range(2)],
                    [self.info, *self.pairs()],
                    micros=1.0,
                )
                sends, self.keeps = out[0::2], list(out[1::2])
            else:
                sends, keeps = [], []
                for k, g, h, bit in zip(self.keeps, self.gots, halves, bits):
                    side = (self.rank >> bit) & 1
                    total = (k.astype(F32) + g.astype(F32)).astype(LOW)
                    sends.append(cut(total, (1 - side) * h, h))
                    keeps.append(cut(total, side * h, h))
                self.keeps = keeps
        elif self.step == self.bits:
            if self.tiled:
                self.small = small
                rows = [v.shape[0] for v in self.keeps]
                if small is not None:
                    rows[0] += EXTRA
                sends = call(
                    functools.partial(sum_kernel, count=count, small=int(small is not None)),
                    [shape((r, v.shape[1]), LOW) for r, v in zip(rows, self.keeps)],
                    self.pairs() + ([small] if small is not None else []),
                    smem=0,
                    micros=1.0,
                )
            else:
                sends = [(k.astype(F32) + g.astype(F32)).astype(LOW) for k, g in zip(self.keeps, self.gots)]
            self.keeps = list(sends)
        else:
            has = self.small is not None
            if self.tiled:
                rows = [2 * v.shape[0] for v in self.keeps]
                if has:
                    rows[0] -= EXTRA
                sends = call(
                    functools.partial(double_kernel, bits=self.now, small=has),
                    [shape((r, v.shape[1]), LOW) for r, v in zip(rows, self.keeps)],
                    [self.info, *self.pairs()],
                    micros=1.0,
                )
            else:
                sends = []
                for k, g, bit in zip(self.keeps, self.gots, self.now):
                    side = (self.rank >> bit) & 1
                    sends.append(
                        jnp.where(side == 0, jnp.concatenate([k, g], axis=0), jnp.concatenate([g, k], axis=0))
                    )
            self.keeps = list(sends)
        self.exchange(sends)
        return sends[0]


def per_device(
    inputs,
    attention_gain,
    query_weight,
    key_weight,
    value_weight,
    out_weight,
    bias_table,
    feedforward_gain,
    gate_weight,
    up_weight,
    down_weight,
    segment,
    bucket,
    cotangent,
):
    parts = lax.axis_size("mp")
    groups = lax.axis_size("dp")
    local, d = inputs.shape
    window = local * parts
    width = query_weight.shape[1]
    heads = width // HEAD
    units = gate_weight.shape[1]
    buckets = bias_table.shape[0]
    half = 2 * local
    rank = lax.axis_index("dp")
    member = lax.axis_index("mp")
    bits = list(range(groups.bit_length() - 1))
    order_one = bits
    order_two = [bits[1], bits[0]] + bits[2:]

    x_across = swap(inputs, "mp", 2)
    from_even = swap(inputs, "dp", 1)
    from_odd = swap_odd(inputs)

    spot = jnp.stack([rank, member]).astype(jnp.int32)
    edge = jnp.full((1,), -1, jnp.int32)
    bucket_rows = jnp.concatenate([edge, bucket]).reshape(-1, CHUNK)
    table = bias_table.T
    gain_one, gain_two = attention_gain[None, :], after(feedforward_gain[None, :], spot)
    band = shape((heads, CHUNK, SPAN), F32)
    info, seg_row, seg_col, bias = call(
        functools.partial(setup_kernel, groups=groups, first_bits=(order_one[0], order_two[0])),
        [shape((8,), jnp.int32), shape((1, window), F32), shape((window, CHUNK), F32), band],
        [spot, segment.reshape(-1, CHUNK), after(bucket_rows, gain_one, gain_two), table],
        out_smem=1,
        micros=3.0,
    )
    x_pieces = (inputs, x_across, swap(inputs, "mp", 1), swap(after(x_across, bias), "mp", 1))
    out_across = swap(out_weight, "mp", 2)
    (near,) = call(near_kernel, [shape((local, d), LOW)], [info, from_even, from_odd], micros=0.5)
    out_core = swap(after(out_across, near), "mp", 1)
    near_across = swap(near, "mp", 2)
    near_core = swap(near, "mp", 1)

    low_rows = shape((window, width), LOW)
    wide_rows = shape((window, width), F32)
    stats = shape((window, CHUNK), F32)
    square_wide = pltpu.VMEM((heads, window, window), F32)
    square_low = pltpu.VMEM((heads, window, window), LOW)
    weight = shape((width, d), LOW)
    x_all, normed, queries, keys, values, acc, top, total, wq, wk, wv = call(
        own_kernel,
        [shape((window, d), LOW)] * 2 + [low_rows] * 3 + [wide_rows, stats, stats] + [weight] * 3,
        [info, after(inputs, out_core), *x_pieces[1:], gain_one, bias, seg_col, seg_row, *[in_hbm(w.T) for w in (query_weight, key_weight, value_weight)]],
        scratch=[square_wide, square_low, pltpu.SemaphoreType.DMA((3,))],
        hbm=3,
        micros=5.0,
    )
    near_pieces = (near, near_across, near_core, swap(after(near_across, acc), "mp", 1))
    cot_across = swap(after(cotangent, near), "mp", 2)
    mixed_low, mixed, lse, queries_near, keys_near, values_near = call(
        partner_kernel,
        [low_rows, wide_rows, stats] + [low_rows] * 3,
        [info, *near_pieces, gain_one, wq, wk, wv, bias, queries, acc, top, total],
        scratch=[
            pltpu.VMEM((window, d), LOW),
            square_wide,
            square_low,
            pltpu.VMEM((window, width), F32),
            pltpu.VMEM((window, CHUNK), F32),
            pltpu.VMEM((window, CHUNK), F32),
        ],
        micros=5.0,
    )
    mixed_across = swap(mixed_low, "mp", 2)
    mixed_core = swap(mixed_low, "mp", 1)
    out_pieces = (out_weight, out_across, swap(after(out_weight, mixed_core), "mp", 1), out_core)
    cot_pieces = (
        cotangent,
        cot_across,
        swap(after(cotangent, mixed_core), "mp", 1),
        swap(after(cot_across, mixed_core), "mp", 1),
    )
    bias_t, flipped_rows = call(
        flipped_kernel,
        [band, shape(bucket_rows.shape, jnp.int32)],
        [after(bucket_rows, mixed_low), table],
        smem=0,
        micros=3.0,
    )
    cot_all, d_act = call(
        cotangent_kernel,
        [shape((window, d), LOW), shape((window, units), F32)],
        [*cot_pieces, after(down_weight, mixed_low)],
        smem=0,
        micros=1.0,
    )
    mixed_pieces = (mixed_low, mixed_across, mixed_core, swap(after(mixed_across, bias_t, d_act), "mp", 1))
    second, hidden, act, d_gate, d_up, second_send, second_keep, gain_two_part = call(
        feed_kernel,
        [shape((window, d), LOW), shape((half, d), F32)]
        + [shape((window, units), LOW)] * 3
        + [shape((half, d), LOW), shape((half, d), F32), shape((1, d), F32)],
        [info, x_all, *mixed_pieces, *out_pieces, d_act, gain_two, gate_weight, up_weight],
        micros=5.0,
    )
    (second_sum,) = call(
        functools.partial(sum_kernel, count=1, small=0),
        [shape((half, d), LOW)],
        [second_keep, swap(second_send, "mp", 1)],
        smem=0,
        micros=1.0,
    )
    second_other = swap(second_sum, "mp", 2)
    rows = d + units // 2 + units // 4
    gate_send, gate_keep, up_send, up_keep = call(
        feed_grad_kernel,
        [shape((rows // 2, units), LOW)] * 4,
        [info, after(second, second_sum), d_gate, d_up, act, cot_all],
        scratch=[pltpu.VMEM((rows, units), LOW)] * 2,
        micros=3.0,
    )
    feed_sums = Sums(info, rank, (order_one, order_two), (gate_send, up_send), (gate_keep, up_keep))
    feed_send, feed_keep = call(
        feed_out_kernel, [shape((half, d), LOW)] * 2, [after(act, gate_send), down_weight], smem=0
    )
    feed_own, feed_cross = call(
        feed_merge_kernel,
        [shape((local, d), LOW)] * 2,
        [feed_keep, swap(feed_send, "mp", 1)],
        smem=0,
        micros=1.0,
    )
    second_other = after(second_other, feed_cross)
    dh, branch_low = call(
        hidden_back_kernel,
        [shape((local, d), F32), shape((half, d), LOW)],
        [second_sum, second_other, hidden, cot_pieces[0], cot_pieces[1], gain_two],
        smem=0,
    )
    payload, stat_back, out_grad = call(
        mixed_back_kernel,
        [shape((window, 2 * CHUNK), LOW), stats, shape((width, d), LOW)],
        [info, branch_low, swap(branch_low, "mp", 1), out_weight, mixed, mixed_low, lse],
        scratch=[pltpu.VMEM((window, d), LOW), pltpu.VMEM((2 * CHUNK, d), LOW)],
    )
    payload_even = swap(payload, "dp", 1)
    payload_odd = swap_odd(payload)
    token = feed_sums.advance(payload)
    fold = pltpu.VMEM((heads, CHUNK, 2 * window), F32)
    d_queries, d_keys, d_values, table_part = call(
        own_back_kernel,
        [wide_rows, wide_rows, wide_rows, shape((heads, CHUNK), F32)],
        [after(queries, token), keys, values, payload, stat_back, bias_t, seg_col, seg_row, flipped_rows],
        scratch=[square_wide, square_wide, square_low, square_low, fold],
        smem=0,
        micros=200.0,
    )
    d_queries, table_part = call(
        far_back_kernel,
        [low_rows, shape((heads, CHUNK), F32)],
        [info, queries, keys_near, values_near, payload, stat_back, bias, bucket_rows, d_queries, table_part],
        scratch=[square_wide, square_wide, square_low, fold],
        micros=3.0,
    )
    one_send, one_keep, two_send, two_keep, first_send, first_keep, small = call(
        partner_back_kernel,
        [shape((width, d), LOW)] * 4
        + [shape((half + EXTRA, d), LOW), shape((half, d), F32), shape((EXTRA // 2, d), F32)],
        [
            info,
            keys,
            values,
            queries_near,
            payload_even,
            payload_odd,
            bias_t,
            d_keys,
            d_values,
            d_queries,
            normed,
            x_all,
            gain_one,
            wq,
            wk,
            wv,
            out_grad,
            gain_two_part,
        ],
        scratch=[pltpu.VMEM((window, 3 * width), LOW), square_wide, square_wide, square_low, square_low],
        micros=300.0,
    )
    joint_sums = Sums(info, rank, (order_one, order_two), (one_send, two_send), (one_keep, two_keep))
    token = feed_sums.advance(one_send)
    first_send, first_own, small = call(
        first_merge_kernel,
        [shape((local + EXTRA, d), LOW), shape((local, d), LOW), shape((EXTRA // 2, d), F32)],
        [after(first_keep, token), swap(first_send, "mp", 1), small],
        smem=0,
        micros=1.0,
    )
    first_got = swap(first_send, "mp", 2)
    token = joint_sums.advance(first_send)
    token = feed_sums.advance(token)
    feed_got = swap(after(feed_cross, token), "mp", 2)
    input_grad, small = call(
        input_back_kernel,
        [shape((local, d), LOW), shape((EXTRA // 2, d), F32)],
        [first_own, first_got, inputs, after(dh, token), gain_one, small, table_part],
        smem=0,
        micros=1.0,
    )
    last = 2 * len(bits)
    while joint_sums.step < last - 1 or feed_sums.step < last:
        if joint_sums.step < last - 1:
            token = joint_sums.advance(token, small)
        if feed_sums.step < last:
            token = feed_sums.advance(token)
    (layer_out,) = call(
        layer_out_kernel,
        [shape((local, d), LOW)],
        [after(hidden, small), feed_own, feed_got],
        smem=0,
        micros=1.0,
    )
    ready = feed_sums.pairs()
    gate_grad, up_grad, down_grad = call(
        feed_total_kernel,
        [shape((d, units), F32)] * 2 + [shape((units, d), F32)],
        [info, after(ready[0], token), *ready[1:]],
        scratch=[pltpu.VMEM((rows, units), LOW)],
        micros=2.0,
    )
    joint_sums.advance(down_grad)
    query_grad, key_grad, value_grad, out_total, small_total = call(
        attention_total_kernel,
        [shape((width, d), F32)] * 4 + [shape((EXTRA // 2, d), F32)],
        [info, *joint_sums.pairs()],
        micros=2.0,
    )
    if not joint_sums.tiled:
        small_total = lax.psum(small, "dp")
    return (
        layer_out,
        input_grad,
        small_total[0],
        query_grad.T,
        key_grad.T,
        value_grad.T,
        out_total,
        small_total[2 : 2 + heads, :buckets].T,
        small_total[1],
        gate_grad,
        up_grad,
        down_grad,
    )


def solution(mesh):
    rows = P(("dp", "mp"), None)
    in_specs = (
        rows,
        P(),
        P(None, "mp"),
        P(None, "mp"),
        P(None, "mp"),
        P("mp", None),
        P(None, "mp"),
        P(),
        P(None, "mp"),
        P(None, "mp"),
        P("mp", None),
        P(),
        P(),
        rows,
    )
    out_specs = (
        rows,
        rows,
        P(),
        P(None, "mp"),
        P(None, "mp"),
        P(None, "mp"),
        P("mp", None),
        P(None, "mp"),
        P(),
        P(None, "mp"),
        P(None, "mp"),
        P("mp", None),
    )
    return jax.shard_map(
        per_device, mesh=mesh, in_specs=in_specs, out_specs=out_specs, check_vma=False
    )
```

profile of v0, /device:TPU:0, one launch (start us, length us, event | category | flops | bytes accessed | tf_op | source)
XLA Modules:
  0.0 176.0 jit_solution(9826180015219254368)
XLA Ops:
  0.6 3.0 %collective-permute-start = (bf16[192,768]{1,0:T(8,128)(2,1)}, bf16[192,768]{1,0:T(8,128)(2,1)S(1)}, u32[]{:S(2)}, u32[]{:S(2)}) collective-permute-start(bf16[192,768]{1,0:T(8,128)(2,1)} %out_w.1), channel_id=1, source_target_pairs={{0,2},{1,3},{2,0},{3,1},{4,6},{5,7},{6,4},{7,5},{8,10},{9,11},{10,... | collective-permute-start | bytes 884744 | tf_op jit(solution)/shard_map/ppermute | solution.py:854
  4.4 4.8 %collective-permute-start.1 = (bf16[128,768]{1,0:T(8,128)(2,1)}, bf16[128,768]{1,0:T(8,128)(2,1)S(1)}, u32[]{:S(2)}, u32[]{:S(2)}) collective-permute-start(bf16[128,768]{1,0:T(8,128)(2,1)} %x_ref.1), channel_id=1, source_target_pairs={{0,4},{4,0},{8,12},{12,8},{16,20},{20,16},{24,28},{28,24},{1,5},{5... | collective-permute-start | bytes 589832 | tf_op jit(solution)/shard_map/ppermute | solution.py:854
  12.8 3.2 %shard_map.229 = (s32[8]{0:T(128)S(1)}, f32[1,512]{1,0:T(1,128)S(1)}, f32[512,128]{1,0:T(8,128)S(1)}, f32[3,128,2048]{2,1,0:T(8,128)S(1)}) custom-call(s32[2]{0:T(128)S(1)} %pad_add_fusion.spot, s32[32,128]{1,0:T(8,128)S(1)} %bitcast.14, s32[16,128]{1,0:T(8,128)S(1)} %add_bitcast_fusion.bucket_ref, f32[3,32]{1,0:T(4,128)S(1)} %bitcast.15), custom_call_target="tpu_custom_call" | custom-call | flops 60000000 | tf_op jit(solution)/shard_map/pallas_call | solution.py:37
  20.5 4.9 %shard_map.231 = (bf16[512,768]{1,0:T(8,128)(2,1)S(1)}, bf16[512,768]{1,0:T(8,128)(2,1)S(1)}, bf16[512,192]{1,0:T(8,128)(2,1)S(1)}, bf16[512,192]{1,0:T(8,128)(2...) custom-call(s32[8]{0:T(128)S(1)} %get-tuple-element.146.info, ...), custom_call_target="tpu_custom_call" | custom-call | flops 100000000 | tf_op jit(solution)/shard_map/pallas_call | solution.py:37
  27.0 4.1 %shard_map.232 = (bf16[512,192]{1,0:T(8,128)(2,1)S(1)}, f32[512,192]{1,0:T(8,128)S(1)}, f32[512,128]{1,0:T(8,128)S(1)}, bf16[512,192]{1,0:T(8,128)(2,1)S(1)}, bf...) custom-call(s32[8]{0:T(128)S(1)} %get-tuple-element.146.info, bf16[128,768]{1,0:T(8,128)(2,1)S(1)} %shard_map.230.x0, ...), custom_call_target="tpu_custom_call" | custom-call | flops 100000000 | tf_op jit(solution)/shard_map/pallas_call | solution.py:37
  37.2 4.6 %collective-permute-done.10.m1 = bf16[512,192]{1,0:T(8,128)(2,1)S(1)} collective-permute-done((bf16[512,192]{1,0:T(8,128)(2,1)S(1)}, bf16[512,192]{1,0:T(8,128)(2,1)S(1)}, u32[]{:S(2)}, u32[]{:S(2)}) %collective-permute-start.10) | collective-permute-done | bytes 196640 | tf_op jit(solution)/shard_map/ppermute | solution.py:854
  43.3 4.4 %shard_map.235 = (bf16[512,768]{1,0:T(8,128)(2,1)S(1)}, f32[256,768]{1,0:T(8,128)S(1)}, bf16[512,512]{1,0:T(8,128)(2,1)S(1)}, bf16[512,512]{1,0:T(8,128)(2,1)S(1...) custom-call(s32[8]{0:T(128)S(1)} %get-tuple-element.146.info, ...), custom_call_target="tpu_custom_call" | custom-call | flops 100000000 | tf_op jit(solution)/shard_map/pallas_call | solution.py:37
  53.6 2.4 %collective-permute-start.24 = (bf16[576,512]{1,0:T(8,128)(2,1)S(1)}, bf16[576,512]{1,0:T(8,128)(2,1)S(1)}, u32[]{:S(2)}, u32[]{:S(2)}) collective-permute-start(bf16[576,512]{1,0:T(8,128)(2,1)S(1)} %get-tuple-element.197), channel_id=1, source_target_pairs={{0,8},{4,12},{8,0},{12,4},{16,24},{20,28},{24,16},{28,20},{1,9},{5... | collective-permute-start | bytes 1769480 | tf_op jit(solution)/shard_map/ppermute | solution.py:854
  57.7 6.2 %collective-permute-done.18.other_ref = bf16[256,768]{1,0:T(8,128)(2,1)S(1)} collective-permute-done((bf16[256,768]{1,0:T(8,128)(2,1)S(1)}, bf16[256,768]{1,0:T(8,128)(2,1)S(1)}, u32[]{:S(2)}, u32[]{:S(2)}) %collective-permute-start.18) | collective-permute-done | bytes 393248 | tf_op jit(solution)/shard_map/ppermute | solution.py:854
  68.5 5.0 %collective-permute-start.21 = (bf16[512,256]{1,0:T(8,128)(2,1)S(1)}, bf16[512,256]{1,0:T(8,128)(2,1)S(1)}, u32[]{:S(2)}, u32[]{:S(2)}) collective-permute-start(bf16[512,256]{1,0:T(8,128)(2,1)S(1)} %get-tuple-element.193.payload_ref), channel_id=1, source_target_pairs={{0,4},{4,0},{8,12},{12,8},{16,20},{20,16},{24,28},{28,24},{1,5},{5... | collective-permute-start | bytes 786440 | tf_op jit(solution)/shard_map/ppermute | solution.py:854
  76.6 3.9 %shard_map.243 = (f32[512,192]{1,0:T(8,128)S(1)}, f32[512,192]{1,0:T(8,128)S(1)}, f32[512,192]{1,0:T(8,128)S(1)}, f32[3,128]{1,0:T(4,128)S(1)}) custom-call(bf16[512,192]{1,0:T(8,128)(2,1)S(1)} %get-tuple-element.199.q_ref, bf16[512,192]{1,0:T(8,128)(2,1)S(1)} %get-tuple-element.173.k_ref, bf16[512,192]{1,0:T(8,128)(2,1)S(1)} %get-tuple-element.174.v_ref, ...), custom_call_target="tpu_custom_call" | custom-call | flops 4000000000 | tf_op jit(solution)/shard_map/pallas_call | solution.py:37
  80.4 3.1 %shard_map.244 = (bf16[512,192]{1,0:T(8,128)(2,1)S(1)}, f32[3,128]{1,0:T(4,128)S(1)}) custom-call(s32[8]{0:T(128)S(1)} %get-tuple-element.146.info, bf16[512,192]{1,0:T(8,128)(2,1)S(1)} %get-tuple-element.199.q_ref, bf16[512,192]{1,0:T(8,128)(2,1)S(1)} %get-tuple-element.204.kp_ref, bf16[512,192]{1,0:T(8,128)(2,1)S(1)} %get-tuple-element.205.vp_ref, ...), custom_call_target="tpu_custom_call" | custom-call | flops 60000000 | tf_op jit(solution)/shard_map/pallas_call | solution.py:37
  84.3 4.6 %shard_map.245 = (bf16[192,768]{1,0:T(8,128)(2,1)S(1)}, bf16[192,768]{1,0:T(8,128)(2,1)S(1)}, bf16[192,768]{1,0:T(8,128)(2,1)S(1)}, bf16[192,768]{1,0:T(8,128)(2...) custom-call(s32[8]{0:T(128)S(1)} %get-tuple-element.146.info, ...), custom_call_target="tpu_custom_call" | custom-call | flops 6000000000 | tf_op jit(solution)/shard_map/pallas_call | solution.py:37
  89.5 3.7 %collective-permute-start.29 = (bf16[192,768]{1,0:T(8,128)(2,1)S(1)}, bf16[192,768]{1,0:T(8,128)(2,1)S(1)}, u32[]{:S(2)}, u32[]{:S(2)}) collective-permute-start(bf16[192,768]{1,0:T(8,128)(2,1)S(1)} %get-tuple-element.214), channel_id=1, source_target_pairs={{0,4},{4,0},{8,12},{12,8},{16,20},{20,16},{24,28},{28,24},{1,5},{5... | collective-permute-start | bytes 884744 | tf_op jit(solution)/shard_map/ppermute | solution.py:854
  97.0 5.8 %collective-permute-done.30.refs_3_ = bf16[192,768]{1,0:T(8,128)(2,1)S(1)} collective-permute-done((bf16[192,768]{1,0:T(8,128)(2,1)S(1)}, bf16[192,768]{1,0:T(8,128)(2,1)S(1)}, u32[]{:S(2)}, u32[]{:S(2)}) %collective-permute-start.30) | collective-permute-done | bytes 294944 | tf_op jit(solution)/shard_map/ppermute | solution.py:854
  104.9 5.2 %collective-permute-done.31.refs_1_ = bf16[144,512]{1,0:T(8,128)(2,1)S(1)} collective-permute-done((bf16[144,512]{1,0:T(8,128)(2,1)S(1)}, bf16[144,512]{1,0:T(8,128)(2,1)S(1)}, u32[]{:S(2)}, u32[]{:S(2)}) %collective-permute-start.31) | collective-permute-done | bytes 147488 | tf_op jit(solution)/shard_map/ppermute | solution.py:854
  110.3 2.9 %collective-permute-start.36 = (bf16[144,512]{1,0:T(8,128)(2,1)S(1)}, bf16[144,512]{1,0:T(8,128)(2,1)S(1)}, u32[]{:S(2)}, u32[]{:S(2)}) collective-permute-start(bf16[144,512]{1,0:T(8,128)(2,1)S(1)} %get-tuple-element.249.refs_0_), channel_id=1, source_target_pairs={{0,16},{4,20},{8,24},{12,28},{16,0},{20,4},{24,8},{28,12},{1,17},{... | collective-permute-start | bytes 442376 | tf_op jit(solution)/shard_map/ppermute | solution.py:854
  113.8 8.2 %collective-permute-done.37.refs_3_ = bf16[144,512]{1,0:T(8,128)(2,1)S(1)} collective-permute-done((bf16[144,512]{1,0:T(8,128)(2,1)S(1)}, bf16[144,512]{1,0:T(8,128)(2,1)S(1)}, u32[]{:S(2)}, u32[]{:S(2)}) %collective-permute-start.37) | collective-permute-done | bytes 147488 | tf_op jit(solution)/shard_map/ppermute | solution.py:854
  122.0 3.1 %collective-permute-done.36.refs_1_ = bf16[144,512]{1,0:T(8,128)(2,1)S(1)} collective-permute-done((bf16[144,512]{1,0:T(8,128)(2,1)S(1)}, bf16[144,512]{1,0:T(8,128)(2,1)S(1)}, u32[]{:S(2)}, u32[]{:S(2)}) %collective-permute-start.36) | collective-permute-done | bytes 147488 | tf_op jit(solution)/shard_map/ppermute | solution.py:854
  130.5 2.9 %collective-permute-done.28.got_ref = bf16[144,768]{1,0:T(8,128)(2,1)S(1)} collective-permute-done((bf16[144,768]{1,0:T(8,128)(2,1)S(1)}, bf16[144,768]{1,0:T(8,128)(2,1)S(1)}, u32[]{:S(2)}, u32[]{:S(2)}) %collective-permute-start.28) | collective-permute-done | bytes 221216 | tf_op jit(solution)/shard_map/ppermute | solution.py:854
  143.5 11.5 %collective-permute-done.43.refs_3_ = bf16[48,768]{1,0:T(8,128)(2,1)S(1)} collective-permute-done((bf16[48,768]{1,0:T(8,128)(2,1)S(1)}, bf16[48,768]{1,0:T(8,128)(2,1)S(1)}, u32[]{:S(2)}, u32[]{:S(2)}) %collective-permute-start.43) | collective-permute-done | bytes 73760 | tf_op jit(solution)/shard_map/ppermute | solution.py:854
  155.6 3.2 %collective-permute-start.46 = (bf16[112,768]{1,0:T(8,128)(2,1)S(1)}, bf16[112,768]{1,0:T(8,128)(2,1)S(1)}, u32[]{:S(2)}, u32[]{:S(2)}) collective-permute-start(bf16[112,768]{1,0:T(8,128)(2,1)S(1)} %get-tuple-element.265.refs_0_), channel_id=1, source_target_pairs={{0,8},{4,12},{8,0},{12,4},{16,24},{20,28},{24,16},{28,20},{1,9},{5... | collective-permute-start | bytes 516104 | tf_op jit(solution)/shard_map/ppermute | solution.py:854
  160.2 3.1 %shard_map.257 = (f32[768,512]{1,0:T(8,128)}, f32[768,512]{1,0:T(8,128)}, f32[512,768]{1,0:T(8,128)}) custom-call(s32[8]{0:T(128)S(1)} %get-tuple-element.146.info, bf16[576,512]{1,0:T(8,128)(2,1)S(1)} %get-tuple-element.262.one, bf16[576,512]{1,0:T(8,128)(2,1)S(1)} %collective-permute-done.44.one_got, bf16[576,512]{1,0:T(8,128)(2,1)S(1)} %get-tuple-element.263.two, ...), custom_call_target="tpu_custom_call" | custom-call | flops 40000000 | tf_op jit(solution)/shard_map/pallas_call | solution.py:37
  167.4 4.6 %collective-permute-done.33.got_ref = bf16[128,768]{1,0:T(8,128)(2,1)S(1)} collective-permute-done((bf16[128,768]{1,0:T(8,128)(2,1)S(1)}, bf16[128,768]{1,0:T(8,128)(2,1)S(1)}, u32[]{:S(2)}, u32[]{:S(2)}) %collective-permute-start.33) | collective-permute-done | bytes 196640 | tf_op jit(solution)/shard_map/ppermute | solution.py:854
  (133 shorter events, 66.6 us)
Async XLA Ops:
  0.6 16.5 %collective-permute-start = (bf16[192,768]{1,0:T(8,128)(2,1)}, bf16[192,768]{1,0:T(8,128)(2,1)S(1)}, u32[]{:S(2)}, u32[]{:S(2)}) collective-permute-start(bf16[192,768]{1,0:T(8,128)(2,1)} %out_w.1), channel_id=1, source_target_pairs={{0,2},{1,3},{2,0},{3,1},{4,6},{5,7},{6,4},{7,5},{8,10},{9,11},{10,... | collective-permute-start | bytes 884744 | tf_op jit(solution)/shard_map/ppermute | solution.py:854
  3.7 14.1 %collective-permute-start.4 = (bf16[128,768]{1,0:T(8,128)(2,1)}, bf16[128,768]{1,0:T(8,128)(2,1)S(1)}, u32[]{:S(2)}, u32[]{:S(2)}) collective-permute-start(bf16[128,768]{1,0:T(8,128)(2,1)} %x_ref.1), channel_id=1, source_target_pairs={{0,2},{1,3},{2,0},{3,1},{4,6},{5,7},{6,4},{7,5},{8,10},{9,11},{10,... | collective-permute-start | bytes 589832 | tf_op jit(solution)/shard_map/ppermute | solution.py:854
  3.8 12.2 %collective-permute-start.2 = (bf16[128,768]{1,0:T(8,128)(2,1)}, bf16[128,768]{1,0:T(8,128)(2,1)S(1)}, u32[]{:S(2)}, u32[]{:S(2)}) collective-permute-start(bf16[128,768]{1,0:T(8,128)(2,1)} %x_ref.1), channel_id=1, source_target_pairs={{4,8},{12,16},{20,24},{8,4},{16,12},{24,20},{5,9},{13,17},{21,25},... | collective-permute-start | bytes 589832 | tf_op jit(solution)/shard_map/ppermute | solution.py:859
  4.4 12.2 %collective-permute-start.1 = (bf16[128,768]{1,0:T(8,128)(2,1)}, bf16[128,768]{1,0:T(8,128)(2,1)S(1)}, u32[]{:S(2)}, u32[]{:S(2)}) collective-permute-start(bf16[128,768]{1,0:T(8,128)(2,1)} %x_ref.1), channel_id=1, source_target_pairs={{0,4},{4,0},{8,12},{12,8},{16,20},{20,16},{24,28},{28,24},{1,5},{5... | collective-permute-start | bytes 589832 | tf_op jit(solution)/shard_map/ppermute | solution.py:854
  52.4 11.4 %collective-permute-start.18 = (bf16[256,768]{1,0:T(8,128)(2,1)S(1)}, bf16[256,768]{1,0:T(8,128)(2,1)S(1)}, u32[]{:S(2)}, u32[]{:S(2)}) collective-permute-start(bf16[256,768]{1,0:T(8,128)(2,1)S(1)} %shard_map.236.sum_ref), channel_id=1, source_target_pairs={{0,2},{1,3},{2,0},{3,1},{4,6},{5,7},{6,4},{7,5},{8,10},{9,11},{10,... | collective-permute-start | bytes 1179656 | tf_op jit(solution)/shard_map/ppermute | solution.py:854
  53.6 19.9 %collective-permute-start.24 = (bf16[576,512]{1,0:T(8,128)(2,1)S(1)}, bf16[576,512]{1,0:T(8,128)(2,1)S(1)}, u32[]{:S(2)}, u32[]{:S(2)}) collective-permute-start(bf16[576,512]{1,0:T(8,128)(2,1)S(1)} %get-tuple-element.197), channel_id=1, source_target_pairs={{0,8},{4,12},{8,0},{12,4},{16,24},{20,28},{24,16},{28,20},{1,9},{5... | collective-permute-start | bytes 1769480 | tf_op jit(solution)/shard_map/ppermute | solution.py:854
  56.1 17.4 %collective-permute-start.23 = (bf16[576,512]{1,0:T(8,128)(2,1)S(1)}, bf16[576,512]{1,0:T(8,128)(2,1)S(1)}, u32[]{:S(2)}, u32[]{:S(2)}) collective-permute-start(bf16[576,512]{1,0:T(8,128)(2,1)S(1)} %get-tuple-element.184), channel_id=1, source_target_pairs={{0,4},{4,0},{8,12},{12,8},{16,20},{20,16},{24,28},{28,24},{1,5},{5... | collective-permute-start | bytes 1769480 | tf_op jit(solution)/shard_map/ppermute | solution.py:854
  67.6 15.9 %collective-permute-start.22 = (bf16[512,256]{1,0:T(8,128)(2,1)S(1)}, bf16[512,256]{1,0:T(8,128)(2,1)S(1)}, u32[]{:S(2)}, u32[]{:S(2)}) collective-permute-start(bf16[512,256]{1,0:T(8,128)(2,1)S(1)} %get-tuple-element.193.payload_ref), channel_id=1, source_target_pairs={{4,8},{12,16},{20,24},{8,4},{16,12},{24,20},{5,9},{13,17},{21,25},... | collective-permute-start | bytes 786440 | tf_op jit(solution)/shard_map/ppermute | solution.py:859
  68.5 15.8 %collective-permute-start.21 = (bf16[512,256]{1,0:T(8,128)(2,1)S(1)}, bf16[512,256]{1,0:T(8,128)(2,1)S(1)}, u32[]{:S(2)}, u32[]{:S(2)}) collective-permute-start(bf16[512,256]{1,0:T(8,128)(2,1)S(1)} %get-tuple-element.193.payload_ref), channel_id=1, source_target_pairs={{0,4},{4,0},{8,12},{12,8},{16,20},{20,16},{24,28},{28,24},{1,5},{5... | collective-permute-start | bytes 786440 | tf_op jit(solution)/shard_map/ppermute | solution.py:854
  74.3 18.9 %collective-permute-start.25 = (bf16[288,512]{1,0:T(8,128)(2,1)S(1)}, bf16[288,512]{1,0:T(8,128)(2,1)S(1)}, u32[]{:S(2)}, u32[]{:S(2)}) collective-permute-start(bf16[288,512]{1,0:T(8,128)(2,1)S(1)} %get-tuple-element.198), channel_id=1, source_target_pairs={{0,8},{4,12},{8,0},{12,4},{16,24},{20,28},{24,16},{28,20},{1,9},{5... | collective-permute-start | bytes 884744 | tf_op jit(solution)/shard_map/ppermute | solution.py:854
  76.2 17.0 %collective-permute-start.26 = (bf16[288,512]{1,0:T(8,128)(2,1)S(1)}, bf16[288,512]{1,0:T(8,128)(2,1)S(1)}, u32[]{:S(2)}, u32[]{:S(2)}) collective-permute-start(bf16[288,512]{1,0:T(8,128)(2,1)S(1)} %get-tuple-element.217), channel_id=1, source_target_pairs={{0,4},{4,0},{8,12},{12,8},{16,20},{20,16},{24,28},{28,24},{1,5},{5... | collective-permute-start | bytes 884744 | tf_op jit(solution)/shard_map/ppermute | solution.py:854
  89.0 13.7 %collective-permute-start.30 = (bf16[192,768]{1,0:T(8,128)(2,1)S(1)}, bf16[192,768]{1,0:T(8,128)(2,1)S(1)}, u32[]{:S(2)}, u32[]{:S(2)}) collective-permute-start(bf16[192,768]{1,0:T(8,128)(2,1)S(1)} %get-tuple-element.229), channel_id=1, source_target_pairs={{0,8},{4,12},{8,0},{12,4},{16,24},{20,28},{24,16},{28,20},{1,9},{5... | collective-permute-start | bytes 884744 | tf_op jit(solution)/shard_map/ppermute | solution.py:854
  89.5 13.2 %collective-permute-start.29 = (bf16[192,768]{1,0:T(8,128)(2,1)S(1)}, bf16[192,768]{1,0:T(8,128)(2,1)S(1)}, u32[]{:S(2)}, u32[]{:S(2)}) collective-permute-start(bf16[192,768]{1,0:T(8,128)(2,1)S(1)} %get-tuple-element.214), channel_id=1, source_target_pairs={{0,4},{4,0},{8,12},{12,8},{16,20},{20,16},{24,28},{28,24},{1,5},{5... | collective-permute-start | bytes 884744 | tf_op jit(solution)/shard_map/ppermute | solution.py:854
  93.9 11.0 %collective-permute-start.32 = (bf16[144,512]{1,0:T(8,128)(2,1)S(1)}, bf16[144,512]{1,0:T(8,128)(2,1)S(1)}, u32[]{:S(2)}, u32[]{:S(2)}) collective-permute-start(bf16[144,512]{1,0:T(8,128)(2,1)S(1)} %get-tuple-element.233), channel_id=1, source_target_pairs={{0,16},{4,20},{8,24},{12,28},{16,0},{20,4},{24,8},{28,12},{1,17},{... | collective-permute-start | bytes 442376 | tf_op jit(solution)/shard_map/ppermute | solution.py:854
  95.1 15.1 %collective-permute-start.31 = (bf16[144,512]{1,0:T(8,128)(2,1)S(1)}, bf16[144,512]{1,0:T(8,128)(2,1)S(1)}, u32[]{:S(2)}, u32[]{:S(2)}) collective-permute-start(bf16[144,512]{1,0:T(8,128)(2,1)S(1)} %get-tuple-element.218), channel_id=1, source_target_pairs={{0,16},{4,20},{8,24},{12,28},{16,0},{20,4},{24,8},{28,12},{1,17},{... | collective-permute-start | bytes 442376 | tf_op jit(solution)/shard_map/ppermute | solution.py:854
  103.4 9.8 %collective-permute-start.34 = (bf16[96,768]{1,0:T(8,128)(2,1)S(1)}, bf16[96,768]{1,0:T(8,128)(2,1)S(1)}, u32[]{:S(2)}, u32[]{:S(2)}) collective-permute-start(bf16[96,768]{1,0:T(8,128)(2,1)S(1)} %get-tuple-element.230), channel_id=1, source_target_pairs={{0,8},{4,12},{8,0},{12,4},{16,24},{20,28},{24,16},{28,20},{1,9},{5... | collective-permute-start | bytes 442376 | tf_op jit(solution)/shard_map/ppermute | solution.py:854
  110.2 11.8 %collective-permute-start.37 = (bf16[144,512]{1,0:T(8,128)(2,1)S(1)}, bf16[144,512]{1,0:T(8,128)(2,1)S(1)}, u32[]{:S(2)}, u32[]{:S(2)}) collective-permute-start(bf16[144,512]{1,0:T(8,128)(2,1)S(1)} %get-tuple-element.250.refs_2_), channel_id=1, source_target_pairs={{0,16},{4,20},{8,24},{12,28},{16,0},{20,4},{24,8},{28,12},{1,17},{... | collective-permute-start | bytes 442376 | tf_op jit(solution)/shard_map/ppermute | solution.py:854
  110.3 14.8 %collective-permute-start.36 = (bf16[144,512]{1,0:T(8,128)(2,1)S(1)}, bf16[144,512]{1,0:T(8,128)(2,1)S(1)}, u32[]{:S(2)}, u32[]{:S(2)}) collective-permute-start(bf16[144,512]{1,0:T(8,128)(2,1)S(1)} %get-tuple-element.249.refs_0_), channel_id=1, source_target_pairs={{0,16},{4,20},{8,24},{12,28},{16,0},{20,4},{24,8},{28,12},{1,17},{... | collective-permute-start | bytes 442376 | tf_op jit(solution)/shard_map/ppermute | solution.py:854
  125.6 10.4 %collective-permute-start.41 = (bf16[288,512]{1,0:T(8,128)(2,1)S(1)}, bf16[288,512]{1,0:T(8,128)(2,1)S(1)}, u32[]{:S(2)}, u32[]{:S(2)}) collective-permute-start(bf16[288,512]{1,0:T(8,128)(2,1)S(1)} %get-tuple-element.257.refs_2_), channel_id=1, source_target_pairs={{0,4},{4,0},{8,12},{12,8},{16,20},{20,16},{24,28},{28,24},{1,5},{5... | collective-permute-start | bytes 884744 | tf_op jit(solution)/shard_map/ppermute | solution.py:854
  126.4 11.7 %collective-permute-start.40 = (bf16[288,512]{1,0:T(8,128)(2,1)S(1)}, bf16[288,512]{1,0:T(8,128)(2,1)S(1)}, u32[]{:S(2)}, u32[]{:S(2)}) collective-permute-start(bf16[288,512]{1,0:T(8,128)(2,1)S(1)} %get-tuple-element.256.refs_0_), channel_id=1, source_target_pairs={{0,8},{4,12},{8,0},{12,4},{16,24},{20,28},{24,16},{28,20},{1,9},{5... | collective-permute-start | bytes 884744 | tf_op jit(solution)/shard_map/ppermute | solution.py:854
  138.8 21.5 %collective-permute-start.45 = (bf16[576,512]{1,0:T(8,128)(2,1)S(1)}, bf16[576,512]{1,0:T(8,128)(2,1)S(1)}, u32[]{:S(2)}, u32[]{:S(2)}) collective-permute-start(bf16[576,512]{1,0:T(8,128)(2,1)S(1)} %get-tuple-element.263.two), channel_id=1, source_target_pairs={{0,8},{4,12},{8,0},{12,4},{16,24},{20,28},{24,16},{28,20},{1,9},{5... | collective-permute-start | bytes 1769480 | tf_op jit(solution)/shard_map/ppermute | solution.py:854
  139.4 20.8 %collective-permute-start.44 = (bf16[576,512]{1,0:T(8,128)(2,1)S(1)}, bf16[576,512]{1,0:T(8,128)(2,1)S(1)}, u32[]{:S(2)}, u32[]{:S(2)}) collective-permute-start(bf16[576,512]{1,0:T(8,128)(2,1)S(1)} %get-tuple-element.262.one), channel_id=1, source_target_pairs={{0,4},{4,0},{8,12},{12,8},{16,20},{20,16},{24,28},{28,24},{1,5},{5... | collective-permute-start | bytes 1769480 | tf_op jit(solution)/shard_map/ppermute | solution.py:854
  140.5 14.5 %collective-permute-start.42 = (bf16[64,768]{1,0:T(8,128)(2,1)S(1)}, bf16[64,768]{1,0:T(8,128)(2,1)S(1)}, u32[]{:S(2)}, u32[]{:S(2)}) collective-permute-start(bf16[64,768]{1,0:T(8,128)(2,1)S(1)} %get-tuple-element.259.refs_0_), channel_id=1, source_target_pairs={{0,16},{4,20},{8,24},{12,28},{16,0},{20,4},{24,8},{28,12},{1,17},{... | collective-permute-start | bytes 294920 | tf_op jit(solution)/shard_map/ppermute | solution.py:854
  142.2 12.8 %collective-permute-start.43 = (bf16[48,768]{1,0:T(8,128)(2,1)S(1)}, bf16[48,768]{1,0:T(8,128)(2,1)S(1)}, u32[]{:S(2)}, u32[]{:S(2)}) collective-permute-start(bf16[48,768]{1,0:T(8,128)(2,1)S(1)} %get-tuple-element.260.refs_2_), channel_id=1, source_target_pairs={{0,16},{4,20},{8,24},{12,28},{16,0},{20,4},{24,8},{28,12},{1,17},{... | collective-permute-start | bytes 221192 | tf_op jit(solution)/shard_map/ppermute | solution.py:854
  (36 other events, 230.7 us)
where the time goes:
time: 176 us
  waiting for transfers between devices  64.1 us (36%)
  starting transfers between devices  57 us (32%)
  Pallas kernels  48.1 us (27%)
  local copies, waits for them, and re-layouts  4.93 us (3%)
    ppermute x48, waiting for transfers between devices, swap(): lax.ppermute(values, axis, [(i, i ^ bit) for i in range(lax.axis_size(axi...  64.1 us
    ppermute x48, starting transfers between devices, swap(): lax.ppermute(values, axis, [(i, i ^ bit) for i in range(lax.axis_size(axi...  55.5 us
    pallas_call x31, Pallas kernels, call(): pl.pallas_call(kernel, out_shape=outs, in_specs=[SMEM] * smem + [VMEM] *...  48.1 us
  transfers between devices with their start and end apart: 50, of which 20 were waited for; matrix products, arithmetic and copies ran while one was open for 1% of the time, Pallas kernels for 21%

commit v1 on v0

--- a/solution.py
+++ b/solution.py
@@ -64,6 +64,10 @@
 
 def rows_norm(values):
     return lax.rsqrt(jnp.mean(values * values, axis=-1, keepdims=True) + 1e-06)
+
+
+def as_row(ref):
+    return jnp.concatenate([ref[k : k + 1, :] for k in range(ref.shape[0])], axis=1)
 
 
 def aligned(start):
@@ -229,7 +233,7 @@
         low = piece[...]
         x_all[rows, :] = low
         wide = low.astype(F32)
-        normed_ref[rows, :] = (wide * rows_norm(wide) * gain[...]).astype(LOW)
+        normed_ref[rows, :] = (wide * rows_norm(wide) * as_row(gain)).astype(LOW)
     for copy in copies:
         copy.wait()
     project(normed_ref[...], slice(None), wq, wk, wv, q_ref, k_ref, v_ref)
@@ -288,7 +292,7 @@
     def _():
         for piece, spot in zip((x0, x1, x2, x3), place(info[0], info[1])):
             wide = piece[...].astype(F32)
-            normed_ref[aligned(spot * CHUNK), :] = (wide * rows_norm(wide) * gain[...]).astype(LOW)
+            normed_ref[aligned(spot * CHUNK), :] = (wide * rows_norm(wide) * as_row(gain)).astype(LOW)
         project(normed_ref[...], slice(None), wq, wk, wv, qp_ref, kp_ref, vp_ref)
         attend(
             q_ref[...],
@@ -362,7 +366,7 @@
 ):
     y, c = info[0], info[1]
     half = 2 * CHUNK
-    gain_sum = jnp.zeros((1, gain.shape[1]), F32)
+    gain_sum = jnp.zeros((1, x_all.shape[1]), F32)
     for part, core in enumerate((1 - c, c)):
         rows = slice(part * half, (part + 1) * half)
         spots = (aligned((2 * y + core) * CHUNK), aligned((2 * (1 - y) + core) * CHUNK))
@@ -378,7 +382,7 @@
         if part == 1:
             hidden_ref[...] = hidden
         unit = hidden * rows_norm(hidden)
-        second = (unit * gain[...]).astype(LOW)
+        second = (unit * as_row(gain)).astype(LOW)
         second_ref[rows, :] = second
         gate = dot_nn(second, gate_w[...])
         up = dot_nn(second, up_w[...])
@@ -464,7 +468,7 @@
         hidden = hidden_ref[rows, :]
         inverse = rows_norm(hidden)
         unit = hidden * inverse
-        scaled = d_second * gain[...]
+        scaled = d_second * as_row(gain)
         dh = cot[...].astype(F32) + inverse * (scaled - unit * jnp.mean(unit * scaled, axis=-1, keepdims=True))
         low_ref[rows, :] = dh.astype(LOW)
         if part == 0:
@@ -748,7 +752,7 @@
             two_keep[...] = halves_two[side]
             two_send[...] = halves_two[1 - side]
 
-    gain_sum = jnp.zeros((1, gain.shape[1]), F32)
+    gain_sum = jnp.zeros((1, x_all.shape[1]), F32)
     for part, core in enumerate((1 - c, c)):
         spots = (aligned((2 * y + core) * CHUNK), aligned((2 * (1 - y) + core) * CHUNK))
         mine = jnp.concatenate([d_all[spots[0], :], d_all[spots[1], :]], axis=0)
@@ -792,7 +796,7 @@
     wide = x_ref[...].astype(F32)
     inverse = rows_norm(wide)
     unit = wide * inverse
-    scaled = d_normed * gain[...]
+    scaled = d_normed * as_row(gain)
     back = inverse * (scaled - unit * jnp.mean(unit * scaled, axis=-1, keepdims=True))
     out_ref[...] = (dh_ref[...] + back).astype(LOW)
     small_ref[...] = small_in[...] + get_small(got_ref, local)
@@ -820,6 +824,16 @@
         target[:rows, :] = (keep[...].astype(F32) + got[...].astype(F32)).astype(LOW)
         if small and k == 0:
             put_small(target, rows, refs[2 * count][...])
+
+
+def pair_kernel(*refs, count, small):
+    for k in range(count):
+        mine, got, target = refs[2 * k], refs[2 * k + 1], refs[2 * count + k]
+        extra = EXTRA if small and k == 0 else 0
+        rows = mine.shape[0] - extra
+        target[:rows, :] = (mine[:rows, :].astype(F32) + got[:rows, :].astype(F32)).astype(LOW)
+        if extra:
+            put_small(target, rows, get_small(mine, rows) + get_small(got, rows))
 
 
 def double_kernel(info, *refs, bits, small):
@@ -876,12 +890,12 @@
     def __init__(self, info, rank, orders, sends, keeps):
         self.info, self.rank, self.orders, self.keeps = info, rank, orders, list(keeps)
         self.bits = len(orders[0])
-        self.tiled = all((k.shape[0] >> (self.bits - 1)) % 16 == 0 for k in keeps)
+        self.tiled = all((k.shape[0] >> (self.bits - 2)) % 16 == 0 for k in keeps)
         self.step, self.small = 0, None
         self.exchange(sends)
 
     def exchange(self, sends):
-        done = self.step if self.step < self.bits else 2 * self.bits - 1 - self.step
+        done = self.step if self.step < self.bits else 2 * self.bits - 2 - self.step
         self.now = [order[done] for order in self.orders]
         self.gots = [swap(v, "dp", 1 << bit) for v, bit in zip(sends, self.now)]
         self.step += 1
@@ -889,10 +903,10 @@
     def pairs(self):
         return [v for pair in zip(self.keeps, self.gots) for v in pair]
 
-    def advance(self, token, small=None):
+    def advance(self, token, small=None, micros=1):
         self.keeps[0] = after(self.keeps[0], token)
         count = len(self.keeps)
-        if self.step < self.bits:
+        if self.step < self.bits - 1:
             bits = [order[self.step] for order in self.orders]
             halves = [v.shape[0] // 2 for v in self.keeps]
             if self.tiled:
@@ -900,7 +914,7 @@
                     functools.partial(halve_kernel, bits=bits),
                     [shape((h, v.shape[1]), LOW) for h, v in zip(halves, self.keeps) for _ in range(2)],
                     [self.info, *self.pairs()],
-                    micros=1.0,
+                    micros=micros,
                 )
                 sends, self.keeps = out[0::2], list(out[1::2])
             else:
@@ -911,7 +925,7 @@
                     sends.append(cut(total, (1 - side) * h, h))
                     keeps.append(cut(total, side * h, h))
                 self.keeps = keeps
-        elif self.step == self.bits:
+        elif self.step == self.bits - 1:
             if self.tiled:
                 self.small = small
                 rows = [v.shape[0] for v in self.keeps]
@@ -922,7 +936,19 @@
                     [shape((r, v.shape[1]), LOW) for r, v in zip(rows, self.keeps)],
                     self.pairs() + ([small] if small is not None else []),
                     smem=0,
-                    micros=1.0,
+                    micros=micros,
+                )
+            else:
+                sends = [(k.astype(F32) + g.astype(F32)).astype(LOW) for k, g in zip(self.keeps, self.gots)]
+            self.keeps = list(sends)
+        elif self.step == self.bits:
+            if self.tiled:
+                sends = call(
+                    functools.partial(pair_kernel, count=count, small=self.small is not None),
+                    [shape(v.shape, LOW) for v in self.keeps],
+                    self.pairs(),
+                    smem=0,
+                    micros=micros,
                 )
             else:
                 sends = [(k.astype(F32) + g.astype(F32)).astype(LOW) for k, g in zip(self.keeps, self.gots)]
@@ -937,7 +963,7 @@
                     functools.partial(double_kernel, bits=self.now, small=has),
                     [shape((r, v.shape[1]), LOW) for r, v in zip(rows, self.keeps)],
                     [self.info, *self.pairs()],
-                    micros=1.0,
+                    micros=micros,
                 )
             else:
                 sends = []
@@ -990,17 +1016,18 @@
     edge = jnp.full((1,), -1, jnp.int32)
     bucket_rows = jnp.concatenate([edge, bucket]).reshape(-1, CHUNK)
     table = bias_table.T
-    gain_one, gain_two = attention_gain[None, :], after(feedforward_gain[None, :], spot)
+    gain_one, gain_two = attention_gain.reshape(-1, CHUNK), feedforward_gain.reshape(-1, CHUNK)
     band = shape((heads, CHUNK, SPAN), F32)
     info, seg_row, seg_col, bias = call(
         functools.partial(setup_kernel, groups=groups, first_bits=(order_one[0], order_two[0])),
         [shape((8,), jnp.int32), shape((1, window), F32), shape((window, CHUNK), F32), band],
-        [spot, segment.reshape(-1, CHUNK), after(bucket_rows, gain_one, gain_two), table],
+        [spot, segment.reshape(-1, CHUNK), bucket_rows, table],
         out_smem=1,
         micros=3.0,
     )
     x_pieces = (inputs, x_across, swap(inputs, "mp", 1), swap(after(x_across, bias), "mp", 1))
     out_across = swap(out_weight, "mp", 2)
+    cot_across = swap(cotangent, "mp", 2)
     (near,) = call(near_kernel, [shape((local, d), LOW)], [info, from_even, from_odd], micros=0.5)
     out_core = swap(after(out_across, near), "mp", 1)
     near_across = swap(near, "mp", 2)
@@ -1021,11 +1048,11 @@
         micros=5.0,
     )
     near_pieces = (near, near_across, near_core, swap(after(near_across, acc), "mp", 1))
-    cot_across = swap(after(cotangent, near), "mp", 2)
+    cot_pieces = (cotangent, cot_across, swap(after(cotangent, near), "mp", 1), swap(after(cot_across, acc), "mp", 1))
     mixed_low, mixed, lse, queries_near, keys_near, values_near = call(
         partner_kernel,
         [low_rows, wide_rows, stats] + [low_rows] * 3,
-        [info, *near_pieces, gain_one, wq, wk, wv, bias, queries, acc, top, total],
+        [info, *near_pieces, gain_one, wq, wk, wv, bias, queries, after(acc, cot_pieces[3]), top, total],
         scratch=[
             pltpu.VMEM((window, d), LOW),
             square_wide,
@@ -1039,12 +1066,6 @@
     mixed_across = swap(mixed_low, "mp", 2)
     mixed_core = swap(mixed_low, "mp", 1)
     out_pieces = (out_weight, out_across, swap(after(out_weight, mixed_core), "mp", 1), out_core)
-    cot_pieces = (
-        cotangent,
-        cot_across,
-        swap(after(cotangent, mixed_core), "mp", 1),
-        swap(after(cot_across, mixed_core), "mp", 1),
-    )
     bias_t, flipped_rows = call(
         flipped_kernel,
         [band, shape(bucket_rows.shape, jnp.int32)],
@@ -1086,26 +1107,27 @@
     )
     feed_sums = Sums(info, rank, (order_one, order_two), (gate_send, up_send), (gate_keep, up_keep))
     feed_send, feed_keep = call(
-        feed_out_kernel, [shape((half, d), LOW)] * 2, [after(act, gate_send), down_weight], smem=0
-    )
-    feed_own, feed_cross = call(
-        feed_merge_kernel,
-        [shape((local, d), LOW)] * 2,
-        [feed_keep, swap(feed_send, "mp", 1)],
-        smem=0,
-        micros=1.0,
-    )
-    second_other = after(second_other, feed_cross)
+        feed_out_kernel, [shape((half, d), LOW)] * 2, [after(act, gate_send), down_weight], smem=0, micros=30
+    )
+    feed_got = swap(feed_send, "mp", 1)
+    second_other = after(second_other, feed_send)
     dh, branch_low = call(
         hidden_back_kernel,
         [shape((local, d), F32), shape((half, d), LOW)],
         [second_sum, second_other, hidden, cot_pieces[0], cot_pieces[1], gain_two],
         smem=0,
     )
+    feed_own, feed_cross = call(
+        feed_merge_kernel,
+        [shape((local, d), LOW)] * 2,
+        [after(feed_keep, branch_low), feed_got],
+        smem=0,
+        micros=100,
+    )
     payload, stat_back, out_grad = call(
         mixed_back_kernel,
         [shape((window, 2 * CHUNK), LOW), stats, shape((width, d), LOW)],
-        [info, branch_low, swap(branch_low, "mp", 1), out_weight, mixed, mixed_low, lse],
+        [info, after(branch_low, feed_cross), swap(branch_low, "mp", 1), out_weight, mixed, mixed_low, lse],
         scratch=[pltpu.VMEM((window, d), LOW), pltpu.VMEM((2 * CHUNK, d), LOW)],
     )
     payload_even = swap(payload, "dp", 1)
@@ -1118,7 +1140,7 @@
         [after(queries, token), keys, values, payload, stat_back, bias_t, seg_col, seg_row, flipped_rows],
         scratch=[square_wide, square_wide, square_low, square_low, fold],
         smem=0,
-        micros=200.0,
+        micros=200,
     )
     d_queries, table_part = call(
         far_back_kernel,
@@ -1152,54 +1174,57 @@
             gain_two_part,
         ],
         scratch=[pltpu.VMEM((window, 3 * width), LOW), square_wide, square_wide, square_low, square_low],
-        micros=300.0,
+        micros=300,
     )
     joint_sums = Sums(info, rank, (order_one, order_two), (one_send, two_send), (one_keep, two_keep))
-    token = feed_sums.advance(one_send)
+    token = feed_sums.advance(one_send, micros=300)
     first_send, first_own, small = call(
         first_merge_kernel,
         [shape((local + EXTRA, d), LOW), shape((local, d), LOW), shape((EXTRA // 2, d), F32)],
         [after(first_keep, token), swap(first_send, "mp", 1), small],
         smem=0,
-        micros=1.0,
+        micros=1,
     )
     first_got = swap(first_send, "mp", 2)
     token = joint_sums.advance(first_send)
-    token = feed_sums.advance(token)
-    feed_got = swap(after(feed_cross, token), "mp", 2)
     input_grad, small = call(
         input_back_kernel,
         [shape((local, d), LOW), shape((EXTRA // 2, d), F32)],
         [first_own, first_got, inputs, after(dh, token), gain_one, small, table_part],
         smem=0,
-        micros=1.0,
-    )
-    last = 2 * len(bits)
-    while joint_sums.step < last - 1 or feed_sums.step < last:
-        if joint_sums.step < last - 1:
-            token = joint_sums.advance(token, small)
+        micros=1,
+    )
+    token = joint_sums.advance(small, small)
+    token = feed_sums.advance(token)
+    feed_got = swap(after(feed_cross, token), "mp", 2)
+    token = joint_sums.advance(token, small, micros=1)
+    token = feed_sums.advance(token)
+    last = 2 * len(bits) - 1
+    while joint_sums.step < last or feed_sums.step < last:
+        if joint_sums.step < last:
+            token = joint_sums.advance(token, small, micros=300)
         if feed_sums.step < last:
             token = feed_sums.advance(token)
     (layer_out,) = call(
         layer_out_kernel,
         [shape((local, d), LOW)],
-        [after(hidden, small), feed_own, feed_got],
+        [after(hidden, token), feed_own, feed_got],
         smem=0,
-        micros=1.0,
+        micros=40,
     )
     ready = feed_sums.pairs()
     gate_grad, up_grad, down_grad = call(
         feed_total_kernel,
         [shape((d, units), F32)] * 2 + [shape((units, d), F32)],
-        [info, after(ready[0], token), *ready[1:]],
+        [info, after(ready[0], layer_out), *ready[1:]],
         scratch=[pltpu.VMEM((rows, units), LOW)],
         micros=2.0,
     )
-    joint_sums.advance(down_grad)
+    ready = joint_sums.pairs()
     query_grad, key_grad, value_grad, out_total, small_total = call(
         attention_total_kernel,
         [shape((width, d), F32)] * 4 + [shape((EXTRA // 2, d), F32)],
-        [info, *joint_sums.pairs()],
+        [info, after(ready[0], down_grad), *ready[1:]],
         micros=2.0,
     )
     if not joint_sums.tiled:

time: 176 us -> 168 us (0.955)
  starting transfers between devices: 57 us -> 45.3 us
  waiting for transfers between devices: 64.1 us -> 70.6 us
  Pallas kernels: 48.1 us -> 45.9 us
    ppermute x48 -> x44, starting transfers between devices: 55.5 us -> 43.7 us  [swap(): lax.ppermute(values, axis, [(i, i ^ bit) for i in range(lax.axis_size(axi...]
    ppermute x48 -> x44, waiting for transfers between devices: 64.1 us -> 70.6 us  [swap(): lax.ppermute(values, axis, [(i, i ^ bit) for i in range(lax.axis_size(axi...]
    pallas_call x31 -> x29, Pallas kernels: 48.1 us -> 45.9 us  [call(): pl.pallas_call(kernel, out_shape=outs, in_specs=[SMEM] * smem + [VMEM] *...]
  transfers between devices with their start and end apart: 50 -> 46, of which waited for: 20 -> 21; matrix products, arithmetic and copies ran while one was open for 1% -> 1% of each run, Pallas kernels for 21% -> 21%
where the time goes in v1:
time: 168 us
  waiting for transfers between devices  70.6 us (42%)
  Pallas kernels  45.9 us (27%)
  starting transfers between devices  45.3 us (27%)
  local copies, waits for them, and re-layouts  4.24 us (3%)
    ppermute x44, waiting for transfers between devices, swap(): lax.ppermute(values, axis, [(i, i ^ bit) for i in range(lax.axis_size(axi...  70.6 us
    pallas_call x29, Pallas kernels, call(): pl.pallas_call(kernel, out_shape=outs, in_specs=[SMEM] * smem + [VMEM] *...  45.9 us
    ppermute x44, starting transfers between devices, swap(): lax.ppermute(values, axis, [(i, i ^ bit) for i in range(lax.axis_size(axi...  43.7 us
  transfers between devices with their start and end apart: 46, of which 21 were waited for; matrix products, arithmetic and copies ran while one was open for 1% of the time, Pallas kernels for 21%

profile of v1, /device:TPU:0, one launch (start us, length us, event | category | flops | bytes accessed | tf_op | source)
XLA Modules:
  0.0 167.9 jit_solution(7276199239675127762)
XLA Ops:
  0.6 3.0 %collective-permute-start = (bf16[192,768]{1,0:T(8,128)(2,1)}, bf16[192,768]{1,0:T(8,128)(2,1)S(1)}, u32[]{:S(2)}, u32[]{:S(2)}) collective-permute-start(bf16[192,768]{1,0:T(8,128)(2,1)} %out_w.1), channel_id=1, source_target_pairs={{0,2},{1,3},{2,0},{3,1},{4,6},{5,7},{6,4},{7,5},{8,10},{9,11},{10,... | collective-permute-start | bytes 884744 | tf_op jit(solution)/shard_map/ppermute | solution.py:868
  4.4 4.8 %collective-permute-start.1 = (bf16[128,768]{1,0:T(8,128)(2,1)}, bf16[128,768]{1,0:T(8,128)(2,1)S(1)}, u32[]{:S(2)}, u32[]{:S(2)}) collective-permute-start(bf16[128,768]{1,0:T(8,128)(2,1)} %x_ref.1), channel_id=1, source_target_pairs={{0,4},{4,0},{8,12},{12,8},{16,20},{20,16},{24,28},{28,24},{1,5},{5... | collective-permute-start | bytes 589832 | tf_op jit(solution)/shard_map/ppermute | solution.py:868
  11.4 3.2 %shard_map.229 = (s32[8]{0:T(128)S(1)}, f32[1,512]{1,0:T(1,128)S(1)}, f32[512,128]{1,0:T(8,128)S(1)}, f32[3,128,2048]{2,1,0:T(8,128)S(1)}) custom-call(s32[2]{0:T(128)S(1)} %pad_add_fusion.spot, s32[32,128]{1,0:T(8,128)S(1)} %bitcast.22, s32[16,128]{1,0:T(8,128)S(1)} %add_bitcast_fusion.bucket_ref, f32[3,32]{1,0:T(4,128)S(1)} %bitcast.23), custom_call_target="tpu_custom_call" | custom-call | flops 60000000 | tf_op jit(solution)/shard_map/pallas_call | solution.py:37
  21.5 4.9 %shard_map.231 = (bf16[512,768]{1,0:T(8,128)(2,1)S(1)}, bf16[512,768]{1,0:T(8,128)(2,1)S(1)}, bf16[512,192]{1,0:T(8,128)(2,1)S(1)}, bf16[512,192]{1,0:T(8,128)(2...) custom-call(s32[8]{0:T(128)S(1)} %get-tuple-element.135.info, ...), custom_call_target="tpu_custom_call" | custom-call | flops 100000000 | tf_op jit(solution)/shard_map/pallas_call | solution.py:37
  27.0 2.5 %collective-permute-done.7.x1 = bf16[128,768]{1,0:T(8,128)(2,1)S(1)} collective-permute-done((bf16[128,768]{1,0:T(8,128)(2,1)S(1)}, bf16[128,768]{1,0:T(8,128)(2,1)S(1)}, u32[]{:S(2)}, u32[]{:S(2)}) %collective-permute-start.7) | collective-permute-done | bytes 196640 | tf_op jit(solution)/shard_map/ppermute | solution.py:868
  31.0 4.1 %shard_map.232 = (bf16[512,192]{1,0:T(8,128)(2,1)S(1)}, f32[512,192]{1,0:T(8,128)S(1)}, f32[512,128]{1,0:T(8,128)S(1)}, bf16[512,192]{1,0:T(8,128)(2,1)S(1)}, bf...) custom-call(s32[8]{0:T(128)S(1)} %get-tuple-element.135.info, bf16[128,768]{1,0:T(8,128)(2,1)S(1)} %shard_map.230.x0, ...), custom_call_target="tpu_custom_call" | custom-call | flops 100000000 | tf_op jit(solution)/shard_map/pallas_call | solution.py:37
  39.7 4.4 %collective-permute-done.12.m1 = bf16[512,192]{1,0:T(8,128)(2,1)S(1)} collective-permute-done((bf16[512,192]{1,0:T(8,128)(2,1)S(1)}, bf16[512,192]{1,0:T(8,128)(2,1)S(1)}, u32[]{:S(2)}, u32[]{:S(2)}) %collective-permute-start.12) | collective-permute-done | bytes 196640 | tf_op jit(solution)/shard_map/ppermute | solution.py:868
  45.6 4.4 %shard_map.235 = (bf16[512,768]{1,0:T(8,128)(2,1)S(1)}, f32[256,768]{1,0:T(8,128)S(1)}, bf16[512,512]{1,0:T(8,128)(2,1)S(1)}, bf16[512,512]{1,0:T(8,128)(2,1)S(1...) custom-call(s32[8]{0:T(128)S(1)} %get-tuple-element.135.info, ...), custom_call_target="tpu_custom_call" | custom-call | flops 100000000 | tf_op jit(solution)/shard_map/pallas_call | solution.py:37
  60.2 2.9 %collective-permute-done.18.other_ref = bf16[256,768]{1,0:T(8,128)(2,1)S(1)} collective-permute-done((bf16[256,768]{1,0:T(8,128)(2,1)S(1)}, bf16[256,768]{1,0:T(8,128)(2,1)S(1)}, u32[]{:S(2)}, u32[]{:S(2)}) %collective-permute-start.18) | collective-permute-done | bytes 393248 | tf_op jit(solution)/shard_map/ppermute | solution.py:868
  67.8 5.2 %collective-permute-start.21 = (bf16[512,256]{1,0:T(8,128)(2,1)S(1)}, bf16[512,256]{1,0:T(8,128)(2,1)S(1)}, u32[]{:S(2)}, u32[]{:S(2)}) collective-permute-start(bf16[512,256]{1,0:T(8,128)(2,1)S(1)} %get-tuple-element.184.payload_ref), channel_id=1, source_target_pairs={{0,4},{4,0},{8,12},{12,8},{16,20},{20,16},{24,28},{28,24},{1,5},{5... | collective-permute-start | bytes 786440 | tf_op jit(solution)/shard_map/ppermute | solution.py:868
  75.8 3.8 %shard_map.243 = (f32[512,192]{1,0:T(8,128)S(1)}, f32[512,192]{1,0:T(8,128)S(1)}, f32[512,192]{1,0:T(8,128)S(1)}, f32[3,128]{1,0:T(4,128)S(1)}) custom-call(bf16[512,192]{1,0:T(8,128)(2,1)S(1)} %get-tuple-element.190.q_ref, bf16[512,192]{1,0:T(8,128)(2,1)S(1)} %get-tuple-element.162.k_ref, bf16[512,192]{1,0:T(8,128)(2,1)S(1)} %get-tuple-element.163.v_ref, ...), custom_call_target="tpu_custom_call" | custom-call | flops 4000000000 | tf_op jit(solution)/shard_map/pallas_call | solution.py:37
  79.7 3.1 %shard_map.244 = (bf16[512,192]{1,0:T(8,128)(2,1)S(1)}, f32[3,128]{1,0:T(4,128)S(1)}) custom-call(s32[8]{0:T(128)S(1)} %get-tuple-element.135.info, bf16[512,192]{1,0:T(8,128)(2,1)S(1)} %get-tuple-element.190.q_ref, bf16[512,192]{1,0:T(8,128)(2,1)S(1)} %get-tuple-element.195.kp_ref, bf16[512,192]{1,0:T(8,128)(2,1)S(1)} %get-tuple-element.196.vp_ref, ...), custom_call_target="tpu_custom_call" | custom-call | flops 60000000 | tf_op jit(solution)/shard_map/pallas_call | solution.py:37
  83.6 4.6 %shard_map.245 = (bf16[192,768]{1,0:T(8,128)(2,1)S(1)}, bf16[192,768]{1,0:T(8,128)(2,1)S(1)}, bf16[192,768]{1,0:T(8,128)(2,1)S(1)}, bf16[192,768]{1,0:T(8,128)(2...) custom-call(s32[8]{0:T(128)S(1)} %get-tuple-element.135.info, ...), custom_call_target="tpu_custom_call" | custom-call | flops 6000000000 | tf_op jit(solution)/shard_map/pallas_call | solution.py:37
  88.3 2.5 %collective-permute-start.28 = (bf16[192,768]{1,0:T(8,128)(2,1)S(1)}, bf16[192,768]{1,0:T(8,128)(2,1)S(1)}, u32[]{:S(2)}, u32[]{:S(2)}) collective-permute-start(bf16[192,768]{1,0:T(8,128)(2,1)S(1)} %get-tuple-element.206), channel_id=1, source_target_pairs={{0,4},{4,0},{8,12},{12,8},{16,20},{20,16},{24,28},{28,24},{1,5},{5... | collective-permute-start | bytes 884744 | tf_op jit(solution)/shard_map/ppermute | solution.py:868
  97.2 7.0 %collective-permute-done.29.refs_3_ = bf16[192,768]{1,0:T(8,128)(2,1)S(1)} collective-permute-done((bf16[192,768]{1,0:T(8,128)(2,1)S(1)}, bf16[192,768]{1,0:T(8,128)(2,1)S(1)}, u32[]{:S(2)}, u32[]{:S(2)}) %collective-permute-start.29) | collective-permute-done | bytes 294944 | tf_op jit(solution)/shard_map/ppermute | solution.py:868
  106.3 3.8 %collective-permute-done.32.refs_3_ = bf16[96,768]{1,0:T(8,128)(2,1)S(1)} collective-permute-done((bf16[96,768]{1,0:T(8,128)(2,1)S(1)}, bf16[96,768]{1,0:T(8,128)(2,1)S(1)}, u32[]{:S(2)}, u32[]{:S(2)}) %collective-permute-start.32) | collective-permute-done | bytes 147488 | tf_op jit(solution)/shard_map/ppermute | solution.py:868
  110.1 4.2 %collective-permute-done.31.refs_1_ = bf16[96,768]{1,0:T(8,128)(2,1)S(1)} collective-permute-done((bf16[96,768]{1,0:T(8,128)(2,1)S(1)}, bf16[96,768]{1,0:T(8,128)(2,1)S(1)}, u32[]{:S(2)}, u32[]{:S(2)}) %collective-permute-start.31) | collective-permute-done | bytes 147488 | tf_op jit(solution)/shard_map/ppermute | solution.py:868
  114.4 3.6 %collective-permute-start.35 = (bf16[112,768]{1,0:T(8,128)(2,1)S(1)}, bf16[112,768]{1,0:T(8,128)(2,1)S(1)}, u32[]{:S(2)}, u32[]{:S(2)}) collective-permute-start(bf16[112,768]{1,0:T(8,128)(2,1)S(1)} %get-tuple-element.233.refs_0_), channel_id=1, source_target_pairs={{0,16},{4,20},{8,24},{12,28},{16,0},{20,4},{24,8},{28,12},{1,17},{... | collective-permute-start | bytes 516104 | tf_op jit(solution)/shard_map/ppermute | solution.py:868
  118.0 11.1 %collective-permute-done.33.refs_1_ = bf16[288,512]{1,0:T(8,128)(2,1)S(1)} collective-permute-done((bf16[288,512]{1,0:T(8,128)(2,1)S(1)}, bf16[288,512]{1,0:T(8,128)(2,1)S(1)}, u32[]{:S(2)}, u32[]{:S(2)}) %collective-permute-start.33) | collective-permute-done | bytes 294944 | tf_op jit(solution)/shard_map/ppermute | solution.py:868
  129.9 5.8 %collective-permute-done.36.refs_3_ = bf16[96,768]{1,0:T(8,128)(2,1)S(1)} collective-permute-done((bf16[96,768]{1,0:T(8,128)(2,1)S(1)}, bf16[96,768]{1,0:T(8,128)(2,1)S(1)}, u32[]{:S(2)}, u32[]{:S(2)}) %collective-permute-start.36) | collective-permute-done | bytes 147488 | tf_op jit(solution)/shard_map/ppermute | solution.py:868
  137.6 4.4 %collective-permute-done.37.refs_1_ = bf16[288,512]{1,0:T(8,128)(2,1)S(1)} collective-permute-done((bf16[288,512]{1,0:T(8,128)(2,1)S(1)}, bf16[288,512]{1,0:T(8,128)(2,1)S(1)}, u32[]{:S(2)}, u32[]{:S(2)}) %collective-permute-start.37) | collective-permute-done | bytes 294944 | tf_op jit(solution)/shard_map/ppermute | solution.py:868
  149.0 4.4 %collective-permute-done.41.got_ref = bf16[128,768]{1,0:T(8,128)(2,1)S(1)} collective-permute-done((bf16[128,768]{1,0:T(8,128)(2,1)S(1)}, bf16[128,768]{1,0:T(8,128)(2,1)S(1)}, u32[]{:S(2)}, u32[]{:S(2)}) %collective-permute-start.41) | collective-permute-done | bytes 196640 | tf_op jit(solution)/shard_map/ppermute | solution.py:868
  154.1 5.4 %collective-permute-done.43.two_got = bf16[576,512]{1,0:T(8,128)(2,1)S(1)} collective-permute-done((bf16[576,512]{1,0:T(8,128)(2,1)S(1)}, bf16[576,512]{1,0:T(8,128)(2,1)S(1)}, u32[]{:S(2)}, u32[]{:S(2)}) %collective-permute-start.43) | collective-permute-done | bytes 589856 | tf_op jit(solution)/shard_map/ppermute | solution.py:868
  159.5 3.1 %shard_map.256 = (f32[768,512]{1,0:T(8,128)}, f32[768,512]{1,0:T(8,128)}, f32[512,768]{1,0:T(8,128)}) custom-call(s32[8]{0:T(128)S(1)} %get-tuple-element.135.info, bf16[576,512]{1,0:T(8,128)(2,1)S(1)} %get-tuple-element.246.one, bf16[576,512]{1,0:T(8,128)(2,1)S(1)} %collective-permute-done.42.one_got, bf16[576,512]{1,0:T(8,128)(2,1)S(1)} %get-tuple-element.247.two, ...), custom_call_target="tpu_custom_call" | custom-call | flops 40000000 | tf_op jit(solution)/shard_map/pallas_call | solution.py:37
  (127 shorter events, 60.6 us)
Async XLA Ops:
  0.6 16.5 %collective-permute-start = (bf16[192,768]{1,0:T(8,128)(2,1)}, bf16[192,768]{1,0:T(8,128)(2,1)S(1)}, u32[]{:S(2)}, u32[]{:S(2)}) collective-permute-start(bf16[192,768]{1,0:T(8,128)(2,1)} %out_w.1), channel_id=1, source_target_pairs={{0,2},{1,3},{2,0},{3,1},{4,6},{5,7},{6,4},{7,5},{8,10},{9,11},{10,... | collective-permute-start | bytes 884744 | tf_op jit(solution)/shard_map/ppermute | solution.py:868
  3.7 14.1 %collective-permute-start.4 = (bf16[128,768]{1,0:T(8,128)(2,1)}, bf16[128,768]{1,0:T(8,128)(2,1)S(1)}, u32[]{:S(2)}, u32[]{:S(2)}) collective-permute-start(bf16[128,768]{1,0:T(8,128)(2,1)} %x_ref.1), channel_id=1, source_target_pairs={{0,2},{1,3},{2,0},{3,1},{4,6},{5,7},{6,4},{7,5},{8,10},{9,11},{10,... | collective-permute-start | bytes 589832 | tf_op jit(solution)/shard_map/ppermute | solution.py:868
  3.8 10.8 %collective-permute-start.2 = (bf16[128,768]{1,0:T(8,128)(2,1)}, bf16[128,768]{1,0:T(8,128)(2,1)S(1)}, u32[]{:S(2)}, u32[]{:S(2)}) collective-permute-start(bf16[128,768]{1,0:T(8,128)(2,1)} %x_ref.1), channel_id=1, source_target_pairs={{4,8},{12,16},{20,24},{8,4},{16,12},{24,20},{5,9},{13,17},{21,25},... | collective-permute-start | bytes 589832 | tf_op jit(solution)/shard_map/ppermute | solution.py:873
  4.4 12.2 %collective-permute-start.1 = (bf16[128,768]{1,0:T(8,128)(2,1)}, bf16[128,768]{1,0:T(8,128)(2,1)S(1)}, u32[]{:S(2)}, u32[]{:S(2)}) collective-permute-start(bf16[128,768]{1,0:T(8,128)(2,1)} %x_ref.1), channel_id=1, source_target_pairs={{0,4},{4,0},{8,12},{12,8},{16,20},{20,16},{24,28},{28,24},{1,5},{5... | collective-permute-start | bytes 589832 | tf_op jit(solution)/shard_map/ppermute | solution.py:868
  19.3 10.2 %collective-permute-start.7 = (bf16[128,768]{1,0:T(8,128)(2,1)S(1)}, bf16[128,768]{1,0:T(8,128)(2,1)S(1)}, u32[]{:S(2)}, u32[]{:S(2)}) collective-permute-start(bf16[128,768]{1,0:T(8,128)(2,1)S(1)} %shard_map.230.x0), channel_id=1, source_target_pairs={{0,2},{1,3},{2,0},{3,1},{4,6},{5,7},{6,4},{7,5},{8,10},{9,11},{10,... | collective-permute-start | bytes 589832 | tf_op jit(solution)/shard_map/ppermute | solution.py:868
  51.9 11.2 %collective-permute-start.18 = (bf16[256,768]{1,0:T(8,128)(2,1)S(1)}, bf16[256,768]{1,0:T(8,128)(2,1)S(1)}, u32[]{:S(2)}, u32[]{:S(2)}) collective-permute-start(bf16[256,768]{1,0:T(8,128)(2,1)S(1)} %shard_map.236.sum_ref), channel_id=1, source_target_pairs={{0,2},{1,3},{2,0},{3,1},{4,6},{5,7},{6,4},{7,5},{8,10},{9,11},{10,... | collective-permute-start | bytes 1179656 | tf_op jit(solution)/shard_map/ppermute | solution.py:868
  55.6 17.4 %collective-permute-start.23 = (bf16[576,512]{1,0:T(8,128)(2,1)S(1)}, bf16[576,512]{1,0:T(8,128)(2,1)S(1)}, u32[]{:S(2)}, u32[]{:S(2)}) collective-permute-start(bf16[576,512]{1,0:T(8,128)(2,1)S(1)} %get-tuple-element.173), channel_id=1, source_target_pairs={{0,4},{4,0},{8,12},{12,8},{16,20},{20,16},{24,28},{28,24},{1,5},{5... | collective-permute-start | bytes 1769480 | tf_op jit(solution)/shard_map/ppermute | solution.py:868
  58.0 15.0 %collective-permute-start.24 = (bf16[576,512]{1,0:T(8,128)(2,1)S(1)}, bf16[576,512]{1,0:T(8,128)(2,1)S(1)}, u32[]{:S(2)}, u32[]{:S(2)}) collective-permute-start(bf16[576,512]{1,0:T(8,128)(2,1)S(1)} %get-tuple-element.188), channel_id=1, source_target_pairs={{0,8},{4,12},{8,0},{12,4},{16,24},{20,28},{24,16},{28,20},{1,9},{5... | collective-permute-start | bytes 1769480 | tf_op jit(solution)/shard_map/ppermute | solution.py:868
  66.9 15.9 %collective-permute-start.22 = (bf16[512,256]{1,0:T(8,128)(2,1)S(1)}, bf16[512,256]{1,0:T(8,128)(2,1)S(1)}, u32[]{:S(2)}, u32[]{:S(2)}) collective-permute-start(bf16[512,256]{1,0:T(8,128)(2,1)S(1)} %get-tuple-element.184.payload_ref), channel_id=1, source_target_pairs={{4,8},{12,16},{20,24},{8,4},{16,12},{24,20},{5,9},{13,17},{21,25},... | collective-permute-start | bytes 786440 | tf_op jit(solution)/shard_map/ppermute | solution.py:873
  67.8 15.8 %collective-permute-start.21 = (bf16[512,256]{1,0:T(8,128)(2,1)S(1)}, bf16[512,256]{1,0:T(8,128)(2,1)S(1)}, u32[]{:S(2)}, u32[]{:S(2)}) collective-permute-start(bf16[512,256]{1,0:T(8,128)(2,1)S(1)} %get-tuple-element.184.payload_ref), channel_id=1, source_target_pairs={{0,4},{4,0},{8,12},{12,8},{16,20},{20,16},{24,28},{28,24},{1,5},{5... | collective-permute-start | bytes 786440 | tf_op jit(solution)/shard_map/ppermute | solution.py:868
  73.8 18.6 %collective-permute-start.25 = (bf16[288,512]{1,0:T(8,128)(2,1)S(1)}, bf16[288,512]{1,0:T(8,128)(2,1)S(1)}, u32[]{:S(2)}, u32[]{:S(2)}) collective-permute-start(bf16[288,512]{1,0:T(8,128)(2,1)S(1)} %get-tuple-element.189), channel_id=1, source_target_pairs={{0,8},{4,12},{8,0},{12,4},{16,24},{20,28},{24,16},{28,20},{1,9},{5... | collective-permute-start | bytes 884744 | tf_op jit(solution)/shard_map/ppermute | solution.py:868
  75.5 16.9 %collective-permute-start.26 = (bf16[288,512]{1,0:T(8,128)(2,1)S(1)}, bf16[288,512]{1,0:T(8,128)(2,1)S(1)}, u32[]{:S(2)}, u32[]{:S(2)}) collective-permute-start(bf16[288,512]{1,0:T(8,128)(2,1)S(1)} %get-tuple-element.209), channel_id=1, source_target_pairs={{0,4},{4,0},{8,12},{12,8},{16,20},{20,16},{24,28},{28,24},{1,5},{5... | collective-permute-start | bytes 884744 | tf_op jit(solution)/shard_map/ppermute | solution.py:868
  88.3 15.9 %collective-permute-start.28 = (bf16[192,768]{1,0:T(8,128)(2,1)S(1)}, bf16[192,768]{1,0:T(8,128)(2,1)S(1)}, u32[]{:S(2)}, u32[]{:S(2)}) collective-permute-start(bf16[192,768]{1,0:T(8,128)(2,1)S(1)} %get-tuple-element.206), channel_id=1, source_target_pairs={{0,4},{4,0},{8,12},{12,8},{16,20},{20,16},{24,28},{28,24},{1,5},{5... | collective-permute-start | bytes 884744 | tf_op jit(solution)/shard_map/ppermute | solution.py:868
  90.8 13.4 %collective-permute-start.29 = (bf16[192,768]{1,0:T(8,128)(2,1)S(1)}, bf16[192,768]{1,0:T(8,128)(2,1)S(1)}, u32[]{:S(2)}, u32[]{:S(2)}) collective-permute-start(bf16[192,768]{1,0:T(8,128)(2,1)S(1)} %get-tuple-element.217), channel_id=1, source_target_pairs={{0,8},{4,12},{8,0},{12,4},{16,24},{20,28},{24,16},{28,20},{1,9},{5... | collective-permute-start | bytes 884744 | tf_op jit(solution)/shard_map/ppermute | solution.py:868
  92.5 25.5 %collective-permute-start.34 = (bf16[288,512]{1,0:T(8,128)(2,1)S(1)}, bf16[288,512]{1,0:T(8,128)(2,1)S(1)}, u32[]{:S(2)}, u32[]{:S(2)}) collective-permute-start(bf16[288,512]{1,0:T(8,128)(2,1)S(1)} %get-tuple-element.231.refs_2_), channel_id=1, source_target_pairs={{0,16},{4,20},{8,24},{12,28},{16,0},{20,4},{24,8},{28,12},{1,17},{... | collective-permute-start | bytes 884744 | tf_op jit(solution)/shard_map/ppermute | solution.py:868
  93.8 35.4 %collective-permute-start.33 = (bf16[288,512]{1,0:T(8,128)(2,1)S(1)}, bf16[288,512]{1,0:T(8,128)(2,1)S(1)}, u32[]{:S(2)}, u32[]{:S(2)}) collective-permute-start(bf16[288,512]{1,0:T(8,128)(2,1)S(1)} %get-tuple-element.230.refs_0_), channel_id=1, source_target_pairs={{0,16},{4,20},{8,24},{12,28},{16,0},{20,4},{24,8},{28,12},{1,17},{... | collective-permute-start | bytes 884744 | tf_op jit(solution)/shard_map/ppermute | solution.py:868
  114.4 21.4 %collective-permute-start.35 = (bf16[112,768]{1,0:T(8,128)(2,1)S(1)}, bf16[112,768]{1,0:T(8,128)(2,1)S(1)}, u32[]{:S(2)}, u32[]{:S(2)}) collective-permute-start(bf16[112,768]{1,0:T(8,128)(2,1)S(1)} %get-tuple-element.233.refs_0_), channel_id=1, source_target_pairs={{0,16},{4,20},{8,24},{12,28},{16,0},{20,4},{24,8},{28,12},{1,17},{... | collective-permute-start | bytes 516104 | tf_op jit(solution)/shard_map/ppermute | solution.py:868
  117.9 17.8 %collective-permute-start.36 = (bf16[96,768]{1,0:T(8,128)(2,1)S(1)}, bf16[96,768]{1,0:T(8,128)(2,1)S(1)}, u32[]{:S(2)}, u32[]{:S(2)}) collective-permute-start(bf16[96,768]{1,0:T(8,128)(2,1)S(1)} %get-tuple-element.234.refs_2_), channel_id=1, source_target_pairs={{0,16},{4,20},{8,24},{12,28},{16,0},{20,4},{24,8},{28,12},{1,17},{... | collective-permute-start | bytes 442376 | tf_op jit(solution)/shard_map/ppermute | solution.py:868
  129.9 12.1 %collective-permute-start.37 = (bf16[288,512]{1,0:T(8,128)(2,1)S(1)}, bf16[288,512]{1,0:T(8,128)(2,1)S(1)}, u32[]{:S(2)}, u32[]{:S(2)}) collective-permute-start(bf16[288,512]{1,0:T(8,128)(2,1)S(1)} %get-tuple-element.236.refs_0_), channel_id=1, source_target_pairs={{0,8},{4,12},{8,0},{12,4},{16,24},{20,28},{24,16},{28,20},{1,9},{5... | collective-permute-start | bytes 884744 | tf_op jit(solution)/shard_map/ppermute | solution.py:868
  135.8 9.9 %collective-permute-start.39 = (bf16[112,768]{1,0:T(8,128)(2,1)S(1)}, bf16[112,768]{1,0:T(8,128)(2,1)S(1)}, u32[]{:S(2)}, u32[]{:S(2)}) collective-permute-start(bf16[112,768]{1,0:T(8,128)(2,1)S(1)} %get-tuple-element.239.refs_0_), channel_id=1, source_target_pairs={{0,8},{4,12},{8,0},{12,4},{16,24},{20,28},{24,16},{28,20},{1,9},{5... | collective-permute-start | bytes 516104 | tf_op jit(solution)/shard_map/ppermute | solution.py:868
  142.6 16.9 %collective-permute-start.42 = (bf16[576,512]{1,0:T(8,128)(2,1)S(1)}, bf16[576,512]{1,0:T(8,128)(2,1)S(1)}, u32[]{:S(2)}, u32[]{:S(2)}) collective-permute-start(bf16[576,512]{1,0:T(8,128)(2,1)S(1)} %get-tuple-element.246.one), channel_id=1, source_target_pairs={{0,4},{4,0},{8,12},{12,8},{16,20},{20,16},{24,28},{28,24},{1,5},{5... | collective-permute-start | bytes 1769480 | tf_op jit(solution)/shard_map/ppermute | solution.py:868
  143.2 16.3 %collective-permute-start.43 = (bf16[576,512]{1,0:T(8,128)(2,1)S(1)}, bf16[576,512]{1,0:T(8,128)(2,1)S(1)}, u32[]{:S(2)}, u32[]{:S(2)}) collective-permute-start(bf16[576,512]{1,0:T(8,128)(2,1)S(1)} %get-tuple-element.247.two), channel_id=1, source_target_pairs={{0,8},{4,12},{8,0},{12,4},{16,24},{20,28},{24,16},{28,20},{1,9},{5... | collective-permute-start | bytes 1769480 | tf_op jit(solution)/shard_map/ppermute | solution.py:868
  146.3 18.4 %collective-permute-start.44 = (bf16[208,768]{1,0:T(8,128)(2,1)S(1)}, bf16[208,768]{1,0:T(8,128)(2,1)S(1)}, u32[]{:S(2)}, u32[]{:S(2)}) collective-permute-start(bf16[208,768]{1,0:T(8,128)(2,1)S(1)} %get-tuple-element.249.one), channel_id=1, source_target_pairs={{0,4},{4,0},{8,12},{12,8},{16,20},{20,16},{24,28},{28,24},{1,5},{5... | collective-permute-start | bytes 958472 | tf_op jit(solution)/shard_map/ppermute | solution.py:868
  146.8 17.8 %collective-permute-start.45 = (bf16[192,768]{1,0:T(8,128)(2,1)S(1)}, bf16[192,768]{1,0:T(8,128)(2,1)S(1)}, u32[]{:S(2)}, u32[]{:S(2)}) collective-permute-start(bf16[192,768]{1,0:T(8,128)(2,1)S(1)} %get-tuple-element.250.two), channel_id=1, source_target_pairs={{0,8},{4,12},{8,0},{12,4},{16,24},{20,28},{24,16},{28,20},{1,9},{5... | collective-permute-start | bytes 884744 | tf_op jit(solution)/shard_map/ppermute | solution.py:868
  (35 other events, 183.2 us)

commit v2 on v1

--- a/solution.py
+++ b/solution.py
@@ -91,7 +91,32 @@
             count *= 2
 
 
-def setup_kernel(spot, segment_ref, bucket_ref, table_ref, info, row_ref, col_ref, bias_ref, *, groups, first_bits):
+def setup_kernel(
+    spot,
+    bucket_ref,
+    segment_hbm,
+    table_hbm,
+    one_hbm,
+    two_hbm,
+    info,
+    row_ref,
+    col_ref,
+    bias_ref,
+    table_ref,
+    one_ref,
+    two_ref,
+    segment_ref,
+    sems,
+    *,
+    groups,
+    first_bits,
+):
+    pairs = ((segment_hbm, segment_ref), (table_hbm, table_ref), (one_hbm, one_ref), (two_hbm, two_ref))
+    copies = [pltpu.make_async_copy(a, b, sems.at[k]) for k, (a, b) in enumerate(pairs)]
+    for copy in copies:
+        copy.start()
+    for copy in copies:
+        copy.wait()
     rank, member = spot[0], spot[1]
     steps = row_ref.shape[1] // CHUNK
     rows = [segment_ref[pl.ds(rank * steps + k, 1), :] for k in range(steps)]
@@ -198,7 +223,6 @@
 
 def own_kernel(
     info,
-    x0,
     x1,
     x2,
     x3,
@@ -206,6 +230,7 @@
     bias,
     seg_col,
     seg_row,
+    x_hbm,
     wq_hbm,
     wk_hbm,
     wv_hbm,
@@ -222,19 +247,23 @@
     wv,
     scores_ref,
     probs_ref,
+    x0,
     sems,
 ):
-    pairs = ((wq_hbm, wq), (wk_hbm, wk), (wv_hbm, wv))
+    pairs = ((x_hbm, x0), (wq_hbm, wq), (wk_hbm, wk), (wv_hbm, wv))
     copies = [pltpu.make_async_copy(a, b, sems.at[k]) for k, (a, b) in enumerate(pairs)]
     for copy in copies:
         copy.start()
-    for piece, spot in zip((x0, x1, x2, x3), place(info[0], info[1])):
+    spots = place(info[0], info[1])
+    for piece, spot in zip((x1, x2, x3, x0), spots[1:] + spots[:1]):
+        if piece is x0:
+            copies[0].wait()
         rows = aligned(spot * CHUNK)
         low = piece[...]
         x_all[rows, :] = low
         wide = low.astype(F32)
         normed_ref[rows, :] = (wide * rows_norm(wide) * as_row(gain)).astype(LOW)
-    for copy in copies:
+    for copy in copies[1:]:
         copy.wait()
     project(normed_ref[...], slice(None), wq, wk, wv, q_ref, k_ref, v_ref)
     attend(
@@ -849,7 +878,9 @@
             put_small(target, 2 * rows, get_small(mine, rows) + get_small(got, rows))
 
 
-def attention_total_kernel(info, one, one_got, two, two_got, q_ref, k_ref, v_ref, out_ref, small_ref):
+def attention_total_kernel(
+    info, one, one_got, two, two_got, q_ref, k_ref, v_ref, out_ref, gain_one_ref, gain_two_ref, table_ref
+):
     rows = q_ref.shape[0]
     first = info[4] == 0
     mine, got = one[:rows, :], one_got[:rows, :]
@@ -859,9 +890,17 @@
     v_ref[...] = jnp.where(first, two[...], two_got[...]).astype(F32)
     out_ref[...] = jnp.where(first, two_got[...], two[...]).astype(F32)
     if one.shape[0] > rows:
-        small_ref[...] = get_small(one, rows) + get_small(one_got, rows)
+        small = get_small(one, rows) + get_small(one_got, rows)
+        for k in range(gain_one_ref.shape[0]):
+            columns = slice(k * CHUNK, (k + 1) * CHUNK)
+            gain_one_ref[k : k + 1, :] = small[0:1, columns]
+            gain_two_ref[k : k + 1, :] = small[1:2, columns]
+        heads, buckets = table_ref.shape
+        table_ref[...] = small[2 : 2 + heads, :buckets]
     else:
-        small_ref[...] = jnp.zeros_like(small_ref)
+        gain_one_ref[...] = jnp.zeros_like(gain_one_ref)
+        gain_two_ref[...] = jnp.zeros_like(gain_two_ref)
+        table_ref[...] = jnp.zeros_like(table_ref)
 
 
 def swap(values, axis, bit):
@@ -1018,20 +1057,22 @@
     table = bias_table.T
     gain_one, gain_two = attention_gain.reshape(-1, CHUNK), feedforward_gain.reshape(-1, CHUNK)
     band = shape((heads, CHUNK, SPAN), F32)
-    info, seg_row, seg_col, bias = call(
+    segments = segment.reshape(-1, CHUNK)
+    info, seg_row, seg_col, bias, table, gain_one, gain_two = call(
         functools.partial(setup_kernel, groups=groups, first_bits=(order_one[0], order_two[0])),
-        [shape((8,), jnp.int32), shape((1, window), F32), shape((window, CHUNK), F32), band],
-        [spot, segment.reshape(-1, CHUNK), bucket_rows, table],
+        [shape((8,), jnp.int32), shape((1, window), F32), shape((window, CHUNK), F32), band]
+        + [shape(v.shape, F32) for v in (table, gain_one, gain_two)],
+        [spot, bucket_rows] + [in_hbm(v) for v in (segments, table, gain_one, gain_two)],
+        scratch=[pltpu.VMEM(segments.shape, jnp.int32), pltpu.SemaphoreType.DMA((4,))],
+        hbm=4,
         out_smem=1,
         micros=3.0,
     )
-    x_pieces = (inputs, x_across, swap(inputs, "mp", 1), swap(after(x_across, bias), "mp", 1))
-    out_across = swap(out_weight, "mp", 2)
     cot_across = swap(cotangent, "mp", 2)
-    (near,) = call(near_kernel, [shape((local, d), LOW)], [info, from_even, from_odd], micros=0.5)
-    out_core = swap(after(out_across, near), "mp", 1)
+    (near,) = call(near_kernel, [shape((local, d), LOW)], [info, after(from_even, x_across, cot_across), from_odd], micros=0.5)
     near_across = swap(near, "mp", 2)
     near_core = swap(near, "mp", 1)
+    x_pieces = (inputs, x_across, swap(inputs, "mp", 1), swap(after(x_across, near_core), "mp", 1))
 
     low_rows = shape((window, width), LOW)
     wide_rows = shape((window, width), F32)
@@ -1042,17 +1083,17 @@
     x_all, normed, queries, keys, values, acc, top, total, wq, wk, wv = call(
         own_kernel,
         [shape((window, d), LOW)] * 2 + [low_rows] * 3 + [wide_rows, stats, stats] + [weight] * 3,
-        [info, after(inputs, out_core), *x_pieces[1:], gain_one, bias, seg_col, seg_row, *[in_hbm(w.T) for w in (query_weight, key_weight, value_weight)]],
-        scratch=[square_wide, square_low, pltpu.SemaphoreType.DMA((3,))],
-        hbm=3,
+        [info, x_across, *x_pieces[2:], gain_one, bias, seg_col, seg_row]
+        + [in_hbm(v) for v in (inputs, query_weight.T, key_weight.T, value_weight.T)],
+        scratch=[square_wide, square_low, pltpu.VMEM((local, d), LOW), pltpu.SemaphoreType.DMA((4,))],
+        hbm=4,
         micros=5.0,
     )
     near_pieces = (near, near_across, near_core, swap(after(near_across, acc), "mp", 1))
-    cot_pieces = (cotangent, cot_across, swap(after(cotangent, near), "mp", 1), swap(after(cot_across, acc), "mp", 1))
     mixed_low, mixed, lse, queries_near, keys_near, values_near = call(
         partner_kernel,
         [low_rows, wide_rows, stats] + [low_rows] * 3,
-        [info, *near_pieces, gain_one, wq, wk, wv, bias, queries, after(acc, cot_pieces[3]), top, total],
+        [info, *near_pieces, gain_one, wq, wk, wv, bias, queries, acc, top, total],
         scratch=[
             pltpu.VMEM((window, d), LOW),
             square_wide,
@@ -1061,11 +1102,23 @@
             pltpu.VMEM((window, CHUNK), F32),
             pltpu.VMEM((window, CHUNK), F32),
         ],
-        micros=5.0,
+        micros=300,
     )
     mixed_across = swap(mixed_low, "mp", 2)
     mixed_core = swap(mixed_low, "mp", 1)
-    out_pieces = (out_weight, out_across, swap(after(out_weight, mixed_core), "mp", 1), out_core)
+    cot_pieces = (
+        cotangent,
+        cot_across,
+        swap(after(cotangent, mixed_core), "mp", 1),
+        swap(after(cot_across, mixed_core), "mp", 1),
+    )
+    out_across = swap(after(out_weight, near), "mp", 2)
+    out_pieces = (
+        out_weight,
+        out_across,
+        swap(after(out_weight, mixed_core), "mp", 1),
+        swap(after(out_across, mixed_core), "mp", 1),
+    )
     bias_t, flipped_rows = call(
         flipped_kernel,
         [band, shape(bucket_rows.shape, jnp.int32)],
@@ -1076,11 +1129,11 @@
     cot_all, d_act = call(
         cotangent_kernel,
         [shape((window, d), LOW), shape((window, units), F32)],
-        [*cot_pieces, after(down_weight, mixed_low)],
+        [*cot_pieces, after(down_weight, mixed_across)],
         smem=0,
         micros=1.0,
     )
-    mixed_pieces = (mixed_low, mixed_across, mixed_core, swap(after(mixed_across, bias_t, d_act), "mp", 1))
+    mixed_pieces = (mixed_low, mixed_across, mixed_core, swap(after(mixed_across, bias_t), "mp", 1))
     second, hidden, act, d_gate, d_up, second_send, second_keep, gain_two_part = call(
         feed_kernel,
         [shape((window, d), LOW), shape((half, d), F32)]
@@ -1176,8 +1229,8 @@
         scratch=[pltpu.VMEM((window, 3 * width), LOW), square_wide, square_wide, square_low, square_low],
         micros=300,
     )
-    joint_sums = Sums(info, rank, (order_one, order_two), (one_send, two_send), (one_keep, two_keep))
     token = feed_sums.advance(one_send, micros=300)
+    joint_sums = Sums(info, rank, (order_one, order_two), (after(one_send, token), two_send), (one_keep, two_keep))
     first_send, first_own, small = call(
         first_merge_kernel,
         [shape((local + EXTRA, d), LOW), shape((local, d), LOW), shape((EXTRA // 2, d), F32)],
@@ -1221,24 +1274,26 @@
         micros=2.0,
     )
     ready = joint_sums.pairs()
-    query_grad, key_grad, value_grad, out_total, small_total = call(
+    query_grad, key_grad, value_grad, out_total, gain_one_total, gain_two_total, table_total = call(
         attention_total_kernel,
-        [shape((width, d), F32)] * 4 + [shape((EXTRA // 2, d), F32)],
+        [shape((width, d), F32)] * 4 + [shape((d // CHUNK, CHUNK), F32)] * 2 + [shape((heads, buckets), F32)],
         [info, after(ready[0], down_grad), *ready[1:]],
         micros=2.0,
     )
     if not joint_sums.tiled:
-        small_total = lax.psum(small, "dp")
+        small = lax.psum(small, "dp")
+        gain_one_total, gain_two_total = small[0].reshape(-1, CHUNK), small[1].reshape(-1, CHUNK)
+        table_total = small[2 : 2 + heads, :buckets]
     return (
         layer_out,
         input_grad,
-        small_total[0],
+        gain_one_total.reshape(-1),
         query_grad.T,
         key_grad.T,
         value_grad.T,
         out_total,
-        small_total[2 : 2 + heads, :buckets].T,
-        small_total[1],
+        table_total.T,
+        gain_two_total.reshape(-1),
         gate_grad,
         up_grad,
         down_grad,

time: 168 us -> 163 us (0.970)
  local copies, waits for them, and re-layouts: 4.24 us -> 0.03 us
  waiting for transfers between devices: 70.6 us -> 66.4 us
  starting transfers between devices: 45.3 us -> 47.6 us
    ppermute x44, waiting for transfers between devices: 70.6 us -> 66.4 us  [swap(): lax.ppermute(values, axis, [(i, i ^ bit) for i in range(lax.axis_size(axi...]
    unnamed x26 -> x12, local copies, waits for them, and re-layouts: 3.05 us -> 0.03 us
    ppermute x44, starting transfers between devices: 43.7 us -> 46 us  [swap(): lax.ppermute(values, axis, [(i, i ^ bit) for i in range(lax.axis_size(axi...]
  transfers between devices with their start and end apart: 46 -> 46, of which waited for: 21 -> 22; matrix products, arithmetic and copies ran while one was open for 1% -> 1% of each run, Pallas kernels for 21% -> 24%
where the time goes in v2:
time: 163 us
  waiting for transfers between devices  66.4 us (41%)
  starting transfers between devices  47.6 us (29%)
  Pallas kernels  46.7 us (29%)
    ppermute x44, waiting for transfers between devices, swap(): lax.ppermute(values, axis, [(i, i ^ bit) for i in range(lax.axis_size(axi...  66.4 us
    pallas_call x29, Pallas kernels, call(): pl.pallas_call(kernel, out_shape=outs, in_specs=[SMEM] * smem + [VMEM] *...  46.7 us
    ppermute x44, starting transfers between devices, swap(): lax.ppermute(values, axis, [(i, i ^ bit) for i in range(lax.axis_size(axi...  46 us
  transfers between devices with their start and end apart: 46, of which 22 were waited for; matrix products, arithmetic and copies ran while one was open for 1% of the time, Pallas kernels for 24%

profile of v2, /device:TPU:0, one launch (start us, length us, event | category | flops | bytes accessed | tf_op | source)
XLA Modules:
  0.0 162.5 jit_solution(13960069744090506898)
XLA Ops:
  1.3 5.8 %collective-permute-start.2 = (bf16[128,768]{1,0:T(8,128)(2,1)}, bf16[128,768]{1,0:T(8,128)(2,1)S(1)}, u32[]{:S(2)}, u32[]{:S(2)}) collective-permute-start(bf16[128,768]{1,0:T(8,128)(2,1)} %x_ref.1), channel_id=1, source_target_pairs={{0,4},{4,0},{8,12},{12,8},{16,20},{20,16},{24,28},{28,24},{1,5},{5... | collective-permute-start | bytes 589832 | tf_op jit(solution)/shard_map/ppermute | solution.py:907
  10.0 3.9 %shard_map.229 = (s32[8]{0:T(128)S(1)}, f32[1,512]{1,0:T(1,128)S(1)}, f32[512,128]{1,0:T(8,128)S(1)}, f32[3,128,2048]{2,1,0:T(8,128)S(1)}, f32[3,32]{1,0:T(4,128...) custom-call(s32[2]{0:T(128)S(1)} %pad_add_fusion.spot, s32[16,128]{1,0:T(8,128)S(1)} %add_bitcast_fusion.bucket_ref, ...), custom_call_target="tpu_custom_call" | custom-call | flops 60000000 | tf_op jit(solution)/shard_map/pallas_call | solution.py:37
  13.8 3.8 %collective-permute-done.3.g1 = bf16[128,768]{1,0:T(8,128)(2,1)S(1)} collective-permute-done((bf16[128,768]{1,0:T(8,128)(2,1)}, bf16[128,768]{1,0:T(8,128)(2,1)S(1)}, u32[]{:S(2)}, u32[]{:S(2)}) %collective-permute-start.3) | collective-permute-done | bytes 196640 | tf_op jit(solution)/shard_map/ppermute | solution.py:907
  21.4 5.0 %shard_map.231 = (bf16[512,768]{1,0:T(8,128)(2,1)S(1)}, bf16[512,768]{1,0:T(8,128)(2,1)S(1)}, bf16[512,192]{1,0:T(8,128)(2,1)S(1)}, bf16[512,192]{1,0:T(8,128)(2...) custom-call(s32[8]{0:T(128)S(1)} %get-tuple-element.141.info, ...), custom_call_target="tpu_custom_call" | custom-call | flops 100000000 | tf_op jit(solution)/shard_map/pallas_call | solution.py:37
  28.6 4.1 %shard_map.232 = (bf16[512,192]{1,0:T(8,128)(2,1)S(1)}, f32[512,192]{1,0:T(8,128)S(1)}, f32[512,128]{1,0:T(8,128)S(1)}, bf16[512,192]{1,0:T(8,128)(2,1)S(1)}, bf...) custom-call(s32[8]{0:T(128)S(1)} %get-tuple-element.141.info, bf16[128,768]{1,0:T(8,128)(2,1)S(1)} %shard_map.230.x0, ...), custom_call_target="tpu_custom_call" | custom-call | flops 6000000000 | tf_op jit(solution)/shard_map/pallas_call | solution.py:37
  34.4 2.5 %collective-permute-done.12.o1 = bf16[192,768]{1,0:T(8,128)(2,1)S(1)} collective-permute-done((bf16[192,768]{1,0:T(8,128)(2,1)S(1)}, bf16[192,768]{1,0:T(8,128)(2,1)S(1)}, u32[]{:S(2)}, u32[]{:S(2)}) %collective-permute-start.12) | collective-permute-done | bytes 294944 | tf_op jit(solution)/shard_map/ppermute | solution.py:907
  43.6 4.4 %shard_map.235 = (bf16[512,768]{1,0:T(8,128)(2,1)S(1)}, f32[256,768]{1,0:T(8,128)S(1)}, bf16[512,512]{1,0:T(8,128)(2,1)S(1)}, bf16[512,512]{1,0:T(8,128)(2,1)S(1...) custom-call(s32[8]{0:T(128)S(1)} %get-tuple-element.141.info, ...), custom_call_target="tpu_custom_call" | custom-call | flops 100000000 | tf_op jit(solution)/shard_map/pallas_call | solution.py:37
  56.3 4.9 %collective-permute-done.18.other_ref = bf16[256,768]{1,0:T(8,128)(2,1)S(1)} collective-permute-done((bf16[256,768]{1,0:T(8,128)(2,1)S(1)}, bf16[256,768]{1,0:T(8,128)(2,1)S(1)}, u32[]{:S(2)}, u32[]{:S(2)}) %collective-permute-start.18) | collective-permute-done | bytes 393248 | tf_op jit(solution)/shard_map/ppermute | solution.py:907
  65.8 4.3 %collective-permute-start.21 = (bf16[512,256]{1,0:T(8,128)(2,1)S(1)}, bf16[512,256]{1,0:T(8,128)(2,1)S(1)}, u32[]{:S(2)}, u32[]{:S(2)}) collective-permute-start(bf16[512,256]{1,0:T(8,128)(2,1)S(1)} %get-tuple-element.193.payload_ref), channel_id=1, source_target_pairs={{0,4},{4,0},{8,12},{12,8},{16,20},{20,16},{24,28},{28,24},{1,5},{5... | collective-permute-start | bytes 786440 | tf_op jit(solution)/shard_map/ppermute | solution.py:907
  73.0 3.8 %shard_map.243 = (f32[512,192]{1,0:T(8,128)S(1)}, f32[512,192]{1,0:T(8,128)S(1)}, f32[512,192]{1,0:T(8,128)S(1)}, f32[3,128]{1,0:T(4,128)S(1)}) custom-call(bf16[512,192]{1,0:T(8,128)(2,1)S(1)} %get-tuple-element.199.q_ref, bf16[512,192]{1,0:T(8,128)(2,1)S(1)} %get-tuple-element.171.k_ref, bf16[512,192]{1,0:T(8,128)(2,1)S(1)} %get-tuple-element.172.v_ref, ...), custom_call_target="tpu_custom_call" | custom-call | flops 4000000000 | tf_op jit(solution)/shard_map/pallas_call | solution.py:37
  76.8 3.1 %shard_map.244 = (bf16[512,192]{1,0:T(8,128)(2,1)S(1)}, f32[3,128]{1,0:T(4,128)S(1)}) custom-call(s32[8]{0:T(128)S(1)} %get-tuple-element.141.info, bf16[512,192]{1,0:T(8,128)(2,1)S(1)} %get-tuple-element.199.q_ref, bf16[512,192]{1,0:T(8,128)(2,1)S(1)} %get-tuple-element.204.kp_ref, bf16[512,192]{1,0:T(8,128)(2,1)S(1)} %get-tuple-element.205.vp_ref, ...), custom_call_target="tpu_custom_call" | custom-call | flops 60000000 | tf_op jit(solution)/shard_map/pallas_call | solution.py:37
  79.9 4.7 %shard_map.245 = (bf16[192,768]{1,0:T(8,128)(2,1)S(1)}, bf16[192,768]{1,0:T(8,128)(2,1)S(1)}, bf16[192,768]{1,0:T(8,128)(2,1)S(1)}, bf16[192,768]{1,0:T(8,128)(2...) custom-call(s32[8]{0:T(128)S(1)} %get-tuple-element.141.info, ...), custom_call_target="tpu_custom_call" | custom-call | flops 6000000000 | tf_op jit(solution)/shard_map/pallas_call | solution.py:37
  86.2 2.5 %collective-permute-start.28 = (bf16[192,768]{1,0:T(8,128)(2,1)S(1)}, bf16[192,768]{1,0:T(8,128)(2,1)S(1)}, u32[]{:S(2)}, u32[]{:S(2)}) collective-permute-start(bf16[192,768]{1,0:T(8,128)(2,1)S(1)} %get-tuple-element.225), channel_id=1, source_target_pairs={{0,4},{4,0},{8,12},{12,8},{16,20},{20,16},{24,28},{28,24},{1,5},{5... | collective-permute-start | bytes 884744 | tf_op jit(solution)/shard_map/ppermute | solution.py:907
  88.7 2.5 %collective-permute-start.34 = (bf16[288,512]{1,0:T(8,128)(2,1)S(1)}, bf16[288,512]{1,0:T(8,128)(2,1)S(1)}, u32[]{:S(2)}, u32[]{:S(2)}) collective-permute-start(bf16[288,512]{1,0:T(8,128)(2,1)S(1)} %get-tuple-element.241.refs_2_), channel_id=1, source_target_pairs={{0,16},{4,20},{8,24},{12,28},{16,0},{20,4},{24,8},{28,12},{1,17},{... | collective-permute-start | bytes 884744 | tf_op jit(solution)/shard_map/ppermute | solution.py:907
  97.0 2.4 %collective-permute-start.32 = (bf16[96,768]{1,0:T(8,128)(2,1)S(1)}, bf16[96,768]{1,0:T(8,128)(2,1)S(1)}, u32[]{:S(2)}, u32[]{:S(2)}) collective-permute-start(bf16[96,768]{1,0:T(8,128)(2,1)S(1)} %get-tuple-element.238), channel_id=1, source_target_pairs={{0,4},{4,0},{8,12},{12,8},{16,20},{20,16},{24,28},{28,24},{1,5},{5... | collective-permute-start | bytes 442376 | tf_op jit(solution)/shard_map/ppermute | solution.py:907
  102.8 5.5 %collective-permute-done.31.refs_1_ = bf16[96,768]{1,0:T(8,128)(2,1)S(1)} collective-permute-done((bf16[96,768]{1,0:T(8,128)(2,1)S(1)}, bf16[96,768]{1,0:T(8,128)(2,1)S(1)}, u32[]{:S(2)}, u32[]{:S(2)}) %collective-permute-start.31) | collective-permute-done | bytes 147488 | tf_op jit(solution)/shard_map/ppermute | solution.py:907
  108.3 4.4 %collective-permute-start.35 = (bf16[112,768]{1,0:T(8,128)(2,1)S(1)}, bf16[112,768]{1,0:T(8,128)(2,1)S(1)}, u32[]{:S(2)}, u32[]{:S(2)}) collective-permute-start(bf16[112,768]{1,0:T(8,128)(2,1)S(1)} %get-tuple-element.243.refs_0_), channel_id=1, source_target_pairs={{0,16},{4,20},{8,24},{12,28},{16,0},{20,4},{24,8},{28,12},{1,17},{... | collective-permute-start | bytes 516104 | tf_op jit(solution)/shard_map/ppermute | solution.py:907
  112.8 12.5 %collective-permute-done.33.refs_1_ = bf16[288,512]{1,0:T(8,128)(2,1)S(1)} collective-permute-done((bf16[288,512]{1,0:T(8,128)(2,1)S(1)}, bf16[288,512]{1,0:T(8,128)(2,1)S(1)}, u32[]{:S(2)}, u32[]{:S(2)}) %collective-permute-start.33) | collective-permute-done | bytes 294944 | tf_op jit(solution)/shard_map/ppermute | solution.py:907
  126.8 4.7 %collective-permute-done.36.refs_3_ = bf16[96,768]{1,0:T(8,128)(2,1)S(1)} collective-permute-done((bf16[96,768]{1,0:T(8,128)(2,1)S(1)}, bf16[96,768]{1,0:T(8,128)(2,1)S(1)}, u32[]{:S(2)}, u32[]{:S(2)}) %collective-permute-start.36) | collective-permute-done | bytes 147488 | tf_op jit(solution)/shard_map/ppermute | solution.py:907
  133.1 4.7 %collective-permute-done.37.refs_1_ = bf16[288,512]{1,0:T(8,128)(2,1)S(1)} collective-permute-done((bf16[288,512]{1,0:T(8,128)(2,1)S(1)}, bf16[288,512]{1,0:T(8,128)(2,1)S(1)}, u32[]{:S(2)}, u32[]{:S(2)}) %collective-permute-start.37) | collective-permute-done | bytes 294944 | tf_op jit(solution)/shard_map/ppermute | solution.py:907
  138.9 2.6 %collective-permute-done.39.refs_1_ = bf16[112,768]{1,0:T(8,128)(2,1)S(1)} collective-permute-done((bf16[112,768]{1,0:T(8,128)(2,1)S(1)}, bf16[112,768]{1,0:T(8,128)(2,1)S(1)}, u32[]{:S(2)}, u32[]{:S(2)}) %collective-permute-start.39) | collective-permute-done | bytes 172064 | tf_op jit(solution)/shard_map/ppermute | solution.py:907
  144.7 4.3 %collective-permute-done.41.got_ref = bf16[128,768]{1,0:T(8,128)(2,1)S(1)} collective-permute-done((bf16[128,768]{1,0:T(8,128)(2,1)S(1)}, bf16[128,768]{1,0:T(8,128)(2,1)S(1)}, u32[]{:S(2)}, u32[]{:S(2)}) %collective-permute-start.41) | collective-permute-done | bytes 196640 | tf_op jit(solution)/shard_map/ppermute | solution.py:907
  149.8 5.3 %collective-permute-done.43.two_got = bf16[576,512]{1,0:T(8,128)(2,1)S(1)} collective-permute-done((bf16[576,512]{1,0:T(8,128)(2,1)S(1)}, bf16[576,512]{1,0:T(8,128)(2,1)S(1)}, u32[]{:S(2)}, u32[]{:S(2)}) %collective-permute-start.43) | collective-permute-done | bytes 589856 | tf_op jit(solution)/shard_map/ppermute | solution.py:907
  155.1 3.1 %shard_map.256 = (f32[768,512]{1,0:T(8,128)}, f32[768,512]{1,0:T(8,128)}, f32[512,768]{1,0:T(8,128)}) custom-call(s32[8]{0:T(128)S(1)} %get-tuple-element.141.info, bf16[576,512]{1,0:T(8,128)(2,1)S(1)} %get-tuple-element.256.one, bf16[576,512]{1,0:T(8,128)(2,1)S(1)} %collective-permute-done.42.one_got, bf16[576,512]{1,0:T(8,128)(2,1)S(1)} %get-tuple-element.257.two, ...), custom_call_target="tpu_custom_call" | custom-call | flops 40000000 | tf_op jit(solution)/shard_map/pallas_call | solution.py:37
  (111 shorter events, 56.9 us)
Async XLA Ops:
  0.6 17.0 %collective-permute-start.4 = (bf16[128,768]{1,0:T(8,128)(2,1)}, bf16[128,768]{1,0:T(8,128)(2,1)S(1)}, u32[]{:S(2)}, u32[]{:S(2)}) collective-permute-start(bf16[128,768]{1,0:T(8,128)(2,1)} %x_ref.1), channel_id=1, source_target_pairs={{4,8},{12,16},{20,24},{8,4},{16,12},{24,20},{5,9},{13,17},{21,25},... | collective-permute-start | bytes 589832 | tf_op jit(solution)/shard_map/ppermute | solution.py:912
  1.3 16.3 %collective-permute-start.2 = (bf16[128,768]{1,0:T(8,128)(2,1)}, bf16[128,768]{1,0:T(8,128)(2,1)S(1)}, u32[]{:S(2)}, u32[]{:S(2)}) collective-permute-start(bf16[128,768]{1,0:T(8,128)(2,1)} %x_ref.1), channel_id=1, source_target_pairs={{0,4},{4,0},{8,12},{12,8},{16,20},{20,16},{24,28},{28,24},{1,5},{5... | collective-permute-start | bytes 589832 | tf_op jit(solution)/shard_map/ppermute | solution.py:907
  7.1 10.5 %collective-permute-start = (bf16[128,768]{1,0:T(8,128)(2,1)}, bf16[128,768]{1,0:T(8,128)(2,1)S(1)}, u32[]{:S(2)}, u32[]{:S(2)}) collective-permute-start(bf16[128,768]{1,0:T(8,128)(2,1)} %x_ref.1), channel_id=1, source_target_pairs={{0,2},{1,3},{2,0},{3,1},{4,6},{5,7},{6,4},{7,5},{8,10},{9,11},{10,... | collective-permute-start | bytes 589832 | tf_op jit(solution)/shard_map/ppermute | solution.py:907
  27.0 9.8 %collective-permute-start.12 = (bf16[192,768]{1,0:T(8,128)(2,1)S(1)}, bf16[192,768]{1,0:T(8,128)(2,1)S(1)}, u32[]{:S(2)}, u32[]{:S(2)}) collective-permute-start(bf16[192,768]{1,0:T(8,128)(2,1)S(1)} %copy-done), channel_id=1, source_target_pairs={{0,2},{1,3},{2,0},{3,1},{4,6},{5,7},{6,4},{7,5},{8,10},{9,11},{10,... | collective-permute-start | bytes 884744 | tf_op jit(solution)/shard_map/ppermute | solution.py:907
  33.0 9.1 %collective-permute-start.9 = (bf16[512,192]{1,0:T(8,128)(2,1)S(1)}, bf16[512,192]{1,0:T(8,128)(2,1)S(1)}, u32[]{:S(2)}, u32[]{:S(2)}) collective-permute-start(bf16[512,192]{1,0:T(8,128)(2,1)S(1)} %get-tuple-element.157.m0.mixed_low), channel_id=1, source_target_pairs={{0,2},{1,3},{2,0},{3,1},{4,6},{5,7},{6,4},{7,5},{8,10},{9,11},{10,... | collective-permute-start | bytes 589832 | tf_op jit(solution)/shard_map/ppermute | solution.py:907
  49.9 11.2 %collective-permute-start.18 = (bf16[256,768]{1,0:T(8,128)(2,1)S(1)}, bf16[256,768]{1,0:T(8,128)(2,1)S(1)}, u32[]{:S(2)}, u32[]{:S(2)}) collective-permute-start(bf16[256,768]{1,0:T(8,128)(2,1)S(1)} %shard_map.236.sum_ref), channel_id=1, source_target_pairs={{0,2},{1,3},{2,0},{3,1},{4,6},{5,7},{6,4},{7,5},{8,10},{9,11},{10,... | collective-permute-start | bytes 1179656 | tf_op jit(solution)/shard_map/ppermute | solution.py:907
  53.6 16.5 %collective-permute-start.23 = (bf16[576,512]{1,0:T(8,128)(2,1)S(1)}, bf16[576,512]{1,0:T(8,128)(2,1)S(1)}, u32[]{:S(2)}, u32[]{:S(2)}) collective-permute-start(bf16[576,512]{1,0:T(8,128)(2,1)S(1)} %get-tuple-element.182), channel_id=1, source_target_pairs={{0,4},{4,0},{8,12},{12,8},{16,20},{20,16},{24,28},{28,24},{1,5},{5... | collective-permute-start | bytes 1769480 | tf_op jit(solution)/shard_map/ppermute | solution.py:907
  54.0 16.1 %collective-permute-start.24 = (bf16[576,512]{1,0:T(8,128)(2,1)S(1)}, bf16[576,512]{1,0:T(8,128)(2,1)S(1)}, u32[]{:S(2)}, u32[]{:S(2)}) collective-permute-start(bf16[576,512]{1,0:T(8,128)(2,1)S(1)} %get-tuple-element.197), channel_id=1, source_target_pairs={{0,8},{4,12},{8,0},{12,4},{16,24},{20,28},{24,16},{28,20},{1,9},{5... | collective-permute-start | bytes 1769480 | tf_op jit(solution)/shard_map/ppermute | solution.py:907
  64.9 15.0 %collective-permute-start.22 = (bf16[512,256]{1,0:T(8,128)(2,1)S(1)}, bf16[512,256]{1,0:T(8,128)(2,1)S(1)}, u32[]{:S(2)}, u32[]{:S(2)}) collective-permute-start(bf16[512,256]{1,0:T(8,128)(2,1)S(1)} %get-tuple-element.193.payload_ref), channel_id=1, source_target_pairs={{4,8},{12,16},{20,24},{8,4},{16,12},{24,20},{5,9},{13,17},{21,25},... | collective-permute-start | bytes 786440 | tf_op jit(solution)/shard_map/ppermute | solution.py:912
  65.8 14.1 %collective-permute-start.21 = (bf16[512,256]{1,0:T(8,128)(2,1)S(1)}, bf16[512,256]{1,0:T(8,128)(2,1)S(1)}, u32[]{:S(2)}, u32[]{:S(2)}) collective-permute-start(bf16[512,256]{1,0:T(8,128)(2,1)S(1)} %get-tuple-element.193.payload_ref), channel_id=1, source_target_pairs={{0,4},{4,0},{8,12},{12,8},{16,20},{20,16},{24,28},{28,24},{1,5},{5... | collective-permute-start | bytes 786440 | tf_op jit(solution)/shard_map/ppermute | solution.py:907
  71.0 15.1 %collective-permute-start.25 = (bf16[288,512]{1,0:T(8,128)(2,1)S(1)}, bf16[288,512]{1,0:T(8,128)(2,1)S(1)}, u32[]{:S(2)}, u32[]{:S(2)}) collective-permute-start(bf16[288,512]{1,0:T(8,128)(2,1)S(1)} %get-tuple-element.198), channel_id=1, source_target_pairs={{0,8},{4,12},{8,0},{12,4},{16,24},{20,28},{24,16},{28,20},{1,9},{5... | collective-permute-start | bytes 884744 | tf_op jit(solution)/shard_map/ppermute | solution.py:907
  72.6 13.4 %collective-permute-start.26 = (bf16[288,512]{1,0:T(8,128)(2,1)S(1)}, bf16[288,512]{1,0:T(8,128)(2,1)S(1)}, u32[]{:S(2)}, u32[]{:S(2)}) collective-permute-start(bf16[288,512]{1,0:T(8,128)(2,1)S(1)} %get-tuple-element.218), channel_id=1, source_target_pairs={{0,4},{4,0},{8,12},{12,8},{16,20},{20,16},{24,28},{28,24},{1,5},{5... | collective-permute-start | bytes 884744 | tf_op jit(solution)/shard_map/ppermute | solution.py:907
  84.5 10.9 %collective-permute-start.29 = (bf16[192,768]{1,0:T(8,128)(2,1)S(1)}, bf16[192,768]{1,0:T(8,128)(2,1)S(1)}, u32[]{:S(2)}, u32[]{:S(2)}) collective-permute-start(bf16[192,768]{1,0:T(8,128)(2,1)S(1)} %get-tuple-element.227), channel_id=1, source_target_pairs={{0,8},{4,12},{8,0},{12,4},{16,24},{20,28},{24,16},{28,20},{1,9},{5... | collective-permute-start | bytes 884744 | tf_op jit(solution)/shard_map/ppermute | solution.py:907
  86.2 10.1 %collective-permute-start.28 = (bf16[192,768]{1,0:T(8,128)(2,1)S(1)}, bf16[192,768]{1,0:T(8,128)(2,1)S(1)}, u32[]{:S(2)}, u32[]{:S(2)}) collective-permute-start(bf16[192,768]{1,0:T(8,128)(2,1)S(1)} %get-tuple-element.225), channel_id=1, source_target_pairs={{0,4},{4,0},{8,12},{12,8},{16,20},{20,16},{24,28},{28,24},{1,5},{5... | collective-permute-start | bytes 884744 | tf_op jit(solution)/shard_map/ppermute | solution.py:907
  88.7 24.1 %collective-permute-start.34 = (bf16[288,512]{1,0:T(8,128)(2,1)S(1)}, bf16[288,512]{1,0:T(8,128)(2,1)S(1)}, u32[]{:S(2)}, u32[]{:S(2)}) collective-permute-start(bf16[288,512]{1,0:T(8,128)(2,1)S(1)} %get-tuple-element.241.refs_2_), channel_id=1, source_target_pairs={{0,16},{4,20},{8,24},{12,28},{16,0},{20,4},{24,8},{28,12},{1,17},{... | collective-permute-start | bytes 884744 | tf_op jit(solution)/shard_map/ppermute | solution.py:907
  91.2 34.1 %collective-permute-start.33 = (bf16[288,512]{1,0:T(8,128)(2,1)S(1)}, bf16[288,512]{1,0:T(8,128)(2,1)S(1)}, u32[]{:S(2)}, u32[]{:S(2)}) collective-permute-start(bf16[288,512]{1,0:T(8,128)(2,1)S(1)} %get-tuple-element.240.refs_0_), channel_id=1, source_target_pairs={{0,16},{4,20},{8,24},{12,28},{16,0},{20,4},{24,8},{28,12},{1,17},{... | collective-permute-start | bytes 884744 | tf_op jit(solution)/shard_map/ppermute | solution.py:907
  108.3 23.2 %collective-permute-start.35 = (bf16[112,768]{1,0:T(8,128)(2,1)S(1)}, bf16[112,768]{1,0:T(8,128)(2,1)S(1)}, u32[]{:S(2)}, u32[]{:S(2)}) collective-permute-start(bf16[112,768]{1,0:T(8,128)(2,1)S(1)} %get-tuple-element.243.refs_0_), channel_id=1, source_target_pairs={{0,16},{4,20},{8,24},{12,28},{16,0},{20,4},{24,8},{28,12},{1,17},{... | collective-permute-start | bytes 516104 | tf_op jit(solution)/shard_map/ppermute | solution.py:907
  112.7 18.8 %collective-permute-start.36 = (bf16[96,768]{1,0:T(8,128)(2,1)S(1)}, bf16[96,768]{1,0:T(8,128)(2,1)S(1)}, u32[]{:S(2)}, u32[]{:S(2)}) collective-permute-start(bf16[96,768]{1,0:T(8,128)(2,1)S(1)} %get-tuple-element.244.refs_2_), channel_id=1, source_target_pairs={{0,16},{4,20},{8,24},{12,28},{16,0},{20,4},{24,8},{28,12},{1,17},{... | collective-permute-start | bytes 442376 | tf_op jit(solution)/shard_map/ppermute | solution.py:907
  126.1 11.7 %collective-permute-start.37 = (bf16[288,512]{1,0:T(8,128)(2,1)S(1)}, bf16[288,512]{1,0:T(8,128)(2,1)S(1)}, u32[]{:S(2)}, u32[]{:S(2)}) collective-permute-start(bf16[288,512]{1,0:T(8,128)(2,1)S(1)} %get-tuple-element.246.refs_0_), channel_id=1, source_target_pairs={{0,8},{4,12},{8,0},{12,4},{16,24},{20,28},{24,16},{28,20},{1,9},{5... | collective-permute-start | bytes 884744 | tf_op jit(solution)/shard_map/ppermute | solution.py:907
  131.6 9.9 %collective-permute-start.39 = (bf16[112,768]{1,0:T(8,128)(2,1)S(1)}, bf16[112,768]{1,0:T(8,128)(2,1)S(1)}, u32[]{:S(2)}, u32[]{:S(2)}) collective-permute-start(bf16[112,768]{1,0:T(8,128)(2,1)S(1)} %get-tuple-element.249.refs_0_), channel_id=1, source_target_pairs={{0,8},{4,12},{8,0},{12,4},{16,24},{20,28},{24,16},{28,20},{1,9},{5... | collective-permute-start | bytes 516104 | tf_op jit(solution)/shard_map/ppermute | solution.py:907
  138.4 16.7 %collective-permute-start.42 = (bf16[576,512]{1,0:T(8,128)(2,1)S(1)}, bf16[576,512]{1,0:T(8,128)(2,1)S(1)}, u32[]{:S(2)}, u32[]{:S(2)}) collective-permute-start(bf16[576,512]{1,0:T(8,128)(2,1)S(1)} %get-tuple-element.256.one), channel_id=1, source_target_pairs={{0,4},{4,0},{8,12},{12,8},{16,20},{20,16},{24,28},{28,24},{1,5},{5... | collective-permute-start | bytes 1769480 | tf_op jit(solution)/shard_map/ppermute | solution.py:907
  138.9 16.3 %collective-permute-start.43 = (bf16[576,512]{1,0:T(8,128)(2,1)S(1)}, bf16[576,512]{1,0:T(8,128)(2,1)S(1)}, u32[]{:S(2)}, u32[]{:S(2)}) collective-permute-start(bf16[576,512]{1,0:T(8,128)(2,1)S(1)} %get-tuple-element.257.two), channel_id=1, source_target_pairs={{0,8},{4,12},{8,0},{12,4},{16,24},{20,28},{24,16},{28,20},{1,9},{5... | collective-permute-start | bytes 1769480 | tf_op jit(solution)/shard_map/ppermute | solution.py:907
  142.1 18.4 %collective-permute-start.44 = (bf16[208,768]{1,0:T(8,128)(2,1)S(1)}, bf16[208,768]{1,0:T(8,128)(2,1)S(1)}, u32[]{:S(2)}, u32[]{:S(2)}) collective-permute-start(bf16[208,768]{1,0:T(8,128)(2,1)S(1)} %get-tuple-element.259.one), channel_id=1, source_target_pairs={{0,4},{4,0},{8,12},{12,8},{16,20},{20,16},{24,28},{28,24},{1,5},{5... | collective-permute-start | bytes 958472 | tf_op jit(solution)/shard_map/ppermute | solution.py:907
  142.4 17.9 %collective-permute-start.45 = (bf16[192,768]{1,0:T(8,128)(2,1)S(1)}, bf16[192,768]{1,0:T(8,128)(2,1)S(1)}, u32[]{:S(2)}, u32[]{:S(2)}) collective-permute-start(bf16[192,768]{1,0:T(8,128)(2,1)S(1)} %get-tuple-element.260.two), channel_id=1, source_target_pairs={{0,8},{4,12},{8,0},{12,4},{16,24},{20,28},{24,16},{28,20},{1,9},{5... | collective-permute-start | bytes 884744 | tf_op jit(solution)/shard_map/ppermute | solution.py:907
  (28 other events, 174.1 us)

commit v3 on v2

--- a/solution.py
+++ b/solution.py
@@ -536,15 +536,43 @@
     grad_ref[...] = dot_tn(mixed_low[...], branch_ref[...]).astype(LOW)
 
 
-def bend(scores_ref, products_ref, probs_ref, ds_ref, h, bias, first, lse_of, delta_of, seg_col, seg_row, fold_ref):
-    window = scores_ref.shape[1]
+def recall_kernel(
+    info, q_ref, k_ref, qp_ref, kp_ref, lse_ref, bias, bias_t, seg_col, seg_row, own_ref, far_ref, near_ref
+):
+    window, width = q_ref.shape
+    heads = width // HEAD
+    queries, keys = q_ref[...], k_ref[...]
+    for h in range(heads):
+        own_ref[h] = dot_nt(keep_head(keys, h), queries)
+    lse = lse_ref[...].T
+    for h in range(heads):
+        for a in range(window // CHUNK):
+            rows = slice(a * CHUNK, (a + 1) * CHUNK)
+            start = SPAN // 2 - a * CHUNK
+            scores = own_ref[h, rows, :] + bias_t[h, :, start : start + window]
+            scores = jnp.where(seg_col[rows, 0:1] == seg_row[...], scores, NEG)
+            own_ref[h, rows, :] = jnp.exp(scores - lse[h : h + 1, :])
+
+    @pl.when(info[3] == 1)
+    def _():
+        first = far_start(info, window)
+        for h in range(heads):
+            far_ref[h] = dot_nt(keep_head(queries, h), kp_ref[...])
+            near_ref[h] = dot_nt(keep_head(keys, h), qp_ref[...])
+        for h in range(heads):
+            for a in range(window // CHUNK):
+                rows = slice(a * CHUNK, (a + 1) * CHUNK)
+                spot = pl.ds(pl.multiple_of(first - a * CHUNK, CHUNK), window)
+                far_ref[h, rows, :] = jnp.exp(far_ref[h, rows, :] + bias[h, :, spot] - lse_ref[rows, h : h + 1])
+                near_ref[h, rows, :] += bias_t[h, :, spot]
+
+
+def bend(weights_of, products_ref, probs_ref, ds_ref, h, delta_of, fold_ref):
+    window = products_ref.shape[1]
     steps = window // CHUNK
     for a in range(steps):
         rows = slice(a * CHUNK, (a + 1) * CHUNK)
-        scores = scores_ref[h, rows, :] + bias[h, :, pl.ds(first - a * CHUNK, window)]
-        if seg_col is not None:
-            scores = jnp.where(seg_col[rows, 0:1] == seg_row[...], scores, NEG)
-        weights = jnp.exp(scores - lse_of(rows))
+        weights = weights_of(rows)
         d_scores = weights * (products_ref[h, rows, :] - delta_of(rows))
         ds_ref[h, rows, :] = d_scores.astype(LOW)
         if probs_ref is not None:
@@ -560,6 +588,15 @@
                 fold_ref[h, :, at : at + window] += d_scores
 
 
+def table_kernel(info, near_fold, far_fold, flipped_ref, bucket_ref, table_ref):
+    window = near_fold.shape[2] // 2
+    table_ref[...] = table_sums(near_fold, flipped_ref, SPAN // 2 - window, table_ref)
+
+    @pl.when(info[3] == 1)
+    def _():
+        table_ref[...] += table_sums(far_fold, bucket_ref, far_start(info, window) - window, table_ref)
+
+
 def table_sums(fold_ref, bucket_ref, start, table_ref):
     heads, buckets = table_ref.shape
     reach = fold_ref.shape[2]
@@ -573,24 +610,19 @@
 
 
 def own_back_kernel(
+    own_ref,
     q_ref,
     k_ref,
     v_ref,
     payload_ref,
     stat_ref,
-    bias_t,
-    seg_col,
-    seg_row,
-    flipped_ref,
     dq_ref,
     dk_ref,
     dv_ref,
-    table_ref,
-    scores_ref,
+    fold_ref,
     products_ref,
     probs_ref,
     ds_ref,
-    fold_ref,
 ):
     window, width = q_ref.shape
     heads = width // HEAD
@@ -598,24 +630,10 @@
     back = payload_ref[:, :width]
     stat = stat_ref[...].T
     for h in range(heads):
-        scores_ref[h] = dot_nt(keep_head(keys, h), queries)
         products_ref[h] = dot_nt(keep_head(values, h), back)
     for h in range(heads):
-        lse, delta = stat[h : h + 1, :], stat[heads + h : heads + h + 1, :]
-        bend(
-            scores_ref,
-            products_ref,
-            probs_ref,
-            ds_ref,
-            h,
-            bias_t,
-            SPAN // 2,
-            lambda rows: lse,
-            lambda rows: delta,
-            seg_col,
-            seg_row,
-            fold_ref,
-        )
+        delta = stat[heads + h : heads + h + 1, :]
+        bend(lambda rows: own_ref[h, rows, :], products_ref, probs_ref, ds_ref, h, lambda rows: delta, fold_ref)
     d_queries = dot_tn(ds_ref[0], keep_head(keys, 0))
     d_keys = dot_nn(ds_ref[0], keep_head(queries, 0))
     d_values = dot_nn(probs_ref[0], keep_head(back, 0))
@@ -626,73 +644,47 @@
     dq_ref[...] = d_queries
     dk_ref[...] = d_keys
     dv_ref[...] = d_values
-    table_ref[...] = table_sums(fold_ref, flipped_ref, SPAN // 2 - window, table_ref)
 
 
 def far_back_kernel(
-    info,
-    q_ref,
-    kp_ref,
-    vp_ref,
-    payload_ref,
-    stat_ref,
-    bias,
-    bucket_ref,
-    dq_in,
-    table_in,
-    dq_ref,
-    table_ref,
-    scores_ref,
-    products_ref,
-    ds_ref,
-    fold_ref,
+    info, far_ref, kp_ref, vp_ref, payload_ref, stat_ref, dq_in, dq_ref, fold_ref, products_ref, ds_ref
 ):
-    window, width = q_ref.shape
+    width = kp_ref.shape[1]
     heads = width // HEAD
 
     @pl.when(info[3] == 1)
     def _():
-        queries, keys, values = q_ref[...], kp_ref[...], vp_ref[...]
+        keys, values = kp_ref[...], vp_ref[...]
         back = payload_ref[:, :width]
-        first = far_start(info, window)
         for h in range(heads):
-            scores_ref[h] = dot_nt(keep_head(queries, h), keys)
             products_ref[h] = dot_nt(keep_head(back, h), values)
         for h in range(heads):
             bend(
-                scores_ref,
+                lambda rows: far_ref[h, rows, :],
                 products_ref,
                 None,
                 ds_ref,
                 h,
-                bias,
-                first,
-                lambda rows: stat_ref[rows, h : h + 1],
                 lambda rows: stat_ref[rows, heads + h : heads + h + 1],
-                None,
-                None,
                 fold_ref,
             )
         d_queries = dq_in[...]
         for h in range(heads):
             d_queries = d_queries + dot_nn(ds_ref[h], keep_head(keys, h))
         dq_ref[...] = (d_queries * HEAD**-0.5).astype(LOW)
-        table_ref[...] = table_in[...] + table_sums(fold_ref, bucket_ref, first - window, table_ref)
 
     @pl.when(info[3] == 0)
     def _():
         dq_ref[...] = (dq_in[...] * HEAD**-0.5).astype(LOW)
-        table_ref[...] = table_in[...]
 
 
 def partner_back_kernel(
     info,
-    k_ref,
+    near_ref,
     v_ref,
     qp_ref,
     from_even,
     from_odd,
-    bias_t,
     dk_in,
     dv_in,
     dq_ref,
@@ -712,12 +704,11 @@
     keep_ref,
     small_ref,
     d_all,
-    scores_ref,
     products_ref,
     probs_ref,
     ds_ref,
 ):
-    window, width = k_ref.shape
+    window, width = v_ref.shape
     heads = width // HEAD
     y, c = info[0], info[1]
     d_all[:, :width] = dq_ref[...]
@@ -725,13 +716,11 @@
     @pl.when(info[3] == 1)
     def _():
         payload = jnp.where(info[6] == 1, from_even[...], from_odd[...])
-        queries, keys, values = qp_ref[...], k_ref[...], v_ref[...]
+        queries, values = qp_ref[...], v_ref[...]
         back = payload[:, :width]
         columns = payload[:, payload.shape[1] - CHUNK :].astype(F32).T
         skip = width % CHUNK
-        first = far_start(info, window)
         for h in range(heads):
-            scores_ref[h] = dot_nt(keep_head(keys, h), queries)
             products_ref[h] = dot_nt(keep_head(values, h), back)
         for h in range(heads):
             at = skip + h
@@ -739,17 +728,12 @@
             at = at + heads
             delta = columns[at : at + 1, :] + columns[at + 2 * heads : at + 2 * heads + 1, :]
             bend(
-                scores_ref,
+                lambda rows: jnp.exp(near_ref[h, rows, :] - lse),
                 products_ref,
                 probs_ref,
                 ds_ref,
                 h,
-                bias_t,
-                first,
-                lambda rows: lse,
                 lambda rows: delta,
-                None,
-                None,
                 None,
             )
         d_keys, d_values = dk_in[...], dv_in[...]
@@ -1163,7 +1147,25 @@
         feed_out_kernel, [shape((half, d), LOW)] * 2, [after(act, gate_send), down_weight], smem=0, micros=30
     )
     feed_got = swap(feed_send, "mp", 1)
-    second_other = after(second_other, feed_send)
+    block = shape((heads, window, window), F32)
+    own_probs, far_probs, near_scores = call(
+        recall_kernel,
+        [block] * 3,
+        [
+            info,
+            after(queries, feed_send),
+            keys,
+            queries_near,
+            keys_near,
+            lse,
+            bias,
+            bias_t,
+            seg_col,
+            seg_row,
+        ],
+        micros=1.0,
+    )
+    second_other = after(second_other, own_probs)
     dh, branch_low = call(
         hidden_back_kernel,
         [shape((local, d), F32), shape((half, d), LOW)],
@@ -1186,20 +1188,20 @@
     payload_even = swap(payload, "dp", 1)
     payload_odd = swap_odd(payload)
     token = feed_sums.advance(payload)
-    fold = pltpu.VMEM((heads, CHUNK, 2 * window), F32)
-    d_queries, d_keys, d_values, table_part = call(
+    fold = shape((heads, CHUNK, 2 * window), F32)
+    d_queries, d_keys, d_values, near_fold = call(
         own_back_kernel,
-        [wide_rows, wide_rows, wide_rows, shape((heads, CHUNK), F32)],
-        [after(queries, token), keys, values, payload, stat_back, bias_t, seg_col, seg_row, flipped_rows],
-        scratch=[square_wide, square_wide, square_low, square_low, fold],
+        [wide_rows, wide_rows, wide_rows, fold],
+        [own_probs, after(queries, token), keys, values, payload, stat_back],
+        scratch=[square_wide, square_low, square_low],
         smem=0,
         micros=200,
     )
-    d_queries, table_part = call(
+    d_queries, far_fold = call(
         far_back_kernel,
-        [low_rows, shape((heads, CHUNK), F32)],
-        [info, queries, keys_near, values_near, payload, stat_back, bias, bucket_rows, d_queries, table_part],
-        scratch=[square_wide, square_wide, square_low, fold],
+        [low_rows, fold],
+        [info, far_probs, keys_near, values_near, payload, stat_back, d_queries],
+        scratch=[square_wide, square_low],
         micros=3.0,
     )
     one_send, one_keep, two_send, two_keep, first_send, first_keep, small = call(
@@ -1208,12 +1210,11 @@
         + [shape((half + EXTRA, d), LOW), shape((half, d), F32), shape((EXTRA // 2, d), F32)],
         [
             info,
-            keys,
+            near_scores,
             values,
             queries_near,
             payload_even,
             payload_odd,
-            bias_t,
             d_keys,
             d_values,
             d_queries,
@@ -1226,7 +1227,7 @@
             out_grad,
             gain_two_part,
         ],
-        scratch=[pltpu.VMEM((window, 3 * width), LOW), square_wide, square_wide, square_low, square_low],
+        scratch=[pltpu.VMEM((window, 3 * width), LOW), square_wide, square_low, square_low],
         micros=300,
     )
     token = feed_sums.advance(one_send, micros=300)
@@ -1240,6 +1241,12 @@
     )
     first_got = swap(first_send, "mp", 2)
     token = joint_sums.advance(first_send)
+    (table_part,) = call(
+        table_kernel,
+        [shape((heads, CHUNK), F32)],
+        [info, after(near_fold, token), far_fold, flipped_rows, bucket_rows],
+        micros=1.0,
+    )
     input_grad, small = call(
         input_back_kernel,
         [shape((local, d), LOW), shape((EXTRA // 2, d), F32)],

time: 163 us -> 158 us (0.969)
  starting transfers between devices: 47.6 us -> 43.2 us
  waiting for transfers between devices: 66.4 us -> 64.3 us
  Pallas kernels: 46.7 us -> 48.5 us
    ppermute x44, starting transfers between devices: 46 us -> 41.6 us  [swap(): lax.ppermute(values, axis, [(i, i ^ bit) for i in range(lax.axis_size(axi...]
    ppermute x44, waiting for transfers between devices: 66.4 us -> 64.3 us  [swap(): lax.ppermute(values, axis, [(i, i ^ bit) for i in range(lax.axis_size(axi...]
    pallas_call x29 -> x31, Pallas kernels: 46.7 us -> 48.5 us  [call(): pl.pallas_call(kernel, out_shape=outs, in_specs=[SMEM] * smem + [VMEM] *...]
  transfers between devices with their start and end apart: 46 -> 46, of which waited for: 22 -> 26; matrix products, arithmetic and copies ran while one was open for 1% -> 1% of each run, Pallas kernels for 24% -> 26%
where the time goes in v3:
time: 158 us
  waiting for transfers between devices  64.3 us (41%)
  Pallas kernels  48.5 us (31%)
  starting transfers between devices  43.2 us (27%)
    ppermute x44, waiting for transfers between devices, swap(): lax.ppermute(values, axis, [(i, i ^ bit) for i in range(lax.axis_size(axi...  64.3 us
    pallas_call x31, Pallas kernels, call(): pl.pallas_call(kernel, out_shape=outs, in_specs=[SMEM] * smem + [VMEM] *...  48.5 us
    ppermute x44, starting transfers between devices, swap(): lax.ppermute(values, axis, [(i, i ^ bit) for i in range(lax.axis_size(axi...  41.6 us
  transfers between devices with their start and end apart: 46, of which 26 were waited for; matrix products, arithmetic and copies ran while one was open for 1% of the time, Pallas kernels for 26%

profile of v3, /device:TPU:0, one launch (start us, length us, event | category | flops | bytes accessed | tf_op | source)
XLA Modules:
  0.0 157.8 jit_solution(7464101925769134833)
XLA Ops:
  0.7 3.0 %collective-permute-start = (bf16[128,768]{1,0:T(8,128)(2,1)}, bf16[128,768]{1,0:T(8,128)(2,1)S(1)}, u32[]{:S(2)}, u32[]{:S(2)}) collective-permute-start(bf16[128,768]{1,0:T(8,128)(2,1)} %x_ref.1), channel_id=1, source_target_pairs={{0,2},{1,3},{2,0},{3,1},{4,6},{5,7},{6,4},{7,5},{8,10},{9,11},{10,... | collective-permute-start | bytes 589832 | tf_op jit(solution)/shard_map/ppermute | solution.py:891
  7.3 3.9 %shard_map.229 = (s32[8]{0:T(128)S(1)}, f32[1,512]{1,0:T(1,128)S(1)}, f32[512,128]{1,0:T(8,128)S(1)}, f32[3,128,2048]{2,1,0:T(8,128)S(1)}, f32[3,32]{1,0:T(4,128...) custom-call(s32[2]{0:T(128)S(1)} %pad_add_fusion.spot, s32[16,128]{1,0:T(8,128)S(1)} %add_bitcast_fusion.bucket_ref, ...), custom_call_target="tpu_custom_call" | custom-call | flops 60000000 | tf_op jit(solution)/shard_map/pallas_call | solution.py:37
  17.1 5.0 %shard_map.231 = (bf16[512,768]{1,0:T(8,128)(2,1)S(1)}, bf16[512,768]{1,0:T(8,128)(2,1)S(1)}, bf16[512,192]{1,0:T(8,128)(2,1)S(1)}, bf16[512,192]{1,0:T(8,128)(2...) custom-call(s32[8]{0:T(128)S(1)} %get-tuple-element.146.info, ...), custom_call_target="tpu_custom_call" | custom-call | flops 100000000 | tf_op jit(solution)/shard_map/pallas_call | solution.py:37
  24.4 4.1 %shard_map.232 = (bf16[512,192]{1,0:T(8,128)(2,1)S(1)}, f32[512,192]{1,0:T(8,128)S(1)}, f32[512,128]{1,0:T(8,128)S(1)}, bf16[512,192]{1,0:T(8,128)(2,1)S(1)}, bf...) custom-call(s32[8]{0:T(128)S(1)} %get-tuple-element.146.info, bf16[128,768]{1,0:T(8,128)(2,1)S(1)} %shard_map.230.x0, ...), custom_call_target="tpu_custom_call" | custom-call | flops 6000000000 | tf_op jit(solution)/shard_map/pallas_call | solution.py:37
  30.0 2.8 %collective-permute-done.12.o1 = bf16[192,768]{1,0:T(8,128)(2,1)S(1)} collective-permute-done((bf16[192,768]{1,0:T(8,128)(2,1)S(1)}, bf16[192,768]{1,0:T(8,128)(2,1)S(1)}, u32[]{:S(2)}, u32[]{:S(2)}) %collective-permute-start.12) | collective-permute-done | bytes 294944 | tf_op jit(solution)/shard_map/ppermute | solution.py:891
  39.6 4.5 %shard_map.235 = (bf16[512,768]{1,0:T(8,128)(2,1)S(1)}, f32[256,768]{1,0:T(8,128)S(1)}, bf16[512,512]{1,0:T(8,128)(2,1)S(1)}, bf16[512,512]{1,0:T(8,128)(2,1)S(1...) custom-call(s32[8]{0:T(128)S(1)} %get-tuple-element.146.info, ...), custom_call_target="tpu_custom_call" | custom-call | flops 100000000 | tf_op jit(solution)/shard_map/pallas_call | solution.py:37
  53.8 2.6 %shard_map.239 = (f32[3,512,512]{2,1,0:T(8,128)S(1)}, f32[3,512,512]{2,1,0:T(8,128)S(1)}, f32[3,512,512]{2,1,0:T(8,128)S(1)}) custom-call(s32[8]{0:T(128)S(1)} %get-tuple-element.146.info, bf16[512,192]{1,0:T(8,128)(2,1)S(1)} %get-tuple-element.208.q_ref, bf16[512,192]{1,0:T(8,128)(2,1)S(1)} %get-tuple-element.188.k_ref, ...), custom_call_target="tpu_custom_call" | custom-call | flops 20000000 | tf_op jit(solution)/shard_map/pallas_call | solution.py:37
  60.9 2.7 %collective-permute-start.21 = (bf16[512,256]{1,0:T(8,128)(2,1)S(1)}, bf16[512,256]{1,0:T(8,128)(2,1)S(1)}, u32[]{:S(2)}, u32[]{:S(2)}) collective-permute-start(bf16[512,256]{1,0:T(8,128)(2,1)S(1)} %get-tuple-element.202.payload_ref), channel_id=1, source_target_pairs={{0,4},{4,0},{8,12},{12,8},{16,20},{20,16},{24,28},{28,24},{1,5},{5... | collective-permute-start | bytes 786440 | tf_op jit(solution)/shard_map/ppermute | solution.py:891
  68.9 2.4 %collective-permute-start.26 = (bf16[288,512]{1,0:T(8,128)(2,1)S(1)}, bf16[288,512]{1,0:T(8,128)(2,1)S(1)}, u32[]{:S(2)}, u32[]{:S(2)}) collective-permute-start(bf16[288,512]{1,0:T(8,128)(2,1)S(1)} %get-tuple-element.225), channel_id=1, source_target_pairs={{0,4},{4,0},{8,12},{12,8},{16,20},{20,16},{24,28},{28,24},{1,5},{5... | collective-permute-start | bytes 884744 | tf_op jit(solution)/shard_map/ppermute | solution.py:891
  71.3 2.5 %shard_map.244 = (f32[512,192]{1,0:T(8,128)S(1)}, f32[512,192]{1,0:T(8,128)S(1)}, f32[512,192]{1,0:T(8,128)S(1)}, f32[3,128,1024]{2,1,0:T(8,128)S(1)}) custom-call(f32[3,512,512]{2,1,0:T(8,128)S(1)} %get-tuple-element.194.own_ref, bf16[512,192]{1,0:T(8,128)(2,1)S(1)} %get-tuple-element.208.q_ref, bf16[512,192]{1,0:T(8,128)(2,1)S(1)} %get-tuple-element.188.k_ref, ...), custom_call_target="tpu_custom_call" | custom-call | flops 4000000000 | tf_op jit(solution)/shard_map/pallas_call | solution.py:37
  75.9 3.9 %shard_map.246 = (bf16[192,768]{1,0:T(8,128)(2,1)S(1)}, bf16[192,768]{1,0:T(8,128)(2,1)S(1)}, bf16[192,768]{1,0:T(8,128)(2,1)S(1)}, bf16[192,768]{1,0:T(8,128)(2...) custom-call(s32[8]{0:T(128)S(1)} %get-tuple-element.146.info, ...), custom_call_target="tpu_custom_call" | custom-call | flops 6000000000 | tf_op jit(solution)/shard_map/pallas_call | solution.py:37
  79.9 2.4 %collective-permute-start.29 = (bf16[192,768]{1,0:T(8,128)(2,1)S(1)}, bf16[192,768]{1,0:T(8,128)(2,1)S(1)}, u32[]{:S(2)}, u32[]{:S(2)}) collective-permute-start(bf16[192,768]{1,0:T(8,128)(2,1)S(1)} %get-tuple-element.234), channel_id=1, source_target_pairs={{0,8},{4,12},{8,0},{12,4},{16,24},{20,28},{24,16},{28,20},{1,9},{5... | collective-permute-start | bytes 884744 | tf_op jit(solution)/shard_map/ppermute | solution.py:891
  84.4 2.6 %collective-permute-start.33 = (bf16[288,512]{1,0:T(8,128)(2,1)S(1)}, bf16[288,512]{1,0:T(8,128)(2,1)S(1)}, u32[]{:S(2)}, u32[]{:S(2)}) collective-permute-start(bf16[288,512]{1,0:T(8,128)(2,1)S(1)} %get-tuple-element.250.refs_0_), channel_id=1, source_target_pairs={{0,16},{4,20},{8,24},{12,28},{16,0},{20,4},{24,8},{28,12},{1,17},{... | collective-permute-start | bytes 884744 | tf_op jit(solution)/shard_map/ppermute | solution.py:891
  88.8 5.4 %collective-permute-done.29.refs_3_ = bf16[192,768]{1,0:T(8,128)(2,1)S(1)} collective-permute-done((bf16[192,768]{1,0:T(8,128)(2,1)S(1)}, bf16[192,768]{1,0:T(8,128)(2,1)S(1)}, u32[]{:S(2)}, u32[]{:S(2)}) %collective-permute-start.29) | collective-permute-done | bytes 294944 | tf_op jit(solution)/shard_map/ppermute | solution.py:891
  97.0 2.5 %shard_map.250.table_ref = f32[3,128]{1,0:T(4,128)S(1)} custom-call(s32[8]{0:T(128)S(1)} %get-tuple-element.146.info, f32[3,128,1024]{2,1,0:T(8,128)S(1)} %get-tuple-element.242.near_fold, f32[3,128,1024]{2,1,0:T(8,128)S(1)} %get-tuple-element.243.far_fold, s32[16,128]{1,0:T(8,128)S(1)} %get-tuple-element.244.flipped_ref, ...), custom_call_target="tpu_custom_call" | custom-call | flops 20000000 | tf_op jit(solution)/shard_map/pallas_call | solution.py:37
  100.5 4.5 %collective-permute-done.31.refs_1_ = bf16[96,768]{1,0:T(8,128)(2,1)S(1)} collective-permute-done((bf16[96,768]{1,0:T(8,128)(2,1)S(1)}, bf16[96,768]{1,0:T(8,128)(2,1)S(1)}, u32[]{:S(2)}, u32[]{:S(2)}) %collective-permute-start.31) | collective-permute-done | bytes 147488 | tf_op jit(solution)/shard_map/ppermute | solution.py:891
  105.1 3.4 %collective-permute-start.35 = (bf16[112,768]{1,0:T(8,128)(2,1)S(1)}, bf16[112,768]{1,0:T(8,128)(2,1)S(1)}, u32[]{:S(2)}, u32[]{:S(2)}) collective-permute-start(bf16[112,768]{1,0:T(8,128)(2,1)S(1)} %get-tuple-element.253.refs_0_), channel_id=1, source_target_pairs={{0,16},{4,20},{8,24},{12,28},{16,0},{20,4},{24,8},{28,12},{1,17},{... | collective-permute-start | bytes 516104 | tf_op jit(solution)/shard_map/ppermute | solution.py:891
  108.5 12.5 %collective-permute-done.34.refs_3_ = bf16[288,512]{1,0:T(8,128)(2,1)S(1)} collective-permute-done((bf16[288,512]{1,0:T(8,128)(2,1)S(1)}, bf16[288,512]{1,0:T(8,128)(2,1)S(1)}, u32[]{:S(2)}, u32[]{:S(2)}) %collective-permute-start.34) | collective-permute-done | bytes 294944 | tf_op jit(solution)/shard_map/ppermute | solution.py:891
  122.1 4.6 %collective-permute-done.36.refs_3_ = bf16[96,768]{1,0:T(8,128)(2,1)S(1)} collective-permute-done((bf16[96,768]{1,0:T(8,128)(2,1)S(1)}, bf16[96,768]{1,0:T(8,128)(2,1)S(1)}, u32[]{:S(2)}, u32[]{:S(2)}) %collective-permute-start.36) | collective-permute-done | bytes 147488 | tf_op jit(solution)/shard_map/ppermute | solution.py:891
  127.3 5.7 %collective-permute-done.37.refs_1_ = bf16[288,512]{1,0:T(8,128)(2,1)S(1)} collective-permute-done((bf16[288,512]{1,0:T(8,128)(2,1)S(1)}, bf16[288,512]{1,0:T(8,128)(2,1)S(1)}, u32[]{:S(2)}, u32[]{:S(2)}) %collective-permute-start.37) | collective-permute-done | bytes 294944 | tf_op jit(solution)/shard_map/ppermute | solution.py:891
  134.1 2.6 %collective-permute-done.39.refs_1_ = bf16[112,768]{1,0:T(8,128)(2,1)S(1)} collective-permute-done((bf16[112,768]{1,0:T(8,128)(2,1)S(1)}, bf16[112,768]{1,0:T(8,128)(2,1)S(1)}, u32[]{:S(2)}, u32[]{:S(2)}) %collective-permute-start.39) | collective-permute-done | bytes 172064 | tf_op jit(solution)/shard_map/ppermute | solution.py:891
  140.0 4.3 %collective-permute-done.41.got_ref = bf16[128,768]{1,0:T(8,128)(2,1)S(1)} collective-permute-done((bf16[128,768]{1,0:T(8,128)(2,1)S(1)}, bf16[128,768]{1,0:T(8,128)(2,1)S(1)}, u32[]{:S(2)}, u32[]{:S(2)}) %collective-permute-start.41) | collective-permute-done | bytes 196640 | tf_op jit(solution)/shard_map/ppermute | solution.py:891
  145.0 4.9 %collective-permute-done.42.one_got = bf16[576,512]{1,0:T(8,128)(2,1)S(1)} collective-permute-done((bf16[576,512]{1,0:T(8,128)(2,1)S(1)}, bf16[576,512]{1,0:T(8,128)(2,1)S(1)}, u32[]{:S(2)}, u32[]{:S(2)}) %collective-permute-start.42) | collective-permute-done | bytes 589856 | tf_op jit(solution)/shard_map/ppermute | solution.py:891
  150.4 3.1 %shard_map.258 = (f32[768,512]{1,0:T(8,128)}, f32[768,512]{1,0:T(8,128)}, f32[512,768]{1,0:T(8,128)}) custom-call(s32[8]{0:T(128)S(1)} %get-tuple-element.146.info, bf16[576,512]{1,0:T(8,128)(2,1)S(1)} %get-tuple-element.266.one, bf16[576,512]{1,0:T(8,128)(2,1)S(1)} %collective-permute-done.42.one_got, bf16[576,512]{1,0:T(8,128)(2,1)S(1)} %get-tuple-element.267.two, ...), custom_call_target="tpu_custom_call" | custom-call | flops 40000000 | tf_op jit(solution)/shard_map/pallas_call | solution.py:37
  (113 shorter events, 60.9 us)
Async XLA Ops:
  0.7 12.4 %collective-permute-start = (bf16[128,768]{1,0:T(8,128)(2,1)}, bf16[128,768]{1,0:T(8,128)(2,1)S(1)}, u32[]{:S(2)}, u32[]{:S(2)}) collective-permute-start(bf16[128,768]{1,0:T(8,128)(2,1)} %x_ref.1), channel_id=1, source_target_pairs={{0,2},{1,3},{2,0},{3,1},{4,6},{5,7},{6,4},{7,5},{8,10},{9,11},{10,... | collective-permute-start | bytes 589832 | tf_op jit(solution)/shard_map/ppermute | solution.py:891
  46.0 11.2 %collective-permute-start.18 = (bf16[256,768]{1,0:T(8,128)(2,1)S(1)}, bf16[256,768]{1,0:T(8,128)(2,1)S(1)}, u32[]{:S(2)}, u32[]{:S(2)}) collective-permute-start(bf16[256,768]{1,0:T(8,128)(2,1)S(1)} %shard_map.236.sum_ref), channel_id=1, source_target_pairs={{0,2},{1,3},{2,0},{3,1},{4,6},{5,7},{6,4},{7,5},{8,10},{9,11},{10,... | collective-permute-start | bytes 1179656 | tf_op jit(solution)/shard_map/ppermute | solution.py:891
  49.3 15.8 %collective-permute-start.23 = (bf16[576,512]{1,0:T(8,128)(2,1)S(1)}, bf16[576,512]{1,0:T(8,128)(2,1)S(1)}, u32[]{:S(2)}, u32[]{:S(2)}) collective-permute-start(bf16[576,512]{1,0:T(8,128)(2,1)S(1)} %get-tuple-element.184), channel_id=1, source_target_pairs={{0,4},{4,0},{8,12},{12,8},{16,20},{20,16},{24,28},{28,24},{1,5},{5... | collective-permute-start | bytes 1769480 | tf_op jit(solution)/shard_map/ppermute | solution.py:891
  51.6 14.8 %collective-permute-start.24 = (bf16[576,512]{1,0:T(8,128)(2,1)S(1)}, bf16[576,512]{1,0:T(8,128)(2,1)S(1)}, u32[]{:S(2)}, u32[]{:S(2)}) collective-permute-start(bf16[576,512]{1,0:T(8,128)(2,1)S(1)} %get-tuple-element.206), channel_id=1, source_target_pairs={{0,8},{4,12},{8,0},{12,4},{16,24},{20,28},{24,16},{28,20},{1,9},{5... | collective-permute-start | bytes 1769480 | tf_op jit(solution)/shard_map/ppermute | solution.py:891
  60.9 15.0 %collective-permute-start.21 = (bf16[512,256]{1,0:T(8,128)(2,1)S(1)}, bf16[512,256]{1,0:T(8,128)(2,1)S(1)}, u32[]{:S(2)}, u32[]{:S(2)}) collective-permute-start(bf16[512,256]{1,0:T(8,128)(2,1)S(1)} %get-tuple-element.202.payload_ref), channel_id=1, source_target_pairs={{0,4},{4,0},{8,12},{12,8},{16,20},{20,16},{24,28},{28,24},{1,5},{5... | collective-permute-start | bytes 786440 | tf_op jit(solution)/shard_map/ppermute | solution.py:891
  63.6 12.3 %collective-permute-start.22 = (bf16[512,256]{1,0:T(8,128)(2,1)S(1)}, bf16[512,256]{1,0:T(8,128)(2,1)S(1)}, u32[]{:S(2)}, u32[]{:S(2)}) collective-permute-start(bf16[512,256]{1,0:T(8,128)(2,1)S(1)} %get-tuple-element.202.payload_ref), channel_id=1, source_target_pairs={{4,8},{12,16},{20,24},{8,4},{16,12},{24,20},{5,9},{13,17},{21,25},... | collective-permute-start | bytes 786440 | tf_op jit(solution)/shard_map/ppermute | solution.py:896
  67.2 15.1 %collective-permute-start.25 = (bf16[288,512]{1,0:T(8,128)(2,1)S(1)}, bf16[288,512]{1,0:T(8,128)(2,1)S(1)}, u32[]{:S(2)}, u32[]{:S(2)}) collective-permute-start(bf16[288,512]{1,0:T(8,128)(2,1)S(1)} %get-tuple-element.207), channel_id=1, source_target_pairs={{0,8},{4,12},{8,0},{12,4},{16,24},{20,28},{24,16},{28,20},{1,9},{5... | collective-permute-start | bytes 884744 | tf_op jit(solution)/shard_map/ppermute | solution.py:891
  68.9 13.4 %collective-permute-start.26 = (bf16[288,512]{1,0:T(8,128)(2,1)S(1)}, bf16[288,512]{1,0:T(8,128)(2,1)S(1)}, u32[]{:S(2)}, u32[]{:S(2)}) collective-permute-start(bf16[288,512]{1,0:T(8,128)(2,1)S(1)} %get-tuple-element.225), channel_id=1, source_target_pairs={{0,4},{4,0},{8,12},{12,8},{16,20},{20,16},{24,28},{28,24},{1,5},{5... | collective-permute-start | bytes 884744 | tf_op jit(solution)/shard_map/ppermute | solution.py:891
  79.9 14.3 %collective-permute-start.29 = (bf16[192,768]{1,0:T(8,128)(2,1)S(1)}, bf16[192,768]{1,0:T(8,128)(2,1)S(1)}, u32[]{:S(2)}, u32[]{:S(2)}) collective-permute-start(bf16[192,768]{1,0:T(8,128)(2,1)S(1)} %get-tuple-element.234), channel_id=1, source_target_pairs={{0,8},{4,12},{8,0},{12,4},{16,24},{20,28},{24,16},{28,20},{1,9},{5... | collective-permute-start | bytes 884744 | tf_op jit(solution)/shard_map/ppermute | solution.py:891
  82.4 11.8 %collective-permute-start.28 = (bf16[192,768]{1,0:T(8,128)(2,1)S(1)}, bf16[192,768]{1,0:T(8,128)(2,1)S(1)}, u32[]{:S(2)}, u32[]{:S(2)}) collective-permute-start(bf16[192,768]{1,0:T(8,128)(2,1)S(1)} %get-tuple-element.232), channel_id=1, source_target_pairs={{0,4},{4,0},{8,12},{12,8},{16,20},{20,16},{24,28},{28,24},{1,5},{5... | collective-permute-start | bytes 884744 | tf_op jit(solution)/shard_map/ppermute | solution.py:891
  84.4 24.1 %collective-permute-start.33 = (bf16[288,512]{1,0:T(8,128)(2,1)S(1)}, bf16[288,512]{1,0:T(8,128)(2,1)S(1)}, u32[]{:S(2)}, u32[]{:S(2)}) collective-permute-start(bf16[288,512]{1,0:T(8,128)(2,1)S(1)} %get-tuple-element.250.refs_0_), channel_id=1, source_target_pairs={{0,16},{4,20},{8,24},{12,28},{16,0},{20,4},{24,8},{28,12},{1,17},{... | collective-permute-start | bytes 884744 | tf_op jit(solution)/shard_map/ppermute | solution.py:891
  87.0 34.0 %collective-permute-start.34 = (bf16[288,512]{1,0:T(8,128)(2,1)S(1)}, bf16[288,512]{1,0:T(8,128)(2,1)S(1)}, u32[]{:S(2)}, u32[]{:S(2)}) collective-permute-start(bf16[288,512]{1,0:T(8,128)(2,1)S(1)} %get-tuple-element.251.refs_2_), channel_id=1, source_target_pairs={{0,16},{4,20},{8,24},{12,28},{16,0},{20,4},{24,8},{28,12},{1,17},{... | collective-permute-start | bytes 884744 | tf_op jit(solution)/shard_map/ppermute | solution.py:891
  87.4 12.1 %collective-permute-start.30 = (bf16[144,768]{1,0:T(8,128)(2,1)S(1)}, bf16[144,768]{1,0:T(8,128)(2,1)S(1)}, u32[]{:S(2)}, u32[]{:S(2)}) collective-permute-start(bf16[144,768]{1,0:T(8,128)(2,1)S(1)} %get-tuple-element.230), channel_id=1, source_target_pairs={{0,2},{1,3},{2,0},{3,1},{4,6},{5,7},{6,4},{7,5},{8,10},{9,11},{10,... | collective-permute-start | bytes 663560 | tf_op jit(solution)/shard_map/ppermute | solution.py:891
  94.9 10.1 %collective-permute-start.31 = (bf16[96,768]{1,0:T(8,128)(2,1)S(1)}, bf16[96,768]{1,0:T(8,128)(2,1)S(1)}, u32[]{:S(2)}, u32[]{:S(2)}) collective-permute-start(bf16[96,768]{1,0:T(8,128)(2,1)S(1)} %get-tuple-element.238), channel_id=1, source_target_pairs={{0,8},{4,12},{8,0},{12,4},{16,24},{20,28},{24,16},{28,20},{1,9},{5... | collective-permute-start | bytes 442376 | tf_op jit(solution)/shard_map/ppermute | solution.py:891
  95.0 10.0 %collective-permute-start.32 = (bf16[96,768]{1,0:T(8,128)(2,1)S(1)}, bf16[96,768]{1,0:T(8,128)(2,1)S(1)}, u32[]{:S(2)}, u32[]{:S(2)}) collective-permute-start(bf16[96,768]{1,0:T(8,128)(2,1)S(1)} %get-tuple-element.248), channel_id=1, source_target_pairs={{0,4},{4,0},{8,12},{12,8},{16,20},{20,16},{24,28},{28,24},{1,5},{5... | collective-permute-start | bytes 442376 | tf_op jit(solution)/shard_map/ppermute | solution.py:891
  105.1 21.7 %collective-permute-start.35 = (bf16[112,768]{1,0:T(8,128)(2,1)S(1)}, bf16[112,768]{1,0:T(8,128)(2,1)S(1)}, u32[]{:S(2)}, u32[]{:S(2)}) collective-permute-start(bf16[112,768]{1,0:T(8,128)(2,1)S(1)} %get-tuple-element.253.refs_0_), channel_id=1, source_target_pairs={{0,16},{4,20},{8,24},{12,28},{16,0},{20,4},{24,8},{28,12},{1,17},{... | collective-permute-start | bytes 516104 | tf_op jit(solution)/shard_map/ppermute | solution.py:891
  108.4 18.3 %collective-permute-start.36 = (bf16[96,768]{1,0:T(8,128)(2,1)S(1)}, bf16[96,768]{1,0:T(8,128)(2,1)S(1)}, u32[]{:S(2)}, u32[]{:S(2)}) collective-permute-start(bf16[96,768]{1,0:T(8,128)(2,1)S(1)} %get-tuple-element.254.refs_2_), channel_id=1, source_target_pairs={{0,16},{4,20},{8,24},{12,28},{16,0},{20,4},{24,8},{28,12},{1,17},{... | collective-permute-start | bytes 442376 | tf_op jit(solution)/shard_map/ppermute | solution.py:891
  121.2 11.8 %collective-permute-start.37 = (bf16[288,512]{1,0:T(8,128)(2,1)S(1)}, bf16[288,512]{1,0:T(8,128)(2,1)S(1)}, u32[]{:S(2)}, u32[]{:S(2)}) collective-permute-start(bf16[288,512]{1,0:T(8,128)(2,1)S(1)} %get-tuple-element.256.refs_0_), channel_id=1, source_target_pairs={{0,8},{4,12},{8,0},{12,4},{16,24},{20,28},{24,16},{28,20},{1,9},{5... | collective-permute-start | bytes 884744 | tf_op jit(solution)/shard_map/ppermute | solution.py:891
  121.3 11.8 %collective-permute-start.38 = (bf16[288,512]{1,0:T(8,128)(2,1)S(1)}, bf16[288,512]{1,0:T(8,128)(2,1)S(1)}, u32[]{:S(2)}, u32[]{:S(2)}) collective-permute-start(bf16[288,512]{1,0:T(8,128)(2,1)S(1)} %get-tuple-element.257.refs_2_), channel_id=1, source_target_pairs={{0,4},{4,0},{8,12},{12,8},{16,20},{20,16},{24,28},{28,24},{1,5},{5... | collective-permute-start | bytes 884744 | tf_op jit(solution)/shard_map/ppermute | solution.py:891
  126.8 9.9 %collective-permute-start.39 = (bf16[112,768]{1,0:T(8,128)(2,1)S(1)}, bf16[112,768]{1,0:T(8,128)(2,1)S(1)}, u32[]{:S(2)}, u32[]{:S(2)}) collective-permute-start(bf16[112,768]{1,0:T(8,128)(2,1)S(1)} %get-tuple-element.259.refs_0_), channel_id=1, source_target_pairs={{0,8},{4,12},{8,0},{12,4},{16,24},{20,28},{24,16},{28,20},{1,9},{5... | collective-permute-start | bytes 516104 | tf_op jit(solution)/shard_map/ppermute | solution.py:891
  133.7 16.3 %collective-permute-start.42 = (bf16[576,512]{1,0:T(8,128)(2,1)S(1)}, bf16[576,512]{1,0:T(8,128)(2,1)S(1)}, u32[]{:S(2)}, u32[]{:S(2)}) collective-permute-start(bf16[576,512]{1,0:T(8,128)(2,1)S(1)} %get-tuple-element.266.one), channel_id=1, source_target_pairs={{0,4},{4,0},{8,12},{12,8},{16,20},{20,16},{24,28},{28,24},{1,5},{5... | collective-permute-start | bytes 1769480 | tf_op jit(solution)/shard_map/ppermute | solution.py:891
  134.1 16.3 %collective-permute-start.43 = (bf16[576,512]{1,0:T(8,128)(2,1)S(1)}, bf16[576,512]{1,0:T(8,128)(2,1)S(1)}, u32[]{:S(2)}, u32[]{:S(2)}) collective-permute-start(bf16[576,512]{1,0:T(8,128)(2,1)S(1)} %get-tuple-element.267.two), channel_id=1, source_target_pairs={{0,8},{4,12},{8,0},{12,4},{16,24},{20,28},{24,16},{28,20},{1,9},{5... | collective-permute-start | bytes 1769480 | tf_op jit(solution)/shard_map/ppermute | solution.py:891
  137.3 18.4 %collective-permute-start.44 = (bf16[208,768]{1,0:T(8,128)(2,1)S(1)}, bf16[208,768]{1,0:T(8,128)(2,1)S(1)}, u32[]{:S(2)}, u32[]{:S(2)}) collective-permute-start(bf16[208,768]{1,0:T(8,128)(2,1)S(1)} %get-tuple-element.269.one), channel_id=1, source_target_pairs={{0,4},{4,0},{8,12},{12,8},{16,20},{20,16},{24,28},{28,24},{1,5},{5... | collective-permute-start | bytes 958472 | tf_op jit(solution)/shard_map/ppermute | solution.py:891
  137.7 17.9 %collective-permute-start.45 = (bf16[192,768]{1,0:T(8,128)(2,1)S(1)}, bf16[192,768]{1,0:T(8,128)(2,1)S(1)}, u32[]{:S(2)}, u32[]{:S(2)}) collective-permute-start(bf16[192,768]{1,0:T(8,128)(2,1)S(1)} %get-tuple-element.270.two), channel_id=1, source_target_pairs={{0,8},{4,12},{8,0},{12,4},{16,24},{20,28},{24,16},{28,20},{1,9},{5... | collective-permute-start | bytes 884744 | tf_op jit(solution)/shard_map/ppermute | solution.py:891
  (28 other events, 208.0 us)

commit v4 on v3

--- a/solution.py
+++ b/solution.py
@@ -186,6 +186,21 @@
     for h in range(1, width // HEAD):
         out = jnp.where(lane >= h * HEAD, packed[:, h : h + 1], out)
     return out
+
+
+def pack_lanes(values, target):
+    rows = values.shape[0]
+    target[:rows, :] = values[:, :CHUNK]
+    rest = values[:, CHUNK:]
+    target[rows : rows + rows // 2, :] = jnp.concatenate([rest[: rows // 2], rest[rows // 2 :]], axis=1)
+
+
+def unpack_lanes(packed, rows):
+    rest = packed[rows : rows + rows // 2, :]
+    half = CHUNK // 2
+    return jnp.concatenate(
+        [packed[:rows, :], jnp.concatenate([rest[:, :half], rest[:, half:]], axis=0)], axis=1
+    )
 
 
 def place(y, c):
@@ -302,6 +317,7 @@
     top_ref,
     sum_ref,
     mixed_low,
+    packed_ref,
     mixed_ref,
     lse_ref,
     qp_ref,
@@ -362,6 +378,8 @@
             mixed_low[rows, :] = mixed.astype(LOW)
             lse_ref[rows, :] = top_ref[rows, :] + jnp.log(whole)
 
+    pack_lanes(mixed_low[...], packed_ref)
+
 
 def cotangent_kernel(g0, g1, g2, g3, down_w, cot_ref, d_act_ref):
     for part, piece in enumerate((g2, g3, g0, g1)):
@@ -369,14 +387,16 @@
     d_act_ref[...] = dot_nt(cot_ref[...], down_w[...])
 
 
+def base_kernel(x_all, m0, o0, base_ref):
+    base_ref[...] = x_all[...].astype(F32) + dot_nn(m0[...], o0[...])
+
+
 def feed_kernel(
     info,
-    x_all,
-    m0,
+    base_ref,
     m1,
     m2,
     m3,
-    o0,
     o1,
     o2,
     o3,
@@ -395,7 +415,7 @@
 ):
     y, c = info[0], info[1]
     half = 2 * CHUNK
-    gain_sum = jnp.zeros((1, x_all.shape[1]), F32)
+    gain_sum = jnp.zeros((1, base_ref.shape[1]), F32)
     for part, core in enumerate((1 - c, c)):
         rows = slice(part * half, (part + 1) * half)
         spots = (aligned((2 * y + core) * CHUNK), aligned((2 * (1 - y) + core) * CHUNK))
@@ -403,11 +423,16 @@
         def pick(ref):
             return jnp.concatenate([ref[spots[0], :], ref[spots[1], :]], axis=0)
 
-        hidden = pick(x_all).astype(F32)
-        branch = dot_nn(pick(m0), o0[...])
-        for m, o in ((m1, o1), (m2, o2), (m3, o3)):
-            branch = branch + dot_nn(pick(m), o[...])
-        hidden = hidden + branch
+        hidden = pick(base_ref)
+        window = base_ref.shape[0]
+        for m, o in ((m2, o2), (m1, o1), (m3, o3)):
+            parts = []
+            for row in (y, 1 - y):
+                block = m[aligned(window + core * CHUNK), :]
+                lane = lax.broadcasted_iota(jnp.int32, block.shape, 1)
+                parts.append(jnp.where(lane // HEAD == row, block, jnp.zeros_like(block)))
+            both = jnp.concatenate([pick(m), jnp.concatenate(parts, axis=0)], axis=1)
+            hidden = hidden + dot_nn(both, jnp.concatenate([o[...], o[CHUNK:, :]], axis=0))
         if part == 1:
             hidden_ref[...] = hidden
         unit = hidden * rows_norm(hidden)
@@ -505,35 +530,28 @@
 
 
 def mixed_back_kernel(
-    info, pair_own, pair_other, out_w, mixed_ref, mixed_low, lse_ref, payload_ref, stat_ref, grad_ref, branch_ref, pad_ref
+    info, pair_own, pair_other, out_w, mixed_ref, lse_ref, payload_ref, back_ref, stat_ref, branch_ref
 ):
-    width = mixed_ref.shape[1]
+    window, width = mixed_ref.shape
     heads = width // HEAD
     pieces = (pair_own[:CHUNK, :], pair_own[CHUNK:, :], pair_other[:CHUNK, :], pair_other[CHUNK:, :])
     for piece, spot in zip(pieces, place(info[0], info[1])):
         branch_ref[aligned(spot * CHUNK), :] = piece
-    pad_ref[:width, :] = out_w[...]
-    pad_ref[width:, :] = jnp.zeros((pad_ref.shape[0] - width, pad_ref.shape[1]), LOW)
-    d_all = dot_nt(branch_ref[...], pad_ref[...]).astype(LOW).astype(F32)
-    for a in range(d_all.shape[0] // CHUNK):
+    d_all = dot_nt(branch_ref[...], out_w[...]).astype(LOW)
+    back_ref[...] = d_all
+    pack_lanes(d_all, payload_ref)
+    first = window + window // 2
+    for a in range(window // CHUNK):
         rows = slice(a * CHUNK, (a + 1) * CHUNK)
-        d_mixed = d_all[rows, :]
-        product = d_mixed[:, :width] * mixed_ref[rows, :]
+        product = d_all[rows, :].astype(F32) * mixed_ref[rows, :]
         deltas = [jnp.sum(keep_head(product, h), axis=-1, keepdims=True) for h in range(heads)]
         stat = pack_columns(deltas, heads, lse_ref[rows, :])
         stat_ref[rows, :] = stat
-        high = stat.astype(LOW).astype(F32)
-        rest = stat - high
-        lane = lax.broadcasted_iota(jnp.int32, (CHUNK, CHUNK), 1)
-        skip = width % CHUNK
-        high = pltpu.roll(high, skip, 1)
-        rest = pltpu.roll(rest, skip + 2 * heads, 1)
-        tail = jnp.where(lane < skip, d_mixed[:, width - skip : width - skip + CHUNK], high)
-        tail = jnp.where(lane >= skip + 2 * heads, rest, tail)
-        tail = jnp.where(lane >= skip + 4 * heads, 0.0, tail)
-        payload_ref[rows, : width - skip] = d_mixed[:, : width - skip].astype(LOW)
-        payload_ref[rows, width - skip :] = tail.astype(LOW)
-    grad_ref[...] = dot_tn(mixed_low[...], branch_ref[...]).astype(LOW)
+        turned = stat.T[: 2 * heads, :]
+        high = turned.astype(LOW).astype(F32)
+        blank = jnp.zeros((EXTRA - 4 * heads, CHUNK), F32)
+        block = jnp.concatenate([high, turned - high, blank], axis=0)
+        payload_ref[first + a * EXTRA : first + (a + 1) * EXTRA, :] = block.astype(LOW)
 
 
 def recall_kernel(
@@ -614,7 +632,7 @@
     q_ref,
     k_ref,
     v_ref,
-    payload_ref,
+    back_ref,
     stat_ref,
     dq_ref,
     dk_ref,
@@ -627,7 +645,7 @@
     window, width = q_ref.shape
     heads = width // HEAD
     queries, keys, values = q_ref[...], k_ref[...], v_ref[...]
-    back = payload_ref[:, :width]
+    back = back_ref[...]
     stat = stat_ref[...].T
     for h in range(heads):
         products_ref[h] = dot_nt(keep_head(values, h), back)
@@ -647,15 +665,29 @@
 
 
 def far_back_kernel(
-    info, far_ref, kp_ref, vp_ref, payload_ref, stat_ref, dq_in, dq_ref, fold_ref, products_ref, ds_ref
+    info,
+    far_ref,
+    kp_ref,
+    vp_ref,
+    back_ref,
+    stat_ref,
+    dq_in,
+    mixed_low,
+    branch_ref,
+    dq_ref,
+    fold_ref,
+    grad_ref,
+    products_ref,
+    ds_ref,
 ):
+    grad_ref[...] = dot_tn(mixed_low[...], branch_ref[...]).astype(LOW)
     width = kp_ref.shape[1]
     heads = width // HEAD
 
     @pl.when(info[3] == 1)
     def _():
         keys, values = kp_ref[...], vp_ref[...]
-        back = payload_ref[:, :width]
+        back = back_ref[...]
         for h in range(heads):
             products_ref[h] = dot_nt(keep_head(back, h), values)
         for h in range(heads):
@@ -717,13 +749,14 @@
     def _():
         payload = jnp.where(info[6] == 1, from_even[...], from_odd[...])
         queries, values = qp_ref[...], v_ref[...]
-        back = payload[:, :width]
-        columns = payload[:, payload.shape[1] - CHUNK :].astype(F32).T
-        skip = width % CHUNK
+        back = unpack_lanes(payload, window)
+        at = window + window // 2
+        blocks = [payload[at + a * EXTRA : at + (a + 1) * EXTRA, :] for a in range(window // CHUNK)]
+        columns = jnp.concatenate(blocks, axis=1).astype(F32)
         for h in range(heads):
             products_ref[h] = dot_nt(keep_head(values, h), back)
         for h in range(heads):
-            at = skip + h
+            at = h
             lse = columns[at : at + 1, :] + columns[at + 2 * heads : at + 2 * heads + 1, :]
             at = at + heads
             delta = columns[at : at + 1, :] + columns[at + 2 * heads : at + 2 * heads + 1, :]
@@ -1074,9 +1107,9 @@
         micros=5.0,
     )
     near_pieces = (near, near_across, near_core, swap(after(near_across, acc), "mp", 1))
-    mixed_low, mixed, lse, queries_near, keys_near, values_near = call(
+    mixed_low, packed, mixed, lse, queries_near, keys_near, values_near = call(
         partner_kernel,
-        [low_rows, wide_rows, stats] + [low_rows] * 3,
+        [low_rows, shape((window + window // 2, CHUNK), LOW), wide_rows, stats] + [low_rows] * 3,
         [info, *near_pieces, gain_one, wq, wk, wv, bias, queries, acc, top, total],
         scratch=[
             pltpu.VMEM((window, d), LOW),
@@ -1088,8 +1121,8 @@
         ],
         micros=300,
     )
-    mixed_across = swap(mixed_low, "mp", 2)
-    mixed_core = swap(mixed_low, "mp", 1)
+    mixed_across = swap(packed, "mp", 2)
+    mixed_core = swap(packed, "mp", 1)
     cot_pieces = (
         cotangent,
         cot_across,
@@ -1117,13 +1150,20 @@
         smem=0,
         micros=1.0,
     )
-    mixed_pieces = (mixed_low, mixed_across, mixed_core, swap(after(mixed_across, bias_t), "mp", 1))
+    (base,) = call(
+        base_kernel,
+        [shape((window, d), F32)],
+        [x_all, after(mixed_low, bias_t), out_weight],
+        smem=0,
+        micros=1.0,
+    )
+    mixed_pieces = (mixed_low, mixed_across, mixed_core, swap(after(mixed_across, bias_t, base), "mp", 1))
     second, hidden, act, d_gate, d_up, second_send, second_keep, gain_two_part = call(
         feed_kernel,
         [shape((window, d), LOW), shape((half, d), F32)]
         + [shape((window, units), LOW)] * 3
         + [shape((half, d), LOW), shape((half, d), F32), shape((1, d), F32)],
-        [info, x_all, *mixed_pieces, *out_pieces, d_act, gain_two, gate_weight, up_weight],
+        [info, base, *mixed_pieces[1:], *out_pieces[1:], d_act, gain_two, gate_weight, up_weight],
         micros=5.0,
     )
     (second_sum,) = call(
@@ -1179,11 +1219,10 @@
         smem=0,
         micros=100,
     )
-    payload, stat_back, out_grad = call(
+    payload, back, stat_back, branch_all = call(
         mixed_back_kernel,
-        [shape((window, 2 * CHUNK), LOW), stats, shape((width, d), LOW)],
-        [info, after(branch_low, feed_cross), swap(branch_low, "mp", 1), out_weight, mixed, mixed_low, lse],
-        scratch=[pltpu.VMEM((window, d), LOW), pltpu.VMEM((2 * CHUNK, d), LOW)],
+        [shape((window + window // 2 + window // CHUNK * EXTRA, CHUNK), LOW), low_rows, stats, shape((window, d), LOW)],
+        [info, after(branch_low, feed_cross), swap(branch_low, "mp", 1), out_weight, mixed, lse],
     )
     payload_even = swap(payload, "dp", 1)
     payload_odd = swap_odd(payload)
@@ -1192,15 +1231,15 @@
     d_queries, d_keys, d_values, near_fold = call(
         own_back_kernel,
         [wide_rows, wide_rows, wide_rows, fold],
-        [own_probs, after(queries, token), keys, values, payload, stat_back],
+        [own_probs, after(queries, token), keys, values, back, stat_back],
         scratch=[square_wide, square_low, square_low],
         smem=0,
         micros=200,
     )
-    d_queries, far_fold = call(
+    d_queries, far_fold, out_grad = call(
         far_back_kernel,
-        [low_rows, fold],
-        [info, far_probs, keys_near, values_near, payload, stat_back, d_queries],
+        [low_rows, fold, shape((width, d), LOW)],
+        [info, far_probs, keys_near, values_near, back, stat_back, d_queries, mixed_low, branch_all],
         scratch=[square_wide, square_low],
         micros=3.0,
     )

time: 158 us -> 154 us (0.975)
  waiting for transfers between devices: 64.3 us -> 61.6 us
  starting transfers between devices: 43.2 us -> 41.4 us
    ppermute x44, waiting for transfers between devices: 64.3 us -> 61.6 us  [swap(): lax.ppermute(values, axis, [(i, i ^ bit) for i in range(lax.axis_size(axi...]
    ppermute x44, starting transfers between devices: 41.6 us -> 39.9 us  [swap(): lax.ppermute(values, axis, [(i, i ^ bit) for i in range(lax.axis_size(axi...]
    pallas_call x31 -> x32, Pallas kernels: 48.5 us -> 48.8 us  [call(): pl.pallas_call(kernel, out_shape=outs, in_specs=[SMEM] * smem + [VMEM] *...]
  transfers between devices with their start and end apart: 46 -> 46, of which waited for: 26 -> 26; matrix products, arithmetic and copies ran while one was open for 1% -> 1% of each run, Pallas kernels for 26% -> 27%
where the time goes in v4:
time: 154 us
  waiting for transfers between devices  61.6 us (40%)
  Pallas kernels  48.8 us (32%)
  starting transfers between devices  41.4 us (27%)
    ppermute x44, waiting for transfers between devices, swap(): lax.ppermute(values, axis, [(i, i ^ bit) for i in range(lax.axis_size(axi...  61.6 us
    pallas_call x32, Pallas kernels, call(): pl.pallas_call(kernel, out_shape=outs, in_specs=[SMEM] * smem + [VMEM] *...  48.8 us
    ppermute x44, starting transfers between devices, swap(): lax.ppermute(values, axis, [(i, i ^ bit) for i in range(lax.axis_size(axi...  39.9 us
  transfers between devices with their start and end apart: 46, of which 26 were waited for; matrix products, arithmetic and copies ran while one was open for 1% of the time, Pallas kernels for 27%

profile of v4, /device:TPU:0, one launch (start us, length us, event | category | flops | bytes accessed | tf_op | source)
XLA Modules:
  0.0 153.7 jit_solution(6319736166447751510)
XLA Ops:
  0.6 3.0 %collective-permute-start = (bf16[128,768]{1,0:T(8,128)(2,1)}, bf16[128,768]{1,0:T(8,128)(2,1)S(1)}, u32[]{:S(2)}, u32[]{:S(2)}) collective-permute-start(bf16[128,768]{1,0:T(8,128)(2,1)} %x_ref.1), channel_id=1, source_target_pairs={{0,2},{1,3},{2,0},{3,1},{4,6},{5,7},{6,4},{7,5},{8,10},{9,11},{10,... | collective-permute-start | bytes 589832 | tf_op jit(solution)/shard_map/ppermute | solution.py:924
  7.3 3.9 %shard_map.229 = (s32[8]{0:T(128)S(1)}, f32[1,512]{1,0:T(1,128)S(1)}, f32[512,128]{1,0:T(8,128)S(1)}, f32[3,128,2048]{2,1,0:T(8,128)S(1)}, f32[3,32]{1,0:T(4,128...) custom-call(s32[2]{0:T(128)S(1)} %pad_add_fusion.spot, s32[16,128]{1,0:T(8,128)S(1)} %add_bitcast_fusion.bucket_ref, ...), custom_call_target="tpu_custom_call" | custom-call | flops 60000000 | tf_op jit(solution)/shard_map/pallas_call | solution.py:37
  17.1 5.0 %shard_map.231 = (bf16[512,768]{1,0:T(8,128)(2,1)S(1)}, bf16[512,768]{1,0:T(8,128)(2,1)S(1)}, bf16[512,192]{1,0:T(8,128)(2,1)S(1)}, bf16[512,192]{1,0:T(8,128)(2...) custom-call(s32[8]{0:T(128)S(1)} %get-tuple-element.150.info, ...), custom_call_target="tpu_custom_call" | custom-call | flops 100000000 | tf_op jit(solution)/shard_map/pallas_call | solution.py:37
  24.4 4.2 %shard_map.232 = (bf16[512,192]{1,0:T(8,128)(2,1)S(1)}, bf16[768,128]{1,0:T(8,128)(2,1)S(1)}, f32[512,192]{1,0:T(8,128)S(1)}, f32[512,128]{1,0:T(8,128)S(1)}, bf...) custom-call(s32[8]{0:T(128)S(1)} %get-tuple-element.150.info, ...), custom_call_target="tpu_custom_call" | custom-call | flops 6000000000 | tf_op jit(solution)/shard_map/pallas_call | solution.py:37
  30.0 2.7 %collective-permute-done.12.o1 = bf16[192,768]{1,0:T(8,128)(2,1)S(1)} collective-permute-done((bf16[192,768]{1,0:T(8,128)(2,1)S(1)}, bf16[192,768]{1,0:T(8,128)(2,1)S(1)}, u32[]{:S(2)}, u32[]{:S(2)}) %collective-permute-start.12) | collective-permute-done | bytes 294944 | tf_op jit(solution)/shard_map/ppermute | solution.py:924
  38.1 4.2 %shard_map.236 = (bf16[512,768]{1,0:T(8,128)(2,1)S(1)}, f32[256,768]{1,0:T(8,128)S(1)}, bf16[512,512]{1,0:T(8,128)(2,1)S(1)}, bf16[512,512]{1,0:T(8,128)(2,1)S(1...) custom-call(s32[8]{0:T(128)S(1)} %get-tuple-element.150.info, ...), custom_call_target="tpu_custom_call" | custom-call | flops 100000000 | tf_op jit(solution)/shard_map/pallas_call | solution.py:37
  47.5 2.3 %collective-permute-start.23 = (bf16[576,512]{1,0:T(8,128)(2,1)S(1)}, bf16[576,512]{1,0:T(8,128)(2,1)S(1)}, u32[]{:S(2)}, u32[]{:S(2)}) collective-permute-start(bf16[576,512]{1,0:T(8,128)(2,1)S(1)} %get-tuple-element.190), channel_id=1, source_target_pairs={{0,4},{4,0},{8,12},{12,8},{16,20},{20,16},{24,28},{28,24},{1,5},{5... | collective-permute-start | bytes 1769480 | tf_op jit(solution)/shard_map/ppermute | solution.py:924
  52.0 2.6 %shard_map.240 = (f32[3,512,512]{2,1,0:T(8,128)S(1)}, f32[3,512,512]{2,1,0:T(8,128)S(1)}, f32[3,512,512]{2,1,0:T(8,128)S(1)}) custom-call(s32[8]{0:T(128)S(1)} %get-tuple-element.150.info, bf16[512,192]{1,0:T(8,128)(2,1)S(1)} %get-tuple-element.214.q_ref, bf16[512,192]{1,0:T(8,128)(2,1)S(1)} %get-tuple-element.194.k_ref, ...), custom_call_target="tpu_custom_call" | custom-call | flops 20000000 | tf_op jit(solution)/shard_map/pallas_call | solution.py:37
  59.0 2.7 %collective-permute-start.21 = (bf16[832,128]{1,0:T(8,128)(2,1)S(1)}, bf16[832,128]{1,0:T(8,128)(2,1)S(1)}, u32[]{:S(2)}, u32[]{:S(2)}) collective-permute-start(bf16[832,128]{1,0:T(8,128)(2,1)S(1)} %get-tuple-element.208), channel_id=1, source_target_pairs={{0,4},{4,0},{8,12},{12,8},{16,20},{20,16},{24,28},{28,24},{1,5},{5... | collective-permute-start | bytes 638984 | tf_op jit(solution)/shard_map/ppermute | solution.py:924
  67.0 2.2 %collective-permute-start.26 = (bf16[288,512]{1,0:T(8,128)(2,1)S(1)}, bf16[288,512]{1,0:T(8,128)(2,1)S(1)}, u32[]{:S(2)}, u32[]{:S(2)}) collective-permute-start(bf16[288,512]{1,0:T(8,128)(2,1)S(1)} %get-tuple-element.233), channel_id=1, source_target_pairs={{0,4},{4,0},{8,12},{12,8},{16,20},{20,16},{24,28},{28,24},{1,5},{5... | collective-permute-start | bytes 884744 | tf_op jit(solution)/shard_map/ppermute | solution.py:924
  69.3 2.5 %shard_map.245 = (f32[512,192]{1,0:T(8,128)S(1)}, f32[512,192]{1,0:T(8,128)S(1)}, f32[512,192]{1,0:T(8,128)S(1)}, f32[3,128,1024]{2,1,0:T(8,128)S(1)}) custom-call(f32[3,512,512]{2,1,0:T(8,128)S(1)} %get-tuple-element.200.own_ref, bf16[512,192]{1,0:T(8,128)(2,1)S(1)} %get-tuple-element.214.q_ref, bf16[512,192]{1,0:T(8,128)(2,1)S(1)} %get-tuple-element.194.k_ref, ...), custom_call_target="tpu_custom_call" | custom-call | flops 4000000000 | tf_op jit(solution)/shard_map/pallas_call | solution.py:37
  73.9 3.8 %shard_map.247 = (bf16[192,768]{1,0:T(8,128)(2,1)S(1)}, bf16[192,768]{1,0:T(8,128)(2,1)S(1)}, bf16[192,768]{1,0:T(8,128)(2,1)S(1)}, bf16[192,768]{1,0:T(8,128)(2...) custom-call(s32[8]{0:T(128)S(1)} %get-tuple-element.150.info, ...), custom_call_target="tpu_custom_call" | custom-call | flops 6000000000 | tf_op jit(solution)/shard_map/pallas_call | solution.py:37
  80.5 2.6 %collective-permute-start.33 = (bf16[288,512]{1,0:T(8,128)(2,1)S(1)}, bf16[288,512]{1,0:T(8,128)(2,1)S(1)}, u32[]{:S(2)}, u32[]{:S(2)}) collective-permute-start(bf16[288,512]{1,0:T(8,128)(2,1)S(1)} %get-tuple-element.258.refs_0_), channel_id=1, source_target_pairs={{0,16},{4,20},{8,24},{12,28},{16,0},{20,4},{24,8},{28,12},{1,17},{... | collective-permute-start | bytes 884744 | tf_op jit(solution)/shard_map/ppermute | solution.py:924
  85.0 6.8 %collective-permute-done.29.refs_3_ = bf16[192,768]{1,0:T(8,128)(2,1)S(1)} collective-permute-done((bf16[192,768]{1,0:T(8,128)(2,1)S(1)}, bf16[192,768]{1,0:T(8,128)(2,1)S(1)}, u32[]{:S(2)}, u32[]{:S(2)}) %collective-permute-start.29) | collective-permute-done | bytes 294944 | tf_op jit(solution)/shard_map/ppermute | solution.py:924
  94.4 2.5 %shard_map.251.table_ref = f32[3,128]{1,0:T(4,128)S(1)} custom-call(s32[8]{0:T(128)S(1)} %get-tuple-element.150.info, f32[3,128,1024]{2,1,0:T(8,128)S(1)} %get-tuple-element.250.near_fold, f32[3,128,1024]{2,1,0:T(8,128)S(1)} %get-tuple-element.251.far_fold, s32[16,128]{1,0:T(8,128)S(1)} %get-tuple-element.252.flipped_ref, ...), custom_call_target="tpu_custom_call" | custom-call | flops 20000000 | tf_op jit(solution)/shard_map/pallas_call | solution.py:37
  97.9 3.2 %collective-permute-done.31.refs_1_ = bf16[96,768]{1,0:T(8,128)(2,1)S(1)} collective-permute-done((bf16[96,768]{1,0:T(8,128)(2,1)S(1)}, bf16[96,768]{1,0:T(8,128)(2,1)S(1)}, u32[]{:S(2)}, u32[]{:S(2)}) %collective-permute-start.31) | collective-permute-done | bytes 147488 | tf_op jit(solution)/shard_map/ppermute | solution.py:924
  101.1 3.4 %collective-permute-start.35 = (bf16[112,768]{1,0:T(8,128)(2,1)S(1)}, bf16[112,768]{1,0:T(8,128)(2,1)S(1)}, u32[]{:S(2)}, u32[]{:S(2)}) collective-permute-start(bf16[112,768]{1,0:T(8,128)(2,1)S(1)} %get-tuple-element.261.refs_0_), channel_id=1, source_target_pairs={{0,16},{4,20},{8,24},{12,28},{16,0},{20,4},{24,8},{28,12},{1,17},{... | collective-permute-start | bytes 516104 | tf_op jit(solution)/shard_map/ppermute | solution.py:924
  104.6 12.5 %collective-permute-done.34.refs_3_ = bf16[288,512]{1,0:T(8,128)(2,1)S(1)} collective-permute-done((bf16[288,512]{1,0:T(8,128)(2,1)S(1)}, bf16[288,512]{1,0:T(8,128)(2,1)S(1)}, u32[]{:S(2)}, u32[]{:S(2)}) %collective-permute-start.34) | collective-permute-done | bytes 294944 | tf_op jit(solution)/shard_map/ppermute | solution.py:924
  118.2 4.5 %collective-permute-done.36.refs_3_ = bf16[96,768]{1,0:T(8,128)(2,1)S(1)} collective-permute-done((bf16[96,768]{1,0:T(8,128)(2,1)S(1)}, bf16[96,768]{1,0:T(8,128)(2,1)S(1)}, u32[]{:S(2)}, u32[]{:S(2)}) %collective-permute-start.36) | collective-permute-done | bytes 147488 | tf_op jit(solution)/shard_map/ppermute | solution.py:924
  123.3 5.6 %collective-permute-done.37.refs_1_ = bf16[288,512]{1,0:T(8,128)(2,1)S(1)} collective-permute-done((bf16[288,512]{1,0:T(8,128)(2,1)S(1)}, bf16[288,512]{1,0:T(8,128)(2,1)S(1)}, u32[]{:S(2)}, u32[]{:S(2)}) %collective-permute-start.37) | collective-permute-done | bytes 294944 | tf_op jit(solution)/shard_map/ppermute | solution.py:924
  130.1 2.6 %collective-permute-done.39.refs_1_ = bf16[112,768]{1,0:T(8,128)(2,1)S(1)} collective-permute-done((bf16[112,768]{1,0:T(8,128)(2,1)S(1)}, bf16[112,768]{1,0:T(8,128)(2,1)S(1)}, u32[]{:S(2)}, u32[]{:S(2)}) %collective-permute-start.39) | collective-permute-done | bytes 172064 | tf_op jit(solution)/shard_map/ppermute | solution.py:924
  136.2 4.1 %collective-permute-done.41.got_ref = bf16[128,768]{1,0:T(8,128)(2,1)S(1)} collective-permute-done((bf16[128,768]{1,0:T(8,128)(2,1)S(1)}, bf16[128,768]{1,0:T(8,128)(2,1)S(1)}, u32[]{:S(2)}, u32[]{:S(2)}) %collective-permute-start.41) | collective-permute-done | bytes 196640 | tf_op jit(solution)/shard_map/ppermute | solution.py:924
  141.0 4.9 %collective-permute-done.42.one_got = bf16[576,512]{1,0:T(8,128)(2,1)S(1)} collective-permute-done((bf16[576,512]{1,0:T(8,128)(2,1)S(1)}, bf16[576,512]{1,0:T(8,128)(2,1)S(1)}, u32[]{:S(2)}, u32[]{:S(2)}) %collective-permute-start.42) | collective-permute-done | bytes 589856 | tf_op jit(solution)/shard_map/ppermute | solution.py:924
  146.3 3.1 %shard_map.259 = (f32[768,512]{1,0:T(8,128)}, f32[768,512]{1,0:T(8,128)}, f32[512,768]{1,0:T(8,128)}) custom-call(s32[8]{0:T(128)S(1)} %get-tuple-element.150.info, bf16[576,512]{1,0:T(8,128)(2,1)S(1)} %get-tuple-element.274.one, bf16[576,512]{1,0:T(8,128)(2,1)S(1)} %collective-permute-done.42.one_got, bf16[576,512]{1,0:T(8,128)(2,1)S(1)} %get-tuple-element.275.two, ...), custom_call_target="tpu_custom_call" | custom-call | flops 40000000 | tf_op jit(solution)/shard_map/pallas_call | solution.py:37
  (114 shorter events, 58.0 us)
Async XLA Ops:
  0.6 12.4 %collective-permute-start = (bf16[128,768]{1,0:T(8,128)(2,1)}, bf16[128,768]{1,0:T(8,128)(2,1)S(1)}, u32[]{:S(2)}, u32[]{:S(2)}) collective-permute-start(bf16[128,768]{1,0:T(8,128)(2,1)} %x_ref.1), channel_id=1, source_target_pairs={{0,2},{1,3},{2,0},{3,1},{4,6},{5,7},{6,4},{7,5},{8,10},{9,11},{10,... | collective-permute-start | bytes 589832 | tf_op jit(solution)/shard_map/ppermute | solution.py:924
  3.7 9.9 %collective-permute-start.2 = (bf16[128,768]{1,0:T(8,128)(2,1)}, bf16[128,768]{1,0:T(8,128)(2,1)S(1)}, u32[]{:S(2)}, u32[]{:S(2)}) collective-permute-start(bf16[128,768]{1,0:T(8,128)(2,1)} %x_ref.1), channel_id=1, source_target_pairs={{0,4},{4,0},{8,12},{12,8},{16,20},{20,16},{24,28},{28,24},{1,5},{5... | collective-permute-start | bytes 589832 | tf_op jit(solution)/shard_map/ppermute | solution.py:924
  23.0 9.8 %collective-permute-start.12 = (bf16[192,768]{1,0:T(8,128)(2,1)S(1)}, bf16[192,768]{1,0:T(8,128)(2,1)S(1)}, u32[]{:S(2)}, u32[]{:S(2)}) collective-permute-start(bf16[192,768]{1,0:T(8,128)(2,1)S(1)} %copy-done), channel_id=1, source_target_pairs={{0,2},{1,3},{2,0},{3,1},{4,6},{5,7},{6,4},{7,5},{8,10},{9,11},{10,... | collective-permute-start | bytes 884744 | tf_op jit(solution)/shard_map/ppermute | solution.py:924
  44.1 11.2 %collective-permute-start.18 = (bf16[256,768]{1,0:T(8,128)(2,1)S(1)}, bf16[256,768]{1,0:T(8,128)(2,1)S(1)}, u32[]{:S(2)}, u32[]{:S(2)}) collective-permute-start(bf16[256,768]{1,0:T(8,128)(2,1)S(1)} %shard_map.237.sum_ref), channel_id=1, source_target_pairs={{0,2},{1,3},{2,0},{3,1},{4,6},{5,7},{6,4},{7,5},{8,10},{9,11},{10,... | collective-permute-start | bytes 1179656 | tf_op jit(solution)/shard_map/ppermute | solution.py:924
  47.5 16.1 %collective-permute-start.23 = (bf16[576,512]{1,0:T(8,128)(2,1)S(1)}, bf16[576,512]{1,0:T(8,128)(2,1)S(1)}, u32[]{:S(2)}, u32[]{:S(2)}) collective-permute-start(bf16[576,512]{1,0:T(8,128)(2,1)S(1)} %get-tuple-element.190), channel_id=1, source_target_pairs={{0,4},{4,0},{8,12},{12,8},{16,20},{20,16},{24,28},{28,24},{1,5},{5... | collective-permute-start | bytes 1769480 | tf_op jit(solution)/shard_map/ppermute | solution.py:924
  49.8 14.8 %collective-permute-start.24 = (bf16[576,512]{1,0:T(8,128)(2,1)S(1)}, bf16[576,512]{1,0:T(8,128)(2,1)S(1)}, u32[]{:S(2)}, u32[]{:S(2)}) collective-permute-start(bf16[576,512]{1,0:T(8,128)(2,1)S(1)} %get-tuple-element.212), channel_id=1, source_target_pairs={{0,8},{4,12},{8,0},{12,4},{16,24},{20,28},{24,16},{28,20},{1,9},{5... | collective-permute-start | bytes 1769480 | tf_op jit(solution)/shard_map/ppermute | solution.py:924
  59.0 14.9 %collective-permute-start.21 = (bf16[832,128]{1,0:T(8,128)(2,1)S(1)}, bf16[832,128]{1,0:T(8,128)(2,1)S(1)}, u32[]{:S(2)}, u32[]{:S(2)}) collective-permute-start(bf16[832,128]{1,0:T(8,128)(2,1)S(1)} %get-tuple-element.208), channel_id=1, source_target_pairs={{0,4},{4,0},{8,12},{12,8},{16,20},{20,16},{24,28},{28,24},{1,5},{5... | collective-permute-start | bytes 638984 | tf_op jit(solution)/shard_map/ppermute | solution.py:924
  61.6 12.3 %collective-permute-start.22 = (bf16[832,128]{1,0:T(8,128)(2,1)S(1)}, bf16[832,128]{1,0:T(8,128)(2,1)S(1)}, u32[]{:S(2)}, u32[]{:S(2)}) collective-permute-start(bf16[832,128]{1,0:T(8,128)(2,1)S(1)} %get-tuple-element.208), channel_id=1, source_target_pairs={{4,8},{12,16},{20,24},{8,4},{16,12},{24,20},{5,9},{13,17},{21,25},... | collective-permute-start | bytes 638984 | tf_op jit(solution)/shard_map/ppermute | solution.py:929
  65.4 12.9 %collective-permute-start.25 = (bf16[288,512]{1,0:T(8,128)(2,1)S(1)}, bf16[288,512]{1,0:T(8,128)(2,1)S(1)}, u32[]{:S(2)}, u32[]{:S(2)}) collective-permute-start(bf16[288,512]{1,0:T(8,128)(2,1)S(1)} %get-tuple-element.213), channel_id=1, source_target_pairs={{0,8},{4,12},{8,0},{12,4},{16,24},{20,28},{24,16},{28,20},{1,9},{5... | collective-permute-start | bytes 884744 | tf_op jit(solution)/shard_map/ppermute | solution.py:924
  67.0 11.3 %collective-permute-start.26 = (bf16[288,512]{1,0:T(8,128)(2,1)S(1)}, bf16[288,512]{1,0:T(8,128)(2,1)S(1)}, u32[]{:S(2)}, u32[]{:S(2)}) collective-permute-start(bf16[288,512]{1,0:T(8,128)(2,1)S(1)} %get-tuple-element.233), channel_id=1, source_target_pairs={{0,4},{4,0},{8,12},{12,8},{16,20},{20,16},{24,28},{28,24},{1,5},{5... | collective-permute-start | bytes 884744 | tf_op jit(solution)/shard_map/ppermute | solution.py:924
  77.8 14.0 %collective-permute-start.29 = (bf16[192,768]{1,0:T(8,128)(2,1)S(1)}, bf16[192,768]{1,0:T(8,128)(2,1)S(1)}, u32[]{:S(2)}, u32[]{:S(2)}) collective-permute-start(bf16[192,768]{1,0:T(8,128)(2,1)S(1)} %get-tuple-element.242), channel_id=1, source_target_pairs={{0,8},{4,12},{8,0},{12,4},{16,24},{20,28},{24,16},{28,20},{1,9},{5... | collective-permute-start | bytes 884744 | tf_op jit(solution)/shard_map/ppermute | solution.py:924
  78.5 13.3 %collective-permute-start.28 = (bf16[192,768]{1,0:T(8,128)(2,1)S(1)}, bf16[192,768]{1,0:T(8,128)(2,1)S(1)}, u32[]{:S(2)}, u32[]{:S(2)}) collective-permute-start(bf16[192,768]{1,0:T(8,128)(2,1)S(1)} %get-tuple-element.240), channel_id=1, source_target_pairs={{0,4},{4,0},{8,12},{12,8},{16,20},{20,16},{24,28},{28,24},{1,5},{5... | collective-permute-start | bytes 884744 | tf_op jit(solution)/shard_map/ppermute | solution.py:924
  80.5 24.1 %collective-permute-start.33 = (bf16[288,512]{1,0:T(8,128)(2,1)S(1)}, bf16[288,512]{1,0:T(8,128)(2,1)S(1)}, u32[]{:S(2)}, u32[]{:S(2)}) collective-permute-start(bf16[288,512]{1,0:T(8,128)(2,1)S(1)} %get-tuple-element.258.refs_0_), channel_id=1, source_target_pairs={{0,16},{4,20},{8,24},{12,28},{16,0},{20,4},{24,8},{28,12},{1,17},{... | collective-permute-start | bytes 884744 | tf_op jit(solution)/shard_map/ppermute | solution.py:924
  83.1 34.1 %collective-permute-start.34 = (bf16[288,512]{1,0:T(8,128)(2,1)S(1)}, bf16[288,512]{1,0:T(8,128)(2,1)S(1)}, u32[]{:S(2)}, u32[]{:S(2)}) collective-permute-start(bf16[288,512]{1,0:T(8,128)(2,1)S(1)} %get-tuple-element.259.refs_2_), channel_id=1, source_target_pairs={{0,16},{4,20},{8,24},{12,28},{16,0},{20,4},{24,8},{28,12},{1,17},{... | collective-permute-start | bytes 884744 | tf_op jit(solution)/shard_map/ppermute | solution.py:924
  83.5 13.4 %collective-permute-start.30 = (bf16[144,768]{1,0:T(8,128)(2,1)S(1)}, bf16[144,768]{1,0:T(8,128)(2,1)S(1)}, u32[]{:S(2)}, u32[]{:S(2)}) collective-permute-start(bf16[144,768]{1,0:T(8,128)(2,1)S(1)} %get-tuple-element.238), channel_id=1, source_target_pairs={{0,2},{1,3},{2,0},{3,1},{4,6},{5,7},{6,4},{7,5},{8,10},{9,11},{10,... | collective-permute-start | bytes 663560 | tf_op jit(solution)/shard_map/ppermute | solution.py:924
  101.1 21.5 %collective-permute-start.35 = (bf16[112,768]{1,0:T(8,128)(2,1)S(1)}, bf16[112,768]{1,0:T(8,128)(2,1)S(1)}, u32[]{:S(2)}, u32[]{:S(2)}) collective-permute-start(bf16[112,768]{1,0:T(8,128)(2,1)S(1)} %get-tuple-element.261.refs_0_), channel_id=1, source_target_pairs={{0,16},{4,20},{8,24},{12,28},{16,0},{20,4},{24,8},{28,12},{1,17},{... | collective-permute-start | bytes 516104 | tf_op jit(solution)/shard_map/ppermute | solution.py:924
  104.5 18.1 %collective-permute-start.36 = (bf16[96,768]{1,0:T(8,128)(2,1)S(1)}, bf16[96,768]{1,0:T(8,128)(2,1)S(1)}, u32[]{:S(2)}, u32[]{:S(2)}) collective-permute-start(bf16[96,768]{1,0:T(8,128)(2,1)S(1)} %get-tuple-element.262.refs_2_), channel_id=1, source_target_pairs={{0,16},{4,20},{8,24},{12,28},{16,0},{20,4},{24,8},{28,12},{1,17},{... | collective-permute-start | bytes 442376 | tf_op jit(solution)/shard_map/ppermute | solution.py:924
  117.3 11.7 %collective-permute-start.37 = (bf16[288,512]{1,0:T(8,128)(2,1)S(1)}, bf16[288,512]{1,0:T(8,128)(2,1)S(1)}, u32[]{:S(2)}, u32[]{:S(2)}) collective-permute-start(bf16[288,512]{1,0:T(8,128)(2,1)S(1)} %get-tuple-element.264.refs_0_), channel_id=1, source_target_pairs={{0,8},{4,12},{8,0},{12,4},{16,24},{20,28},{24,16},{28,20},{1,9},{5... | collective-permute-start | bytes 884744 | tf_op jit(solution)/shard_map/ppermute | solution.py:924
  117.4 11.6 %collective-permute-start.38 = (bf16[288,512]{1,0:T(8,128)(2,1)S(1)}, bf16[288,512]{1,0:T(8,128)(2,1)S(1)}, u32[]{:S(2)}, u32[]{:S(2)}) collective-permute-start(bf16[288,512]{1,0:T(8,128)(2,1)S(1)} %get-tuple-element.265.refs_2_), channel_id=1, source_target_pairs={{0,4},{4,0},{8,12},{12,8},{16,20},{20,16},{24,28},{28,24},{1,5},{5... | collective-permute-start | bytes 884744 | tf_op jit(solution)/shard_map/ppermute | solution.py:924
  122.7 9.9 %collective-permute-start.39 = (bf16[112,768]{1,0:T(8,128)(2,1)S(1)}, bf16[112,768]{1,0:T(8,128)(2,1)S(1)}, u32[]{:S(2)}, u32[]{:S(2)}) collective-permute-start(bf16[112,768]{1,0:T(8,128)(2,1)S(1)} %get-tuple-element.267.refs_0_), channel_id=1, source_target_pairs={{0,8},{4,12},{8,0},{12,4},{16,24},{20,28},{24,16},{28,20},{1,9},{5... | collective-permute-start | bytes 516104 | tf_op jit(solution)/shard_map/ppermute | solution.py:924
  129.6 16.3 %collective-permute-start.42 = (bf16[576,512]{1,0:T(8,128)(2,1)S(1)}, bf16[576,512]{1,0:T(8,128)(2,1)S(1)}, u32[]{:S(2)}, u32[]{:S(2)}) collective-permute-start(bf16[576,512]{1,0:T(8,128)(2,1)S(1)} %get-tuple-element.274.one), channel_id=1, source_target_pairs={{0,4},{4,0},{8,12},{12,8},{16,20},{20,16},{24,28},{28,24},{1,5},{5... | collective-permute-start | bytes 1769480 | tf_op jit(solution)/shard_map/ppermute | solution.py:924
  130.1 16.3 %collective-permute-start.43 = (bf16[576,512]{1,0:T(8,128)(2,1)S(1)}, bf16[576,512]{1,0:T(8,128)(2,1)S(1)}, u32[]{:S(2)}, u32[]{:S(2)}) collective-permute-start(bf16[576,512]{1,0:T(8,128)(2,1)S(1)} %get-tuple-element.275.two), channel_id=1, source_target_pairs={{0,8},{4,12},{8,0},{12,4},{16,24},{20,28},{24,16},{28,20},{1,9},{5... | collective-permute-start | bytes 1769480 | tf_op jit(solution)/shard_map/ppermute | solution.py:924
  133.2 18.4 %collective-permute-start.44 = (bf16[208,768]{1,0:T(8,128)(2,1)S(1)}, bf16[208,768]{1,0:T(8,128)(2,1)S(1)}, u32[]{:S(2)}, u32[]{:S(2)}) collective-permute-start(bf16[208,768]{1,0:T(8,128)(2,1)S(1)} %get-tuple-element.277.one), channel_id=1, source_target_pairs={{0,4},{4,0},{8,12},{12,8},{16,20},{20,16},{24,28},{28,24},{1,5},{5... | collective-permute-start | bytes 958472 | tf_op jit(solution)/shard_map/ppermute | solution.py:924
  133.6 17.9 %collective-permute-start.45 = (bf16[192,768]{1,0:T(8,128)(2,1)S(1)}, bf16[192,768]{1,0:T(8,128)(2,1)S(1)}, u32[]{:S(2)}, u32[]{:S(2)}) collective-permute-start(bf16[192,768]{1,0:T(8,128)(2,1)S(1)} %get-tuple-element.278.two), channel_id=1, source_target_pairs={{0,8},{4,12},{8,0},{12,4},{16,24},{20,28},{24,16},{28,20},{1,9},{5... | collective-permute-start | bytes 884744 | tf_op jit(solution)/shard_map/ppermute | solution.py:924
  (28 other events, 132.7 us)

commit v5 on v4

--- a/solution.py
+++ b/solution.py
@@ -1089,7 +1089,7 @@
     (near,) = call(near_kernel, [shape((local, d), LOW)], [info, after(from_even, x_across, cot_across), from_odd], micros=0.5)
     near_across = swap(near, "mp", 2)
     near_core = swap(near, "mp", 1)
-    x_pieces = (inputs, x_across, swap(inputs, "mp", 1), swap(after(x_across, near_core), "mp", 1))
+    x_pieces = (inputs, x_across, swap(inputs, "mp", 1), swap(after(x_across, bias), "mp", 1))
 
     low_rows = shape((window, width), LOW)
     wide_rows = shape((window, width), F32)

time: 154 us -> 153 us (level)
  starting transfers between devices: 41.4 us -> 39.1 us
    ppermute x44, starting transfers between devices: 39.9 us -> 37.5 us  [swap(): lax.ppermute(values, axis, [(i, i ^ bit) for i in range(lax.axis_size(axi...]
  transfers between devices with their start and end apart: 46 -> 46, of which waited for: 26 -> 24; matrix products, arithmetic and copies ran while one was open for 1% -> 1% of each run, Pallas kernels for 27% -> 28%
where the time goes in v5:
time: 153 us; the launch traced here: 152 us
  waiting for transfers between devices  62.7 us (41%)
  Pallas kernels  48.8 us (32%)
  starting transfers between devices  39.1 us (26%)
    ppermute x44, waiting for transfers between devices, swap(): lax.ppermute(values, axis, [(i, i ^ bit) for i in range(lax.axis_size(axi...  62.7 us
    pallas_call x32, Pallas kernels, call(): pl.pallas_call(kernel, out_shape=outs, in_specs=[SMEM] * smem + [VMEM] *...  48.8 us
    ppermute x44, starting transfers between devices, swap(): lax.ppermute(values, axis, [(i, i ^ bit) for i in range(lax.axis_size(axi...  37.5 us
  transfers between devices with their start and end apart: 46, of which 24 were waited for; matrix products, arithmetic and copies ran while one was open for 1% of the time, Pallas kernels for 28%

profile of v5, /device:TPU:0, one launch (start us, length us, event | category | flops | bytes accessed | tf_op | source)
XLA Modules:
  0.0 152.4 jit_solution(12722581971322127379)
XLA Ops:
  0.6 3.0 %collective-permute-start = (bf16[128,768]{1,0:T(8,128)(2,1)}, bf16[128,768]{1,0:T(8,128)(2,1)S(1)}, u32[]{:S(2)}, u32[]{:S(2)}) collective-permute-start(bf16[128,768]{1,0:T(8,128)(2,1)} %x_ref.1), channel_id=1, source_target_pairs={{0,2},{1,3},{2,0},{3,1},{4,6},{5,7},{6,4},{7,5},{8,10},{9,11},{10,... | collective-permute-start | bytes 589832 | tf_op jit(solution)/shard_map/ppermute | solution.py:924
  7.3 3.9 %shard_map.229 = (s32[8]{0:T(128)S(1)}, f32[1,512]{1,0:T(1,128)S(1)}, f32[512,128]{1,0:T(8,128)S(1)}, f32[3,128,2048]{2,1,0:T(8,128)S(1)}, f32[3,32]{1,0:T(4,128...) custom-call(s32[2]{0:T(128)S(1)} %pad_add_fusion.spot, s32[16,128]{1,0:T(8,128)S(1)} %add_bitcast_fusion.bucket_ref, ...), custom_call_target="tpu_custom_call" | custom-call | flops 60000000 | tf_op jit(solution)/shard_map/pallas_call | solution.py:37
  15.7 5.0 %shard_map.230 = (bf16[512,768]{1,0:T(8,128)(2,1)S(1)}, bf16[512,768]{1,0:T(8,128)(2,1)S(1)}, bf16[512,192]{1,0:T(8,128)(2,1)S(1)}, bf16[512,192]{1,0:T(8,128)(2...) custom-call(s32[8]{0:T(128)S(1)} %get-tuple-element.150.info, ...), custom_call_target="tpu_custom_call" | custom-call | flops 100000000 | tf_op jit(solution)/shard_map/pallas_call | solution.py:37
  23.0 4.2 %shard_map.232 = (bf16[512,192]{1,0:T(8,128)(2,1)S(1)}, bf16[768,128]{1,0:T(8,128)(2,1)S(1)}, f32[512,192]{1,0:T(8,128)S(1)}, f32[512,128]{1,0:T(8,128)S(1)}, bf...) custom-call(s32[8]{0:T(128)S(1)} %get-tuple-element.150.info, ...), custom_call_target="tpu_custom_call" | custom-call | flops 6000000000 | tf_op jit(solution)/shard_map/pallas_call | solution.py:37
  28.5 2.9 %collective-permute-done.12.o1 = bf16[192,768]{1,0:T(8,128)(2,1)S(1)} collective-permute-done((bf16[192,768]{1,0:T(8,128)(2,1)S(1)}, bf16[192,768]{1,0:T(8,128)(2,1)S(1)}, u32[]{:S(2)}, u32[]{:S(2)}) %collective-permute-start.12) | collective-permute-done | bytes 294944 | tf_op jit(solution)/shard_map/ppermute | solution.py:924
  36.7 4.2 %shard_map.236 = (bf16[512,768]{1,0:T(8,128)(2,1)S(1)}, f32[256,768]{1,0:T(8,128)S(1)}, bf16[512,512]{1,0:T(8,128)(2,1)S(1)}, bf16[512,512]{1,0:T(8,128)(2,1)S(1...) custom-call(s32[8]{0:T(128)S(1)} %get-tuple-element.150.info, ...), custom_call_target="tpu_custom_call" | custom-call | flops 100000000 | tf_op jit(solution)/shard_map/pallas_call | solution.py:37
  45.7 2.7 %collective-permute-start.23 = (bf16[576,512]{1,0:T(8,128)(2,1)S(1)}, bf16[576,512]{1,0:T(8,128)(2,1)S(1)}, u32[]{:S(2)}, u32[]{:S(2)}) collective-permute-start(bf16[576,512]{1,0:T(8,128)(2,1)S(1)} %get-tuple-element.190), channel_id=1, source_target_pairs={{0,4},{4,0},{8,12},{12,8},{16,20},{20,16},{24,28},{28,24},{1,5},{5... | collective-permute-start | bytes 1769480 | tf_op jit(solution)/shard_map/ppermute | solution.py:924
  50.6 2.6 %shard_map.240 = (f32[3,512,512]{2,1,0:T(8,128)S(1)}, f32[3,512,512]{2,1,0:T(8,128)S(1)}, f32[3,512,512]{2,1,0:T(8,128)S(1)}) custom-call(s32[8]{0:T(128)S(1)} %get-tuple-element.150.info, bf16[512,192]{1,0:T(8,128)(2,1)S(1)} %get-tuple-element.214.q_ref, bf16[512,192]{1,0:T(8,128)(2,1)S(1)} %get-tuple-element.194.k_ref, ...), custom_call_target="tpu_custom_call" | custom-call | flops 20000000 | tf_op jit(solution)/shard_map/pallas_call | solution.py:37
  57.6 2.5 %collective-permute-start.21 = (bf16[832,128]{1,0:T(8,128)(2,1)S(1)}, bf16[832,128]{1,0:T(8,128)(2,1)S(1)}, u32[]{:S(2)}, u32[]{:S(2)}) collective-permute-start(bf16[832,128]{1,0:T(8,128)(2,1)S(1)} %get-tuple-element.208), channel_id=1, source_target_pairs={{0,4},{4,0},{8,12},{12,8},{16,20},{20,16},{24,28},{28,24},{1,5},{5... | collective-permute-start | bytes 638984 | tf_op jit(solution)/shard_map/ppermute | solution.py:924
  67.8 2.5 %shard_map.245 = (f32[512,192]{1,0:T(8,128)S(1)}, f32[512,192]{1,0:T(8,128)S(1)}, f32[512,192]{1,0:T(8,128)S(1)}, f32[3,128,1024]{2,1,0:T(8,128)S(1)}) custom-call(f32[3,512,512]{2,1,0:T(8,128)S(1)} %get-tuple-element.200.own_ref, bf16[512,192]{1,0:T(8,128)(2,1)S(1)} %get-tuple-element.214.q_ref, bf16[512,192]{1,0:T(8,128)(2,1)S(1)} %get-tuple-element.194.k_ref, ...), custom_call_target="tpu_custom_call" | custom-call | flops 4000000000 | tf_op jit(solution)/shard_map/pallas_call | solution.py:37
  72.4 3.8 %shard_map.247 = (bf16[192,768]{1,0:T(8,128)(2,1)S(1)}, bf16[192,768]{1,0:T(8,128)(2,1)S(1)}, bf16[192,768]{1,0:T(8,128)(2,1)S(1)}, bf16[192,768]{1,0:T(8,128)(2...) custom-call(s32[8]{0:T(128)S(1)} %get-tuple-element.150.info, ...), custom_call_target="tpu_custom_call" | custom-call | flops 6000000000 | tf_op jit(solution)/shard_map/pallas_call | solution.py:37
  76.6 2.5 %collective-permute-start.28 = (bf16[192,768]{1,0:T(8,128)(2,1)S(1)}, bf16[192,768]{1,0:T(8,128)(2,1)S(1)}, u32[]{:S(2)}, u32[]{:S(2)}) collective-permute-start(bf16[192,768]{1,0:T(8,128)(2,1)S(1)} %get-tuple-element.240), channel_id=1, source_target_pairs={{0,4},{4,0},{8,12},{12,8},{16,20},{20,16},{24,28},{28,24},{1,5},{5... | collective-permute-start | bytes 884744 | tf_op jit(solution)/shard_map/ppermute | solution.py:924
  79.1 2.6 %collective-permute-start.33 = (bf16[288,512]{1,0:T(8,128)(2,1)S(1)}, bf16[288,512]{1,0:T(8,128)(2,1)S(1)}, u32[]{:S(2)}, u32[]{:S(2)}) collective-permute-start(bf16[288,512]{1,0:T(8,128)(2,1)S(1)} %get-tuple-element.258.refs_0_), channel_id=1, source_target_pairs={{0,16},{4,20},{8,24},{12,28},{16,0},{20,4},{24,8},{28,12},{1,17},{... | collective-permute-start | bytes 884744 | tf_op jit(solution)/shard_map/ppermute | solution.py:924
  83.3 7.0 %collective-permute-done.29.refs_3_ = bf16[192,768]{1,0:T(8,128)(2,1)S(1)} collective-permute-done((bf16[192,768]{1,0:T(8,128)(2,1)S(1)}, bf16[192,768]{1,0:T(8,128)(2,1)S(1)}, u32[]{:S(2)}, u32[]{:S(2)}) %collective-permute-start.29) | collective-permute-done | bytes 294944 | tf_op jit(solution)/shard_map/ppermute | solution.py:924
  91.8 2.5 %shard_map.251.table_ref = f32[3,128]{1,0:T(4,128)S(1)} custom-call(s32[8]{0:T(128)S(1)} %get-tuple-element.150.info, f32[3,128,1024]{2,1,0:T(8,128)S(1)} %get-tuple-element.250.near_fold, f32[3,128,1024]{2,1,0:T(8,128)S(1)} %get-tuple-element.251.far_fold, s32[16,128]{1,0:T(8,128)S(1)} %get-tuple-element.252.flipped_ref, ...), custom_call_target="tpu_custom_call" | custom-call | flops 20000000 | tf_op jit(solution)/shard_map/pallas_call | solution.py:37
  95.3 4.1 %collective-permute-done.31.refs_1_ = bf16[96,768]{1,0:T(8,128)(2,1)S(1)} collective-permute-done((bf16[96,768]{1,0:T(8,128)(2,1)S(1)}, bf16[96,768]{1,0:T(8,128)(2,1)S(1)}, u32[]{:S(2)}, u32[]{:S(2)}) %collective-permute-start.31) | collective-permute-done | bytes 147488 | tf_op jit(solution)/shard_map/ppermute | solution.py:924
  99.4 4.0 %collective-permute-start.35 = (bf16[112,768]{1,0:T(8,128)(2,1)S(1)}, bf16[112,768]{1,0:T(8,128)(2,1)S(1)}, u32[]{:S(2)}, u32[]{:S(2)}) collective-permute-start(bf16[112,768]{1,0:T(8,128)(2,1)S(1)} %get-tuple-element.261.refs_0_), channel_id=1, source_target_pairs={{0,16},{4,20},{8,24},{12,28},{16,0},{20,4},{24,8},{28,12},{1,17},{... | collective-permute-start | bytes 516104 | tf_op jit(solution)/shard_map/ppermute | solution.py:924
  103.5 12.3 %collective-permute-done.34.refs_3_ = bf16[288,512]{1,0:T(8,128)(2,1)S(1)} collective-permute-done((bf16[288,512]{1,0:T(8,128)(2,1)S(1)}, bf16[288,512]{1,0:T(8,128)(2,1)S(1)}, u32[]{:S(2)}, u32[]{:S(2)}) %collective-permute-start.34) | collective-permute-done | bytes 294944 | tf_op jit(solution)/shard_map/ppermute | solution.py:924
  117.1 4.3 %collective-permute-done.36.refs_3_ = bf16[96,768]{1,0:T(8,128)(2,1)S(1)} collective-permute-done((bf16[96,768]{1,0:T(8,128)(2,1)S(1)}, bf16[96,768]{1,0:T(8,128)(2,1)S(1)}, u32[]{:S(2)}, u32[]{:S(2)}) %collective-permute-start.36) | collective-permute-done | bytes 147488 | tf_op jit(solution)/shard_map/ppermute | solution.py:924
  122.1 5.6 %collective-permute-done.37.refs_1_ = bf16[288,512]{1,0:T(8,128)(2,1)S(1)} collective-permute-done((bf16[288,512]{1,0:T(8,128)(2,1)S(1)}, bf16[288,512]{1,0:T(8,128)(2,1)S(1)}, u32[]{:S(2)}, u32[]{:S(2)}) %collective-permute-start.37) | collective-permute-done | bytes 294944 | tf_op jit(solution)/shard_map/ppermute | solution.py:924
  128.9 2.5 %collective-permute-done.39.refs_1_ = bf16[112,768]{1,0:T(8,128)(2,1)S(1)} collective-permute-done((bf16[112,768]{1,0:T(8,128)(2,1)S(1)}, bf16[112,768]{1,0:T(8,128)(2,1)S(1)}, u32[]{:S(2)}, u32[]{:S(2)}) %collective-permute-start.39) | collective-permute-done | bytes 172064 | tf_op jit(solution)/shard_map/ppermute | solution.py:924
  134.5 4.5 %collective-permute-done.41.got_ref = bf16[128,768]{1,0:T(8,128)(2,1)S(1)} collective-permute-done((bf16[128,768]{1,0:T(8,128)(2,1)S(1)}, bf16[128,768]{1,0:T(8,128)(2,1)S(1)}, u32[]{:S(2)}, u32[]{:S(2)}) %collective-permute-start.41) | collective-permute-done | bytes 196640 | tf_op jit(solution)/shard_map/ppermute | solution.py:924
  139.7 4.9 %collective-permute-done.42.one_got = bf16[576,512]{1,0:T(8,128)(2,1)S(1)} collective-permute-done((bf16[576,512]{1,0:T(8,128)(2,1)S(1)}, bf16[576,512]{1,0:T(8,128)(2,1)S(1)}, u32[]{:S(2)}, u32[]{:S(2)}) %collective-permute-start.42) | collective-permute-done | bytes 589856 | tf_op jit(solution)/shard_map/ppermute | solution.py:924
  145.1 3.1 %shard_map.259 = (f32[768,512]{1,0:T(8,128)}, f32[768,512]{1,0:T(8,128)}, f32[512,768]{1,0:T(8,128)}) custom-call(s32[8]{0:T(128)S(1)} %get-tuple-element.150.info, bf16[576,512]{1,0:T(8,128)(2,1)S(1)} %get-tuple-element.274.one, bf16[576,512]{1,0:T(8,128)(2,1)S(1)} %collective-permute-done.42.one_got, bf16[576,512]{1,0:T(8,128)(2,1)S(1)} %get-tuple-element.275.two, ...), custom_call_target="tpu_custom_call" | custom-call | flops 40000000 | tf_op jit(solution)/shard_map/pallas_call | solution.py:37
  (114 shorter events, 54.3 us)
Async XLA Ops:
  0.6 10.5 %collective-permute-start = (bf16[128,768]{1,0:T(8,128)(2,1)}, bf16[128,768]{1,0:T(8,128)(2,1)S(1)}, u32[]{:S(2)}, u32[]{:S(2)}) collective-permute-start(bf16[128,768]{1,0:T(8,128)(2,1)} %x_ref.1), channel_id=1, source_target_pairs={{0,2},{1,3},{2,0},{3,1},{4,6},{5,7},{6,4},{7,5},{8,10},{9,11},{10,... | collective-permute-start | bytes 589832 | tf_op jit(solution)/shard_map/ppermute | solution.py:924
  3.7 12.0 %collective-permute-start.1 = (bf16[128,768]{1,0:T(8,128)(2,1)}, bf16[128,768]{1,0:T(8,128)(2,1)S(1)}, u32[]{:S(2)}, u32[]{:S(2)}) collective-permute-start(bf16[128,768]{1,0:T(8,128)(2,1)} %x_ref.1), channel_id=1, source_target_pairs={{0,1},{1,0},{2,3},{3,2},{4,5},{5,4},{6,7},{7,6},{8,9},{9,8},{10,11... | collective-permute-start | bytes 589832 | tf_op jit(solution)/shard_map/ppermute | solution.py:924
  3.7 10.9 %collective-permute-start.3 = (bf16[128,768]{1,0:T(8,128)(2,1)}, bf16[128,768]{1,0:T(8,128)(2,1)S(1)}, u32[]{:S(2)}, u32[]{:S(2)}) collective-permute-start(bf16[128,768]{1,0:T(8,128)(2,1)} %x_ref.1), channel_id=1, source_target_pairs={{0,4},{4,0},{8,12},{12,8},{16,20},{20,16},{24,28},{28,24},{1,5},{5... | collective-permute-start | bytes 589832 | tf_op jit(solution)/shard_map/ppermute | solution.py:924
  42.7 11.2 %collective-permute-start.18 = (bf16[256,768]{1,0:T(8,128)(2,1)S(1)}, bf16[256,768]{1,0:T(8,128)(2,1)S(1)}, u32[]{:S(2)}, u32[]{:S(2)}) collective-permute-start(bf16[256,768]{1,0:T(8,128)(2,1)S(1)} %shard_map.237.sum_ref), channel_id=1, source_target_pairs={{0,2},{1,3},{2,0},{3,1},{4,6},{5,7},{6,4},{7,5},{8,10},{9,11},{10,... | collective-permute-start | bytes 1179656 | tf_op jit(solution)/shard_map/ppermute | solution.py:924
  45.7 16.6 %collective-permute-start.23 = (bf16[576,512]{1,0:T(8,128)(2,1)S(1)}, bf16[576,512]{1,0:T(8,128)(2,1)S(1)}, u32[]{:S(2)}, u32[]{:S(2)}) collective-permute-start(bf16[576,512]{1,0:T(8,128)(2,1)S(1)} %get-tuple-element.190), channel_id=1, source_target_pairs={{0,4},{4,0},{8,12},{12,8},{16,20},{20,16},{24,28},{28,24},{1,5},{5... | collective-permute-start | bytes 1769480 | tf_op jit(solution)/shard_map/ppermute | solution.py:924
  48.4 14.8 %collective-permute-start.24 = (bf16[576,512]{1,0:T(8,128)(2,1)S(1)}, bf16[576,512]{1,0:T(8,128)(2,1)S(1)}, u32[]{:S(2)}, u32[]{:S(2)}) collective-permute-start(bf16[576,512]{1,0:T(8,128)(2,1)S(1)} %get-tuple-element.212), channel_id=1, source_target_pairs={{0,8},{4,12},{8,0},{12,4},{16,24},{20,28},{24,16},{28,20},{1,9},{5... | collective-permute-start | bytes 1769480 | tf_op jit(solution)/shard_map/ppermute | solution.py:924
  57.6 14.8 %collective-permute-start.21 = (bf16[832,128]{1,0:T(8,128)(2,1)S(1)}, bf16[832,128]{1,0:T(8,128)(2,1)S(1)}, u32[]{:S(2)}, u32[]{:S(2)}) collective-permute-start(bf16[832,128]{1,0:T(8,128)(2,1)S(1)} %get-tuple-element.208), channel_id=1, source_target_pairs={{0,4},{4,0},{8,12},{12,8},{16,20},{20,16},{24,28},{28,24},{1,5},{5... | collective-permute-start | bytes 638984 | tf_op jit(solution)/shard_map/ppermute | solution.py:924
  60.1 12.3 %collective-permute-start.22 = (bf16[832,128]{1,0:T(8,128)(2,1)S(1)}, bf16[832,128]{1,0:T(8,128)(2,1)S(1)}, u32[]{:S(2)}, u32[]{:S(2)}) collective-permute-start(bf16[832,128]{1,0:T(8,128)(2,1)S(1)} %get-tuple-element.208), channel_id=1, source_target_pairs={{4,8},{12,16},{20,24},{8,4},{16,12},{24,20},{5,9},{13,17},{21,25},... | collective-permute-start | bytes 638984 | tf_op jit(solution)/shard_map/ppermute | solution.py:929
  64.0 12.4 %collective-permute-start.25 = (bf16[288,512]{1,0:T(8,128)(2,1)S(1)}, bf16[288,512]{1,0:T(8,128)(2,1)S(1)}, u32[]{:S(2)}, u32[]{:S(2)}) collective-permute-start(bf16[288,512]{1,0:T(8,128)(2,1)S(1)} %get-tuple-element.213), channel_id=1, source_target_pairs={{0,8},{4,12},{8,0},{12,4},{16,24},{20,28},{24,16},{28,20},{1,9},{5... | collective-permute-start | bytes 884744 | tf_op jit(solution)/shard_map/ppermute | solution.py:924
  65.7 10.8 %collective-permute-start.26 = (bf16[288,512]{1,0:T(8,128)(2,1)S(1)}, bf16[288,512]{1,0:T(8,128)(2,1)S(1)}, u32[]{:S(2)}, u32[]{:S(2)}) collective-permute-start(bf16[288,512]{1,0:T(8,128)(2,1)S(1)} %get-tuple-element.233), channel_id=1, source_target_pairs={{0,4},{4,0},{8,12},{12,8},{16,20},{20,16},{24,28},{28,24},{1,5},{5... | collective-permute-start | bytes 884744 | tf_op jit(solution)/shard_map/ppermute | solution.py:924
  76.3 14.1 %collective-permute-start.29 = (bf16[192,768]{1,0:T(8,128)(2,1)S(1)}, bf16[192,768]{1,0:T(8,128)(2,1)S(1)}, u32[]{:S(2)}, u32[]{:S(2)}) collective-permute-start(bf16[192,768]{1,0:T(8,128)(2,1)S(1)} %get-tuple-element.242), channel_id=1, source_target_pairs={{0,8},{4,12},{8,0},{12,4},{16,24},{20,28},{24,16},{28,20},{1,9},{5... | collective-permute-start | bytes 884744 | tf_op jit(solution)/shard_map/ppermute | solution.py:924
  76.6 13.8 %collective-permute-start.28 = (bf16[192,768]{1,0:T(8,128)(2,1)S(1)}, bf16[192,768]{1,0:T(8,128)(2,1)S(1)}, u32[]{:S(2)}, u32[]{:S(2)}) collective-permute-start(bf16[192,768]{1,0:T(8,128)(2,1)S(1)} %get-tuple-element.240), channel_id=1, source_target_pairs={{0,4},{4,0},{8,12},{12,8},{16,20},{20,16},{24,28},{28,24},{1,5},{5... | collective-permute-start | bytes 884744 | tf_op jit(solution)/shard_map/ppermute | solution.py:924
  79.1 24.4 %collective-permute-start.33 = (bf16[288,512]{1,0:T(8,128)(2,1)S(1)}, bf16[288,512]{1,0:T(8,128)(2,1)S(1)}, u32[]{:S(2)}, u32[]{:S(2)}) collective-permute-start(bf16[288,512]{1,0:T(8,128)(2,1)S(1)} %get-tuple-element.258.refs_0_), channel_id=1, source_target_pairs={{0,16},{4,20},{8,24},{12,28},{16,0},{20,4},{24,8},{28,12},{1,17},{... | collective-permute-start | bytes 884744 | tf_op jit(solution)/shard_map/ppermute | solution.py:924
  81.8 34.0 %collective-permute-start.34 = (bf16[288,512]{1,0:T(8,128)(2,1)S(1)}, bf16[288,512]{1,0:T(8,128)(2,1)S(1)}, u32[]{:S(2)}, u32[]{:S(2)}) collective-permute-start(bf16[288,512]{1,0:T(8,128)(2,1)S(1)} %get-tuple-element.259.refs_2_), channel_id=1, source_target_pairs={{0,16},{4,20},{8,24},{12,28},{16,0},{20,4},{24,8},{28,12},{1,17},{... | collective-permute-start | bytes 884744 | tf_op jit(solution)/shard_map/ppermute | solution.py:924
  82.1 12.2 %collective-permute-start.30 = (bf16[144,768]{1,0:T(8,128)(2,1)S(1)}, bf16[144,768]{1,0:T(8,128)(2,1)S(1)}, u32[]{:S(2)}, u32[]{:S(2)}) collective-permute-start(bf16[144,768]{1,0:T(8,128)(2,1)S(1)} %get-tuple-element.238), channel_id=1, source_target_pairs={{0,2},{1,3},{2,0},{3,1},{4,6},{5,7},{6,4},{7,5},{8,10},{9,11},{10,... | collective-permute-start | bytes 663560 | tf_op jit(solution)/shard_map/ppermute | solution.py:924
  99.4 21.9 %collective-permute-start.35 = (bf16[112,768]{1,0:T(8,128)(2,1)S(1)}, bf16[112,768]{1,0:T(8,128)(2,1)S(1)}, u32[]{:S(2)}, u32[]{:S(2)}) collective-permute-start(bf16[112,768]{1,0:T(8,128)(2,1)S(1)} %get-tuple-element.261.refs_0_), channel_id=1, source_target_pairs={{0,16},{4,20},{8,24},{12,28},{16,0},{20,4},{24,8},{28,12},{1,17},{... | collective-permute-start | bytes 516104 | tf_op jit(solution)/shard_map/ppermute | solution.py:924
  103.4 18.0 %collective-permute-start.36 = (bf16[96,768]{1,0:T(8,128)(2,1)S(1)}, bf16[96,768]{1,0:T(8,128)(2,1)S(1)}, u32[]{:S(2)}, u32[]{:S(2)}) collective-permute-start(bf16[96,768]{1,0:T(8,128)(2,1)S(1)} %get-tuple-element.262.refs_2_), channel_id=1, source_target_pairs={{0,16},{4,20},{8,24},{12,28},{16,0},{20,4},{24,8},{28,12},{1,17},{... | collective-permute-start | bytes 442376 | tf_op jit(solution)/shard_map/ppermute | solution.py:924
  115.9 11.8 %collective-permute-start.37 = (bf16[288,512]{1,0:T(8,128)(2,1)S(1)}, bf16[288,512]{1,0:T(8,128)(2,1)S(1)}, u32[]{:S(2)}, u32[]{:S(2)}) collective-permute-start(bf16[288,512]{1,0:T(8,128)(2,1)S(1)} %get-tuple-element.264.refs_0_), channel_id=1, source_target_pairs={{0,8},{4,12},{8,0},{12,4},{16,24},{20,28},{24,16},{28,20},{1,9},{5... | collective-permute-start | bytes 884744 | tf_op jit(solution)/shard_map/ppermute | solution.py:924
  116.0 11.7 %collective-permute-start.38 = (bf16[288,512]{1,0:T(8,128)(2,1)S(1)}, bf16[288,512]{1,0:T(8,128)(2,1)S(1)}, u32[]{:S(2)}, u32[]{:S(2)}) collective-permute-start(bf16[288,512]{1,0:T(8,128)(2,1)S(1)} %get-tuple-element.265.refs_2_), channel_id=1, source_target_pairs={{0,4},{4,0},{8,12},{12,8},{16,20},{20,16},{24,28},{28,24},{1,5},{5... | collective-permute-start | bytes 884744 | tf_op jit(solution)/shard_map/ppermute | solution.py:924
  121.5 9.9 %collective-permute-start.39 = (bf16[112,768]{1,0:T(8,128)(2,1)S(1)}, bf16[112,768]{1,0:T(8,128)(2,1)S(1)}, u32[]{:S(2)}, u32[]{:S(2)}) collective-permute-start(bf16[112,768]{1,0:T(8,128)(2,1)S(1)} %get-tuple-element.267.refs_0_), channel_id=1, source_target_pairs={{0,8},{4,12},{8,0},{12,4},{16,24},{20,28},{24,16},{28,20},{1,9},{5... | collective-permute-start | bytes 516104 | tf_op jit(solution)/shard_map/ppermute | solution.py:924
  128.3 16.3 %collective-permute-start.42 = (bf16[576,512]{1,0:T(8,128)(2,1)S(1)}, bf16[576,512]{1,0:T(8,128)(2,1)S(1)}, u32[]{:S(2)}, u32[]{:S(2)}) collective-permute-start(bf16[576,512]{1,0:T(8,128)(2,1)S(1)} %get-tuple-element.274.one), channel_id=1, source_target_pairs={{0,4},{4,0},{8,12},{12,8},{16,20},{20,16},{24,28},{28,24},{1,5},{5... | collective-permute-start | bytes 1769480 | tf_op jit(solution)/shard_map/ppermute | solution.py:924
  128.9 16.3 %collective-permute-start.43 = (bf16[576,512]{1,0:T(8,128)(2,1)S(1)}, bf16[576,512]{1,0:T(8,128)(2,1)S(1)}, u32[]{:S(2)}, u32[]{:S(2)}) collective-permute-start(bf16[576,512]{1,0:T(8,128)(2,1)S(1)} %get-tuple-element.275.two), channel_id=1, source_target_pairs={{0,8},{4,12},{8,0},{12,4},{16,24},{20,28},{24,16},{28,20},{1,9},{5... | collective-permute-start | bytes 1769480 | tf_op jit(solution)/shard_map/ppermute | solution.py:924
  132.0 18.4 %collective-permute-start.44 = (bf16[208,768]{1,0:T(8,128)(2,1)S(1)}, bf16[208,768]{1,0:T(8,128)(2,1)S(1)}, u32[]{:S(2)}, u32[]{:S(2)}) collective-permute-start(bf16[208,768]{1,0:T(8,128)(2,1)S(1)} %get-tuple-element.277.one), channel_id=1, source_target_pairs={{0,4},{4,0},{8,12},{12,8},{16,20},{20,16},{24,28},{28,24},{1,5},{5... | collective-permute-start | bytes 958472 | tf_op jit(solution)/shard_map/ppermute | solution.py:924
  132.4 17.8 %collective-permute-start.45 = (bf16[192,768]{1,0:T(8,128)(2,1)S(1)}, bf16[192,768]{1,0:T(8,128)(2,1)S(1)}, u32[]{:S(2)}, u32[]{:S(2)}) collective-permute-start(bf16[192,768]{1,0:T(8,128)(2,1)S(1)} %get-tuple-element.278.two), channel_id=1, source_target_pairs={{0,8},{4,12},{8,0},{12,4},{16,24},{20,28},{24,16},{28,20},{1,9},{5... | collective-permute-start | bytes 884744 | tf_op jit(solution)/shard_map/ppermute | solution.py:924
  (28 other events, 148.4 us)

commit v6 on v5

--- a/solution.py
+++ b/solution.py
@@ -33,12 +33,12 @@
     return lax.dot_general(a, b, (((0,), (0,)), ((), ())), preferred_element_type=F32)
 
 
-def call(kernel, outs, ins, scratch=(), smem=1, hbm=0, micros=2.0, out_smem=0, limit=20):
+def call(kernel, outs, ins, scratch=(), smem=1, hbm=0, micros=2.0, out_smem=0, out_hbm=0, limit=20):
     return pl.pallas_call(
         kernel,
         out_shape=outs,
         in_specs=[SMEM] * smem + [VMEM] * (len(ins) - smem - hbm) + [HBM] * hbm,
-        out_specs=[SMEM] * out_smem + [VMEM] * (len(outs) - out_smem),
+        out_specs=[SMEM] * out_smem + [HBM] * out_hbm + [VMEM] * (len(outs) - out_smem - out_hbm),
         scratch_shapes=list(scratch),
         cost_estimate=pl.CostEstimate(flops=int(micros * 2e7), bytes_accessed=0, transcendentals=0),
         compiler_params=pltpu.CompilerParams(vmem_limit_bytes=limit * 1024 * 1024),
@@ -896,16 +896,38 @@
 
 
 def attention_total_kernel(
-    info, one, one_got, two, two_got, q_ref, k_ref, v_ref, out_ref, gain_one_ref, gain_two_ref, table_ref
+    info,
+    one,
+    one_got,
+    two,
+    two_got,
+    q_hbm,
+    k_hbm,
+    v_hbm,
+    out_hbm,
+    gain_one_ref,
+    gain_two_ref,
+    table_ref,
+    q_ref,
+    k_ref,
+    v_ref,
+    out_ref,
+    sems,
 ):
     rows = q_ref.shape[0]
+    pairs = ((q_ref, q_hbm), (k_ref, k_hbm), (v_ref, v_hbm), (out_ref, out_hbm))
+    copies = [pltpu.make_async_copy(a, b, sems.at[k]) for k, (a, b) in enumerate(pairs)]
     first = info[4] == 0
     mine, got = one[:rows, :], one_got[:rows, :]
     q_ref[...] = jnp.where(first, mine, got).astype(F32)
+    copies[0].start()
     k_ref[...] = jnp.where(first, got, mine).astype(F32)
+    copies[1].start()
     first = info[5] == 0
     v_ref[...] = jnp.where(first, two[...], two_got[...]).astype(F32)
+    copies[2].start()
     out_ref[...] = jnp.where(first, two_got[...], two[...]).astype(F32)
+    copies[3].start()
     if one.shape[0] > rows:
         small = get_small(one, rows) + get_small(one_got, rows)
         for k in range(gain_one_ref.shape[0]):
@@ -918,6 +940,8 @@
         gain_one_ref[...] = jnp.zeros_like(gain_one_ref)
         gain_two_ref[...] = jnp.zeros_like(gain_two_ref)
         table_ref[...] = jnp.zeros_like(table_ref)
+    for copy in copies:
+        copy.wait()
 
 
 def swap(values, axis, bit):
@@ -1324,6 +1348,8 @@
         attention_total_kernel,
         [shape((width, d), F32)] * 4 + [shape((d // CHUNK, CHUNK), F32)] * 2 + [shape((heads, buckets), F32)],
         [info, after(ready[0], down_grad), *ready[1:]],
+        scratch=[pltpu.VMEM((width, d), F32)] * 4 + [pltpu.SemaphoreType.DMA((4,))],
+        out_hbm=4,
         micros=2.0,
     )
     if not joint_sums.tiled:

time: 153 us -> 154 us (level)
  no operation moved by 1% of the time
where the time goes in v6:
time: 154 us; the launch traced here: 153 us
  waiting for transfers between devices  62.7 us (41%)
  Pallas kernels  49.4 us (32%)
  starting transfers between devices  39.1 us (25%)
    ppermute x44, waiting for transfers between devices, swap(): lax.ppermute(values, axis, [(i, i ^ bit) for i in range(lax.axis_size(axi...  62.7 us
    pallas_call x32, Pallas kernels, call(): pl.pallas_call(kernel, out_shape=outs, in_specs=[SMEM] * smem + [VMEM] *...  49.4 us
    ppermute x44, starting transfers between devices, swap(): lax.ppermute(values, axis, [(i, i ^ bit) for i in range(lax.axis_size(axi...  37.5 us
  transfers between devices with their start and end apart: 46, of which 24 were waited for; matrix products, arithmetic and copies ran while one was open for 1% of the time, Pallas kernels for 28%

profile of v6, /device:TPU:0, one launch (start us, length us, event | category | flops | bytes accessed | tf_op | source)
XLA Modules:
  0.0 153.2 jit_solution(1809925871471675893)
XLA Ops:
  0.6 3.0 %collective-permute-start = (bf16[128,768]{1,0:T(8,128)(2,1)}, bf16[128,768]{1,0:T(8,128)(2,1)S(1)}, u32[]{:S(2)}, u32[]{:S(2)}) collective-permute-start(bf16[128,768]{1,0:T(8,128)(2,1)} %x_ref.1), channel_id=1, source_target_pairs={{0,2},{1,3},{2,0},{3,1},{4,6},{5,7},{6,4},{7,5},{8,10},{9,11},{10,... | collective-permute-start | bytes 589832 | tf_op jit(solution)/shard_map/ppermute | solution.py:948
  7.3 3.9 %shard_map.229 = (s32[8]{0:T(128)S(1)}, f32[1,512]{1,0:T(1,128)S(1)}, f32[512,128]{1,0:T(8,128)S(1)}, f32[3,128,2048]{2,1,0:T(8,128)S(1)}, f32[3,32]{1,0:T(4,128...) custom-call(s32[2]{0:T(128)S(1)} %pad_add_fusion.spot, s32[16,128]{1,0:T(8,128)S(1)} %add_bitcast_fusion.bucket_ref, ...), custom_call_target="tpu_custom_call" | custom-call | flops 60000000 | tf_op jit(solution)/shard_map/pallas_call | solution.py:37
  15.7 5.0 %shard_map.230 = (bf16[512,768]{1,0:T(8,128)(2,1)S(1)}, bf16[512,768]{1,0:T(8,128)(2,1)S(1)}, bf16[512,192]{1,0:T(8,128)(2,1)S(1)}, bf16[512,192]{1,0:T(8,128)(2...) custom-call(s32[8]{0:T(128)S(1)} %get-tuple-element.150.info, ...), custom_call_target="tpu_custom_call" | custom-call | flops 100000000 | tf_op jit(solution)/shard_map/pallas_call | solution.py:37
  23.0 4.2 %shard_map.232 = (bf16[512,192]{1,0:T(8,128)(2,1)S(1)}, bf16[768,128]{1,0:T(8,128)(2,1)S(1)}, f32[512,192]{1,0:T(8,128)S(1)}, f32[512,128]{1,0:T(8,128)S(1)}, bf...) custom-call(s32[8]{0:T(128)S(1)} %get-tuple-element.150.info, ...), custom_call_target="tpu_custom_call" | custom-call | flops 6000000000 | tf_op jit(solution)/shard_map/pallas_call | solution.py:37
  28.5 2.9 %collective-permute-done.12.o1 = bf16[192,768]{1,0:T(8,128)(2,1)S(1)} collective-permute-done((bf16[192,768]{1,0:T(8,128)(2,1)S(1)}, bf16[192,768]{1,0:T(8,128)(2,1)S(1)}, u32[]{:S(2)}, u32[]{:S(2)}) %collective-permute-start.12) | collective-permute-done | bytes 294944 | tf_op jit(solution)/shard_map/ppermute | solution.py:948
  36.7 4.2 %shard_map.236 = (bf16[512,768]{1,0:T(8,128)(2,1)S(1)}, f32[256,768]{1,0:T(8,128)S(1)}, bf16[512,512]{1,0:T(8,128)(2,1)S(1)}, bf16[512,512]{1,0:T(8,128)(2,1)S(1...) custom-call(s32[8]{0:T(128)S(1)} %get-tuple-element.150.info, ...), custom_call_target="tpu_custom_call" | custom-call | flops 100000000 | tf_op jit(solution)/shard_map/pallas_call | solution.py:37
  45.7 2.7 %collective-permute-start.23 = (bf16[576,512]{1,0:T(8,128)(2,1)S(1)}, bf16[576,512]{1,0:T(8,128)(2,1)S(1)}, u32[]{:S(2)}, u32[]{:S(2)}) collective-permute-start(bf16[576,512]{1,0:T(8,128)(2,1)S(1)} %get-tuple-element.190), channel_id=1, source_target_pairs={{0,4},{4,0},{8,12},{12,8},{16,20},{20,16},{24,28},{28,24},{1,5},{5... | collective-permute-start | bytes 1769480 | tf_op jit(solution)/shard_map/ppermute | solution.py:948
  50.6 2.6 %shard_map.240 = (f32[3,512,512]{2,1,0:T(8,128)S(1)}, f32[3,512,512]{2,1,0:T(8,128)S(1)}, f32[3,512,512]{2,1,0:T(8,128)S(1)}) custom-call(s32[8]{0:T(128)S(1)} %get-tuple-element.150.info, bf16[512,192]{1,0:T(8,128)(2,1)S(1)} %get-tuple-element.214.q_ref, bf16[512,192]{1,0:T(8,128)(2,1)S(1)} %get-tuple-element.194.k_ref, ...), custom_call_target="tpu_custom_call" | custom-call | flops 20000000 | tf_op jit(solution)/shard_map/pallas_call | solution.py:37
  57.6 2.5 %collective-permute-start.21 = (bf16[832,128]{1,0:T(8,128)(2,1)S(1)}, bf16[832,128]{1,0:T(8,128)(2,1)S(1)}, u32[]{:S(2)}, u32[]{:S(2)}) collective-permute-start(bf16[832,128]{1,0:T(8,128)(2,1)S(1)} %get-tuple-element.208), channel_id=1, source_target_pairs={{0,4},{4,0},{8,12},{12,8},{16,20},{20,16},{24,28},{28,24},{1,5},{5... | collective-permute-start | bytes 638984 | tf_op jit(solution)/shard_map/ppermute | solution.py:948
  67.8 2.5 %shard_map.245 = (f32[512,192]{1,0:T(8,128)S(1)}, f32[512,192]{1,0:T(8,128)S(1)}, f32[512,192]{1,0:T(8,128)S(1)}, f32[3,128,1024]{2,1,0:T(8,128)S(1)}) custom-call(f32[3,512,512]{2,1,0:T(8,128)S(1)} %get-tuple-element.200.own_ref, bf16[512,192]{1,0:T(8,128)(2,1)S(1)} %get-tuple-element.214.q_ref, bf16[512,192]{1,0:T(8,128)(2,1)S(1)} %get-tuple-element.194.k_ref, ...), custom_call_target="tpu_custom_call" | custom-call | flops 4000000000 | tf_op jit(solution)/shard_map/pallas_call | solution.py:37
  72.4 3.8 %shard_map.247 = (bf16[192,768]{1,0:T(8,128)(2,1)S(1)}, bf16[192,768]{1,0:T(8,128)(2,1)S(1)}, bf16[192,768]{1,0:T(8,128)(2,1)S(1)}, bf16[192,768]{1,0:T(8,128)(2...) custom-call(s32[8]{0:T(128)S(1)} %get-tuple-element.150.info, ...), custom_call_target="tpu_custom_call" | custom-call | flops 6000000000 | tf_op jit(solution)/shard_map/pallas_call | solution.py:37
  76.6 2.5 %collective-permute-start.28 = (bf16[192,768]{1,0:T(8,128)(2,1)S(1)}, bf16[192,768]{1,0:T(8,128)(2,1)S(1)}, u32[]{:S(2)}, u32[]{:S(2)}) collective-permute-start(bf16[192,768]{1,0:T(8,128)(2,1)S(1)} %get-tuple-element.240), channel_id=1, source_target_pairs={{0,4},{4,0},{8,12},{12,8},{16,20},{20,16},{24,28},{28,24},{1,5},{5... | collective-permute-start | bytes 884744 | tf_op jit(solution)/shard_map/ppermute | solution.py:948
  79.1 2.6 %collective-permute-start.33 = (bf16[288,512]{1,0:T(8,128)(2,1)S(1)}, bf16[288,512]{1,0:T(8,128)(2,1)S(1)}, u32[]{:S(2)}, u32[]{:S(2)}) collective-permute-start(bf16[288,512]{1,0:T(8,128)(2,1)S(1)} %get-tuple-element.258.refs_0_), channel_id=1, source_target_pairs={{0,16},{4,20},{8,24},{12,28},{16,0},{20,4},{24,8},{28,12},{1,17},{... | collective-permute-start | bytes 884744 | tf_op jit(solution)/shard_map/ppermute | solution.py:948
  83.3 7.0 %collective-permute-done.29.refs_3_ = bf16[192,768]{1,0:T(8,128)(2,1)S(1)} collective-permute-done((bf16[192,768]{1,0:T(8,128)(2,1)S(1)}, bf16[192,768]{1,0:T(8,128)(2,1)S(1)}, u32[]{:S(2)}, u32[]{:S(2)}) %collective-permute-start.29) | collective-permute-done | bytes 294944 | tf_op jit(solution)/shard_map/ppermute | solution.py:948
  91.8 2.5 %shard_map.251.table_ref = f32[3,128]{1,0:T(4,128)S(1)} custom-call(s32[8]{0:T(128)S(1)} %get-tuple-element.150.info, f32[3,128,1024]{2,1,0:T(8,128)S(1)} %get-tuple-element.250.near_fold, f32[3,128,1024]{2,1,0:T(8,128)S(1)} %get-tuple-element.251.far_fold, s32[16,128]{1,0:T(8,128)S(1)} %get-tuple-element.252.flipped_ref, ...), custom_call_target="tpu_custom_call" | custom-call | flops 20000000 | tf_op jit(solution)/shard_map/pallas_call | solution.py:37
  95.3 4.1 %collective-permute-done.31.refs_1_ = bf16[96,768]{1,0:T(8,128)(2,1)S(1)} collective-permute-done((bf16[96,768]{1,0:T(8,128)(2,1)S(1)}, bf16[96,768]{1,0:T(8,128)(2,1)S(1)}, u32[]{:S(2)}, u32[]{:S(2)}) %collective-permute-start.31) | collective-permute-done | bytes 147488 | tf_op jit(solution)/shard_map/ppermute | solution.py:948
  99.4 4.0 %collective-permute-start.35 = (bf16[112,768]{1,0:T(8,128)(2,1)S(1)}, bf16[112,768]{1,0:T(8,128)(2,1)S(1)}, u32[]{:S(2)}, u32[]{:S(2)}) collective-permute-start(bf16[112,768]{1,0:T(8,128)(2,1)S(1)} %get-tuple-element.261.refs_0_), channel_id=1, source_target_pairs={{0,16},{4,20},{8,24},{12,28},{16,0},{20,4},{24,8},{28,12},{1,17},{... | collective-permute-start | bytes 516104 | tf_op jit(solution)/shard_map/ppermute | solution.py:948
  103.5 12.3 %collective-permute-done.34.refs_3_ = bf16[288,512]{1,0:T(8,128)(2,1)S(1)} collective-permute-done((bf16[288,512]{1,0:T(8,128)(2,1)S(1)}, bf16[288,512]{1,0:T(8,128)(2,1)S(1)}, u32[]{:S(2)}, u32[]{:S(2)}) %collective-permute-start.34) | collective-permute-done | bytes 294944 | tf_op jit(solution)/shard_map/ppermute | solution.py:948
  117.1 4.3 %collective-permute-done.36.refs_3_ = bf16[96,768]{1,0:T(8,128)(2,1)S(1)} collective-permute-done((bf16[96,768]{1,0:T(8,128)(2,1)S(1)}, bf16[96,768]{1,0:T(8,128)(2,1)S(1)}, u32[]{:S(2)}, u32[]{:S(2)}) %collective-permute-start.36) | collective-permute-done | bytes 147488 | tf_op jit(solution)/shard_map/ppermute | solution.py:948
  122.1 5.6 %collective-permute-done.37.refs_1_ = bf16[288,512]{1,0:T(8,128)(2,1)S(1)} collective-permute-done((bf16[288,512]{1,0:T(8,128)(2,1)S(1)}, bf16[288,512]{1,0:T(8,128)(2,1)S(1)}, u32[]{:S(2)}, u32[]{:S(2)}) %collective-permute-start.37) | collective-permute-done | bytes 294944 | tf_op jit(solution)/shard_map/ppermute | solution.py:948
  134.5 4.5 %collective-permute-done.41.got_ref = bf16[128,768]{1,0:T(8,128)(2,1)S(1)} collective-permute-done((bf16[128,768]{1,0:T(8,128)(2,1)S(1)}, bf16[128,768]{1,0:T(8,128)(2,1)S(1)}, u32[]{:S(2)}, u32[]{:S(2)}) %collective-permute-start.41) | collective-permute-done | bytes 196640 | tf_op jit(solution)/shard_map/ppermute | solution.py:948
  139.7 4.9 %collective-permute-done.42.one_got = bf16[576,512]{1,0:T(8,128)(2,1)S(1)} collective-permute-done((bf16[576,512]{1,0:T(8,128)(2,1)S(1)}, bf16[576,512]{1,0:T(8,128)(2,1)S(1)}, u32[]{:S(2)}, u32[]{:S(2)}) %collective-permute-start.42) | collective-permute-done | bytes 589856 | tf_op jit(solution)/shard_map/ppermute | solution.py:948
  145.1 3.1 %shard_map.259 = (f32[768,512]{1,0:T(8,128)}, f32[768,512]{1,0:T(8,128)}, f32[512,768]{1,0:T(8,128)}) custom-call(s32[8]{0:T(128)S(1)} %get-tuple-element.150.info, bf16[576,512]{1,0:T(8,128)(2,1)S(1)} %get-tuple-element.274.one, bf16[576,512]{1,0:T(8,128)(2,1)S(1)} %collective-permute-done.42.one_got, bf16[576,512]{1,0:T(8,128)(2,1)S(1)} %get-tuple-element.275.two, ...), custom_call_target="tpu_custom_call" | custom-call | flops 40000000 | tf_op jit(solution)/shard_map/pallas_call | solution.py:37
  150.4 2.6 %shard_map.260 = (f32[192,768]{1,0:T(8,128)}, f32[192,768]{1,0:T(8,128)}, f32[192,768]{1,0:T(8,128)}, f32[192,768]{1,0:T(8,128)}, f32[6,128]{1,0:T(8,128)}, /*index=5*/f32[6,128]{1,0:T(8,128)}, f32[3,32]{1,0:T(4,128)}) custom-call(s32[8]{0:T(128)S(1)} %get-tuple-element.150.info, bf16[208,768]{1,0:T(8,128)(2,1)S(1)} %get-tuple-element.277.one, ...), custom_call_target="tpu_custom_call" | custom-call | flops 40000000 | tf_op jit(solution)/shard_map/pallas_call | solution.py:37
  (114 shorter events, 54.7 us)
Async XLA Ops:
  0.6 10.5 %collective-permute-start = (bf16[128,768]{1,0:T(8,128)(2,1)}, bf16[128,768]{1,0:T(8,128)(2,1)S(1)}, u32[]{:S(2)}, u32[]{:S(2)}) collective-permute-start(bf16[128,768]{1,0:T(8,128)(2,1)} %x_ref.1), channel_id=1, source_target_pairs={{0,2},{1,3},{2,0},{3,1},{4,6},{5,7},{6,4},{7,5},{8,10},{9,11},{10,... | collective-permute-start | bytes 589832 | tf_op jit(solution)/shard_map/ppermute | solution.py:948
  3.7 12.0 %collective-permute-start.1 = (bf16[128,768]{1,0:T(8,128)(2,1)}, bf16[128,768]{1,0:T(8,128)(2,1)S(1)}, u32[]{:S(2)}, u32[]{:S(2)}) collective-permute-start(bf16[128,768]{1,0:T(8,128)(2,1)} %x_ref.1), channel_id=1, source_target_pairs={{0,1},{1,0},{2,3},{3,2},{4,5},{5,4},{6,7},{7,6},{8,9},{9,8},{10,11... | collective-permute-start | bytes 589832 | tf_op jit(solution)/shard_map/ppermute | solution.py:948
  3.7 10.9 %collective-permute-start.3 = (bf16[128,768]{1,0:T(8,128)(2,1)}, bf16[128,768]{1,0:T(8,128)(2,1)S(1)}, u32[]{:S(2)}, u32[]{:S(2)}) collective-permute-start(bf16[128,768]{1,0:T(8,128)(2,1)} %x_ref.1), channel_id=1, source_target_pairs={{0,4},{4,0},{8,12},{12,8},{16,20},{20,16},{24,28},{28,24},{1,5},{5... | collective-permute-start | bytes 589832 | tf_op jit(solution)/shard_map/ppermute | solution.py:948
  42.7 11.2 %collective-permute-start.18 = (bf16[256,768]{1,0:T(8,128)(2,1)S(1)}, bf16[256,768]{1,0:T(8,128)(2,1)S(1)}, u32[]{:S(2)}, u32[]{:S(2)}) collective-permute-start(bf16[256,768]{1,0:T(8,128)(2,1)S(1)} %shard_map.237.sum_ref), channel_id=1, source_target_pairs={{0,2},{1,3},{2,0},{3,1},{4,6},{5,7},{6,4},{7,5},{8,10},{9,11},{10,... | collective-permute-start | bytes 1179656 | tf_op jit(solution)/shard_map/ppermute | solution.py:948
  45.7 16.6 %collective-permute-start.23 = (bf16[576,512]{1,0:T(8,128)(2,1)S(1)}, bf16[576,512]{1,0:T(8,128)(2,1)S(1)}, u32[]{:S(2)}, u32[]{:S(2)}) collective-permute-start(bf16[576,512]{1,0:T(8,128)(2,1)S(1)} %get-tuple-element.190), channel_id=1, source_target_pairs={{0,4},{4,0},{8,12},{12,8},{16,20},{20,16},{24,28},{28,24},{1,5},{5... | collective-permute-start | bytes 1769480 | tf_op jit(solution)/shard_map/ppermute | solution.py:948
  48.4 14.8 %collective-permute-start.24 = (bf16[576,512]{1,0:T(8,128)(2,1)S(1)}, bf16[576,512]{1,0:T(8,128)(2,1)S(1)}, u32[]{:S(2)}, u32[]{:S(2)}) collective-permute-start(bf16[576,512]{1,0:T(8,128)(2,1)S(1)} %get-tuple-element.212), channel_id=1, source_target_pairs={{0,8},{4,12},{8,0},{12,4},{16,24},{20,28},{24,16},{28,20},{1,9},{5... | collective-permute-start | bytes 1769480 | tf_op jit(solution)/shard_map/ppermute | solution.py:948
  57.6 14.8 %collective-permute-start.21 = (bf16[832,128]{1,0:T(8,128)(2,1)S(1)}, bf16[832,128]{1,0:T(8,128)(2,1)S(1)}, u32[]{:S(2)}, u32[]{:S(2)}) collective-permute-start(bf16[832,128]{1,0:T(8,128)(2,1)S(1)} %get-tuple-element.208), channel_id=1, source_target_pairs={{0,4},{4,0},{8,12},{12,8},{16,20},{20,16},{24,28},{28,24},{1,5},{5... | collective-permute-start | bytes 638984 | tf_op jit(solution)/shard_map/ppermute | solution.py:948
  60.1 12.3 %collective-permute-start.22 = (bf16[832,128]{1,0:T(8,128)(2,1)S(1)}, bf16[832,128]{1,0:T(8,128)(2,1)S(1)}, u32[]{:S(2)}, u32[]{:S(2)}) collective-permute-start(bf16[832,128]{1,0:T(8,128)(2,1)S(1)} %get-tuple-element.208), channel_id=1, source_target_pairs={{4,8},{12,16},{20,24},{8,4},{16,12},{24,20},{5,9},{13,17},{21,25},... | collective-permute-start | bytes 638984 | tf_op jit(solution)/shard_map/ppermute | solution.py:953
  64.0 12.4 %collective-permute-start.25 = (bf16[288,512]{1,0:T(8,128)(2,1)S(1)}, bf16[288,512]{1,0:T(8,128)(2,1)S(1)}, u32[]{:S(2)}, u32[]{:S(2)}) collective-permute-start(bf16[288,512]{1,0:T(8,128)(2,1)S(1)} %get-tuple-element.213), channel_id=1, source_target_pairs={{0,8},{4,12},{8,0},{12,4},{16,24},{20,28},{24,16},{28,20},{1,9},{5... | collective-permute-start | bytes 884744 | tf_op jit(solution)/shard_map/ppermute | solution.py:948
  65.7 10.8 %collective-permute-start.26 = (bf16[288,512]{1,0:T(8,128)(2,1)S(1)}, bf16[288,512]{1,0:T(8,128)(2,1)S(1)}, u32[]{:S(2)}, u32[]{:S(2)}) collective-permute-start(bf16[288,512]{1,0:T(8,128)(2,1)S(1)} %get-tuple-element.233), channel_id=1, source_target_pairs={{0,4},{4,0},{8,12},{12,8},{16,20},{20,16},{24,28},{28,24},{1,5},{5... | collective-permute-start | bytes 884744 | tf_op jit(solution)/shard_map/ppermute | solution.py:948
  76.3 14.1 %collective-permute-start.29 = (bf16[192,768]{1,0:T(8,128)(2,1)S(1)}, bf16[192,768]{1,0:T(8,128)(2,1)S(1)}, u32[]{:S(2)}, u32[]{:S(2)}) collective-permute-start(bf16[192,768]{1,0:T(8,128)(2,1)S(1)} %get-tuple-element.242), channel_id=1, source_target_pairs={{0,8},{4,12},{8,0},{12,4},{16,24},{20,28},{24,16},{28,20},{1,9},{5... | collective-permute-start | bytes 884744 | tf_op jit(solution)/shard_map/ppermute | solution.py:948
  76.6 13.8 %collective-permute-start.28 = (bf16[192,768]{1,0:T(8,128)(2,1)S(1)}, bf16[192,768]{1,0:T(8,128)(2,1)S(1)}, u32[]{:S(2)}, u32[]{:S(2)}) collective-permute-start(bf16[192,768]{1,0:T(8,128)(2,1)S(1)} %get-tuple-element.240), channel_id=1, source_target_pairs={{0,4},{4,0},{8,12},{12,8},{16,20},{20,16},{24,28},{28,24},{1,5},{5... | collective-permute-start | bytes 884744 | tf_op jit(solution)/shard_map/ppermute | solution.py:948
  79.1 24.4 %collective-permute-start.33 = (bf16[288,512]{1,0:T(8,128)(2,1)S(1)}, bf16[288,512]{1,0:T(8,128)(2,1)S(1)}, u32[]{:S(2)}, u32[]{:S(2)}) collective-permute-start(bf16[288,512]{1,0:T(8,128)(2,1)S(1)} %get-tuple-element.258.refs_0_), channel_id=1, source_target_pairs={{0,16},{4,20},{8,24},{12,28},{16,0},{20,4},{24,8},{28,12},{1,17},{... | collective-permute-start | bytes 884744 | tf_op jit(solution)/shard_map/ppermute | solution.py:948
  81.8 34.0 %collective-permute-start.34 = (bf16[288,512]{1,0:T(8,128)(2,1)S(1)}, bf16[288,512]{1,0:T(8,128)(2,1)S(1)}, u32[]{:S(2)}, u32[]{:S(2)}) collective-permute-start(bf16[288,512]{1,0:T(8,128)(2,1)S(1)} %get-tuple-element.259.refs_2_), channel_id=1, source_target_pairs={{0,16},{4,20},{8,24},{12,28},{16,0},{20,4},{24,8},{28,12},{1,17},{... | collective-permute-start | bytes 884744 | tf_op jit(solution)/shard_map/ppermute | solution.py:948
  82.1 12.2 %collective-permute-start.30 = (bf16[144,768]{1,0:T(8,128)(2,1)S(1)}, bf16[144,768]{1,0:T(8,128)(2,1)S(1)}, u32[]{:S(2)}, u32[]{:S(2)}) collective-permute-start(bf16[144,768]{1,0:T(8,128)(2,1)S(1)} %get-tuple-element.238), channel_id=1, source_target_pairs={{0,2},{1,3},{2,0},{3,1},{4,6},{5,7},{6,4},{7,5},{8,10},{9,11},{10,... | collective-permute-start | bytes 663560 | tf_op jit(solution)/shard_map/ppermute | solution.py:948
  99.4 21.9 %collective-permute-start.35 = (bf16[112,768]{1,0:T(8,128)(2,1)S(1)}, bf16[112,768]{1,0:T(8,128)(2,1)S(1)}, u32[]{:S(2)}, u32[]{:S(2)}) collective-permute-start(bf16[112,768]{1,0:T(8,128)(2,1)S(1)} %get-tuple-element.261.refs_0_), channel_id=1, source_target_pairs={{0,16},{4,20},{8,24},{12,28},{16,0},{20,4},{24,8},{28,12},{1,17},{... | collective-permute-start | bytes 516104 | tf_op jit(solution)/shard_map/ppermute | solution.py:948
  103.4 18.0 %collective-permute-start.36 = (bf16[96,768]{1,0:T(8,128)(2,1)S(1)}, bf16[96,768]{1,0:T(8,128)(2,1)S(1)}, u32[]{:S(2)}, u32[]{:S(2)}) collective-permute-start(bf16[96,768]{1,0:T(8,128)(2,1)S(1)} %get-tuple-element.262.refs_2_), channel_id=1, source_target_pairs={{0,16},{4,20},{8,24},{12,28},{16,0},{20,4},{24,8},{28,12},{1,17},{... | collective-permute-start | bytes 442376 | tf_op jit(solution)/shard_map/ppermute | solution.py:948
  115.9 11.8 %collective-permute-start.37 = (bf16[288,512]{1,0:T(8,128)(2,1)S(1)}, bf16[288,512]{1,0:T(8,128)(2,1)S(1)}, u32[]{:S(2)}, u32[]{:S(2)}) collective-permute-start(bf16[288,512]{1,0:T(8,128)(2,1)S(1)} %get-tuple-element.264.refs_0_), channel_id=1, source_target_pairs={{0,8},{4,12},{8,0},{12,4},{16,24},{20,28},{24,16},{28,20},{1,9},{5... | collective-permute-start | bytes 884744 | tf_op jit(solution)/shard_map/ppermute | solution.py:948
  116.0 11.7 %collective-permute-start.38 = (bf16[288,512]{1,0:T(8,128)(2,1)S(1)}, bf16[288,512]{1,0:T(8,128)(2,1)S(1)}, u32[]{:S(2)}, u32[]{:S(2)}) collective-permute-start(bf16[288,512]{1,0:T(8,128)(2,1)S(1)} %get-tuple-element.265.refs_2_), channel_id=1, source_target_pairs={{0,4},{4,0},{8,12},{12,8},{16,20},{20,16},{24,28},{28,24},{1,5},{5... | collective-permute-start | bytes 884744 | tf_op jit(solution)/shard_map/ppermute | solution.py:948
  121.5 9.9 %collective-permute-start.39 = (bf16[112,768]{1,0:T(8,128)(2,1)S(1)}, bf16[112,768]{1,0:T(8,128)(2,1)S(1)}, u32[]{:S(2)}, u32[]{:S(2)}) collective-permute-start(bf16[112,768]{1,0:T(8,128)(2,1)S(1)} %get-tuple-element.267.refs_0_), channel_id=1, source_target_pairs={{0,8},{4,12},{8,0},{12,4},{16,24},{20,28},{24,16},{28,20},{1,9},{5... | collective-permute-start | bytes 516104 | tf_op jit(solution)/shard_map/ppermute | solution.py:948
  128.3 16.3 %collective-permute-start.42 = (bf16[576,512]{1,0:T(8,128)(2,1)S(1)}, bf16[576,512]{1,0:T(8,128)(2,1)S(1)}, u32[]{:S(2)}, u32[]{:S(2)}) collective-permute-start(bf16[576,512]{1,0:T(8,128)(2,1)S(1)} %get-tuple-element.274.one), channel_id=1, source_target_pairs={{0,4},{4,0},{8,12},{12,8},{16,20},{20,16},{24,28},{28,24},{1,5},{5... | collective-permute-start | bytes 1769480 | tf_op jit(solution)/shard_map/ppermute | solution.py:948
  128.9 16.3 %collective-permute-start.43 = (bf16[576,512]{1,0:T(8,128)(2,1)S(1)}, bf16[576,512]{1,0:T(8,128)(2,1)S(1)}, u32[]{:S(2)}, u32[]{:S(2)}) collective-permute-start(bf16[576,512]{1,0:T(8,128)(2,1)S(1)} %get-tuple-element.275.two), channel_id=1, source_target_pairs={{0,8},{4,12},{8,0},{12,4},{16,24},{20,28},{24,16},{28,20},{1,9},{5... | collective-permute-start | bytes 1769480 | tf_op jit(solution)/shard_map/ppermute | solution.py:948
  132.0 18.4 %collective-permute-start.44 = (bf16[208,768]{1,0:T(8,128)(2,1)S(1)}, bf16[208,768]{1,0:T(8,128)(2,1)S(1)}, u32[]{:S(2)}, u32[]{:S(2)}) collective-permute-start(bf16[208,768]{1,0:T(8,128)(2,1)S(1)} %get-tuple-element.277.one), channel_id=1, source_target_pairs={{0,4},{4,0},{8,12},{12,8},{16,20},{20,16},{24,28},{28,24},{1,5},{5... | collective-permute-start | bytes 958472 | tf_op jit(solution)/shard_map/ppermute | solution.py:948
  132.4 17.8 %collective-permute-start.45 = (bf16[192,768]{1,0:T(8,128)(2,1)S(1)}, bf16[192,768]{1,0:T(8,128)(2,1)S(1)}, u32[]{:S(2)}, u32[]{:S(2)}) collective-permute-start(bf16[192,768]{1,0:T(8,128)(2,1)S(1)} %get-tuple-element.278.two), channel_id=1, source_target_pairs={{0,8},{4,12},{8,0},{12,4},{16,24},{20,28},{24,16},{28,20},{1,9},{5... | collective-permute-start | bytes 884744 | tf_op jit(solution)/shard_map/ppermute | solution.py:948
  (28 other events, 148.4 us)
